TPU v7x, 32 devices: a whole 2x2x4 slice. The times are simulated.
32 devices in a mesh: row: 2 (over z_hi), tm: 8 (over y, x, core), space: 2 (over z_lo).
Axes of the slice: x: 2, y: 2, z: 4 (z_hi: 2, z_lo: 2; z = z_hi * 2 + z_lo), core: 2. Of those that a mesh axis runs over, the one named last changes fastest.
Arguments:
- block_input: bfloat16 [2, 32, 256, 1024], P('row', 'tm', 'space'), may hold values from -6 to 6
- action_table: bfloat16 [8, 1024], P(None, 'tm'), may hold values from -3 to 3
- norm_gain: bfloat16 [3, 1024], P(None, 'tm'), may hold values from 0.5 to 1.5
- norm_bias: bfloat16 [3, 1024], P(None, 'tm'), may hold values from -2 to 2
- space_qkv: bfloat16 [1024, 3072], P('tm'), may hold values from -0.1875 to 0.1875
- space_out: bfloat16 [1024, 1024], P('tm'), may hold values from -0.75 to 0.75
- time_qkv: bfloat16 [1024, 3072], P('tm'), may hold values from -0.1875 to 0.1875
- time_out: bfloat16 [1024, 1024], P('tm'), may hold values from -0.375 to 0.375
- ffn_in: bfloat16 [1024, 4096], P('tm'), may hold values from -0.1875 to 0.1875
- ffn_bias_in: bfloat16 [4096], P('tm'), may hold values from -2 to 2
- ffn_out: bfloat16 [4096, 1024], P('tm'), may hold values from -0.09375 to 0.09375
- ffn_bias_out: bfloat16 [1024], P('tm'), may hold values from -2 to 2
- out_grad: bfloat16 [2, 32, 256, 1024], P('row', 'tm', 'space'), may hold values from -6 to 6
- frame_segment: int32 [2, 32], P('row'), may hold values from 0 to 1, as said below
- frame_action: int32 [2, 32], P('row', 'tm'), may hold values from 0 to 7
Outputs:
- block_output: bfloat16 [2, 32, 256, 1024], P('row', 'tm', 'space')
- input_grad: float32 [2, 32, 256, 1024], P('row', 'tm', 'space')
- action_table_grad: float32 [8, 1024], P(None, 'tm')
- norm_gain_grad: float32 [3, 1024], P(None, 'tm')
- norm_bias_grad: float32 [3, 1024], P(None, 'tm')
- space_qkv_grad: float32 [1024, 3072], P('tm')
- space_out_grad: float32 [1024, 1024], P('tm')
- time_qkv_grad: float32 [1024, 3072], P('tm')
- time_out_grad: float32 [1024, 1024], P('tm')
- ffn_in_grad: float32 [1024, 4096], P('tm')
- ffn_bias_in_grad: float32 [4096], P('tm')
- ffn_out_grad: float32 [4096, 1024], P('tm')
- ffn_bias_out_grad: float32 [1024], P('tm')
Inputs may be any that keep to these rules, and one draw needn't show every extreme that they name: `frame_segment`: in each row the ids never fall, start at 0 and rise by one from clip to clip; each clip spans 12 to 20 frames, and in every row one clip spans exactly 20 frames.
All inputs are finite; a program needn't handle non-finite values.
Results may differ from a plain program's by a relative error of at most 0.019.
Values may be sent and summed in bfloat16 or wider, within the bound.
A program may use at most 256 MiB of HBM per device.

v0:
```python
import math

import jax
import jax.numpy as jnp
from jax import lax
from jax.sharding import PartitionSpec as P

MODEL = 1024
HEADS = 16
HEAD_DIM = 64
ACTIONS = 8
SEG_MOST = 20


EPSILON = 1e-05
NEG_FILL = -1e30


def passed_along(block, axis, distance):
    devices = range(lax.axis_size(axis))
    route = [(i - distance, i) for i in devices if i - distance in devices]
    return lax.ppermute(block, axis, route)


def layer_norm(values, gain_row, shift_row):
    row_mean = jnp.mean(values, axis=-1, keepdims=True)
    centred = values - row_mean
    spread = jnp.mean(centred * centred, axis=-1, keepdims=True)
    return centred * lax.rsqrt(spread + EPSILON) * gain_row + shift_row


def forward_dot(values, weight):
    return jnp.dot(values, weight, preferred_element_type=jnp.float32)


def weight_grad(left_rows, right_rows):
    return lax.dot_general(
        left_rows, right_rows, (((0,), (0,)), ((), ())), preferred_element_type=jnp.float32
    )


def back_dot(grad_rows, weight):
    return lax.dot_general(
        grad_rows, weight, (((1,), (1,)), ((), ())), preferred_element_type=jnp.float32
    )


def masked_softmax(scores, allowed):
    filled = jnp.where(allowed, scores, NEG_FILL)
    row_top = jnp.max(filled, axis=-1, keepdims=True)
    raised = jnp.exp(filled - row_top)
    totals = jnp.sum(raised, axis=-1, keepdims=True)
    return (raised / totals, row_top + jnp.log(totals))


def body(
    block_input,
    action_table,
    norm_gain,
    norm_bias,
    space_qkv,
    space_out,
    time_qkv,
    time_out,
    ffn_in,
    ffn_bias_in,
    ffn_out,
    ffn_bias_out,
    out_grad,
    frame_segment,
    frame_action,
):
    gathered = (
        lax.all_gather(action_table, "tm", axis=1, tiled=True),
        lax.all_gather(norm_gain, "tm", axis=1, tiled=True),
        lax.all_gather(norm_bias, "tm", axis=1, tiled=True),
        lax.all_gather(space_qkv, "tm", axis=0, tiled=True),
        lax.all_gather(space_out, "tm", axis=0, tiled=True),
        lax.all_gather(time_qkv, "tm", axis=0, tiled=True),
        lax.all_gather(time_out, "tm", axis=0, tiled=True),
        lax.all_gather(ffn_in, "tm", axis=0, tiled=True),
        lax.all_gather(ffn_bias_in, "tm", axis=0, tiled=True),
        lax.all_gather(ffn_out, "tm", axis=0, tiled=True),
        lax.all_gather(ffn_bias_out, "tm", axis=0, tiled=True),
    )
    (
        table_full,
        gain_full,
        shift_full,
        space_in_w,
        space_out_w,
        time_in_w,
        time_out_w,
        ffn_in_w,
        bias_in_w,
        ffn_out_w,
        bias_out_w,
    ) = gathered
    frame_count = block_input.shape[1]
    half_grid = block_input.shape[2]
    rows_dev = frame_count * half_grid
    score_scale = 1.0 / math.sqrt(HEAD_DIM)
    gains = gain_full.astype(jnp.float32)
    shifts = shift_full.astype(jnp.float32)
    inputs = block_input[0].astype(jnp.float32)
    one_hot = (frame_action[0][:, None] == jnp.arange(ACTIONS)[None, :]).astype(jnp.bfloat16)
    embedded = forward_dot(one_hot, table_full)
    hidden_zero = (inputs + embedded[:, None, :]).reshape(rows_dev, MODEL)
    normed_one = layer_norm(hidden_zero, gains[0], shifts[0]).astype(jnp.bfloat16)
    packed_one = forward_dot(normed_one, space_in_w).astype(jnp.bfloat16)
    query_one = packed_one[:, :MODEL].reshape(frame_count, half_grid, HEADS, HEAD_DIM)
    key_one = packed_one[:, MODEL : 2 * MODEL].reshape(frame_count, half_grid, MODEL)
    value_one = packed_one[:, 2 * MODEL :].reshape(frame_count, half_grid, MODEL)
    space_keys, space_values = (
        lax.all_gather(key_one, "space", axis=1, tiled=True),
        lax.all_gather(value_one, "space", axis=1, tiled=True),
    )
    key_heads = space_keys.reshape(frame_count, -1, HEADS, HEAD_DIM)
    value_heads = space_values.reshape(frame_count, -1, HEADS, HEAD_DIM)
    space_scores = (
        jnp.einsum("fqhe,fkhe->fhqk", query_one, key_heads, preferred_element_type=jnp.float32)
        * score_scale
    )
    space_probs = masked_softmax(space_scores, True)[0]
    space_probs_low = space_probs.astype(jnp.bfloat16)
    space_mixed = (
        jnp.einsum(
            "fhqk,fkhe->fqhe", space_probs_low, value_heads, preferred_element_type=jnp.float32
        )
        .astype(jnp.bfloat16)
        .reshape(rows_dev, MODEL)
    )
    hidden_one = hidden_zero + forward_dot(space_mixed, space_out_w)
    normed_two = layer_norm(hidden_one, gains[1], shifts[1]).astype(jnp.bfloat16)
    packed_two = forward_dot(normed_two, time_in_w).astype(jnp.bfloat16)
    query_two = packed_two[:, :MODEL].reshape(frame_count, half_grid, HEADS, HEAD_DIM)
    key_two = packed_two[:, MODEL : 2 * MODEL].reshape(frame_count, half_grid, MODEL)
    value_two = packed_two[:, 2 * MODEL :].reshape(frame_count, half_grid, MODEL)
    reach = (SEG_MOST + frame_count - 2) // frame_count
    key_pieces = [key_two]
    value_pieces = [value_two]
    for step in range(1, reach + 1):
        earlier_keys, earlier_values = passed_along((key_two, value_two), "tm", step)
        key_pieces.insert(0, earlier_keys)
        value_pieces.insert(0, earlier_values)
    window = (reach + 1) * frame_count
    key_frames = jnp.concatenate(key_pieces, axis=0).reshape(window, half_grid, HEADS, HEAD_DIM)
    value_frames = jnp.concatenate(value_pieces, axis=0).reshape(window, half_grid, HEADS, HEAD_DIM)
    segments = frame_segment[0]
    row_frames = segments.shape[0]
    first_frame = lax.axis_index("tm") * frame_count
    own_frames = first_frame + jnp.arange(frame_count)
    own_segments = jnp.take(segments, own_frames)
    window_frames = first_frame - reach * frame_count + jnp.arange(window)
    window_segments = jnp.take(segments, jnp.clip(window_frames, 0, row_frames - 1))
    allowed = (
        (window_frames[None, :] >= 0)
        & (window_frames[None, :] <= own_frames[:, None])
        & (window_segments[None, :] == own_segments[:, None])
    )
    time_scores = (
        jnp.einsum("fphe,gphe->phfg", query_two, key_frames, preferred_element_type=jnp.float32)
        * score_scale
    )
    time_probs, time_lse = masked_softmax(time_scores, allowed[None, None])
    time_probs_low = time_probs.astype(jnp.bfloat16)
    time_mixed = (
        jnp.einsum(
            "phfg,gphe->fphe", time_probs_low, value_frames, preferred_element_type=jnp.float32
        )
        .astype(jnp.bfloat16)
        .reshape(rows_dev, MODEL)
    )
    hidden_two = hidden_one + forward_dot(time_mixed, time_out_w)
    normed_three = layer_norm(hidden_two, gains[2], shifts[2]).astype(jnp.bfloat16)
    pre_act = forward_dot(normed_three, ffn_in_w) + bias_in_w.astype(jnp.float32)
    activated, gelu_pull = jax.vjp(jax.nn.gelu, pre_act)
    act_low = activated.astype(jnp.bfloat16)
    block_out = hidden_two + forward_dot(act_low, ffn_out_w) + bias_out_w.astype(jnp.float32)
    block_output = block_out.astype(jnp.bfloat16).reshape(block_input.shape)
    grad_out = out_grad[0].reshape(rows_dev, MODEL).astype(jnp.float32)
    grad_ffn_low = grad_out.astype(jnp.bfloat16)
    ffn_out_grad = weight_grad(act_low, grad_ffn_low)
    bias_out_grad = jnp.sum(grad_ffn_low.astype(jnp.float32), axis=0)
    grad_pre = gelu_pull(back_dot(grad_ffn_low, ffn_out_w))[0]
    grad_pre_low = grad_pre.astype(jnp.bfloat16)
    ffn_in_grad = weight_grad(normed_three, grad_pre_low)
    bias_in_grad = jnp.sum(grad_pre_low.astype(jnp.float32), axis=0)
    norm_pull = jax.vjp(layer_norm, hidden_two, gains[2], shifts[2])[1]
    grad_hidden, gain_three, shift_three = norm_pull(back_dot(grad_pre_low, ffn_in_w))
    grad_two = grad_out + grad_hidden
    time_branch = grad_two.astype(jnp.bfloat16)
    time_out_grad = weight_grad(time_mixed, time_branch)
    time_grad_mixed = (
        back_dot(time_branch, time_out_w)
        .astype(jnp.bfloat16)
        .reshape(frame_count, half_grid, HEADS, HEAD_DIM)
    )
    time_grad_probs = jnp.einsum(
        "fphe,gphe->phfg", time_grad_mixed, value_frames, preferred_element_type=jnp.float32
    )
    time_delta = jnp.sum(time_grad_probs * time_probs, axis=-1, keepdims=True)
    time_grad_scores = (time_probs * (time_grad_probs - time_delta)).astype(jnp.bfloat16)
    time_grad_query = (
        jnp.einsum(
            "phfg,gphe->fphe", time_grad_scores, key_frames, preferred_element_type=jnp.float32
        )
        * score_scale
    )
    key_part = (
        jnp.einsum(
            "phfg,fphe->gphe", time_grad_scores, query_two, preferred_element_type=jnp.float32
        )
        * score_scale
    )
    value_part = jnp.einsum(
        "phfg,fphe->gphe", time_probs_low, time_grad_mixed, preferred_element_type=jnp.float32
    )
    both_terms = jnp.concatenate(
        (key_part.reshape(window, half_grid, MODEL), value_part.reshape(window, half_grid, MODEL)),
        axis=-1,
    )
    both_grads = both_terms[reach * frame_count :]
    for step in range(1, reach + 1):
        lower = (reach - step) * frame_count
        both_grads = both_grads + passed_along(
            both_terms[lower : lower + frame_count].astype(jnp.bfloat16), "tm", -step
        ).astype(jnp.float32)
    time_key_grad = both_grads[:, :, :MODEL]
    time_value_grad = both_grads[:, :, MODEL:]
    grad_packed_two = jnp.concatenate(
        (
            time_grad_query.reshape(rows_dev, MODEL),
            time_key_grad.reshape(rows_dev, MODEL),
            time_value_grad.reshape(rows_dev, MODEL),
        ),
        axis=1,
    ).astype(jnp.bfloat16)
    time_qkv_grad = weight_grad(normed_two, grad_packed_two)
    norm_pull = jax.vjp(layer_norm, hidden_one, gains[1], shifts[1])[1]
    grad_hidden, gain_two, shift_two = norm_pull(back_dot(grad_packed_two, time_in_w))
    grad_one = grad_two + grad_hidden
    space_branch = grad_one.astype(jnp.bfloat16)
    space_out_grad = weight_grad(space_mixed, space_branch)
    space_grad_mixed = (
        back_dot(space_branch, space_out_w)
        .astype(jnp.bfloat16)
        .reshape(frame_count, half_grid, HEADS, HEAD_DIM)
    )
    space_grad_probs = jnp.einsum(
        "fqhe,fkhe->fhqk", space_grad_mixed, value_heads, preferred_element_type=jnp.float32
    )
    space_delta = jnp.sum(space_grad_probs * space_probs, axis=-1, keepdims=True)
    space_grad_scores = (space_probs * (space_grad_probs - space_delta)).astype(jnp.bfloat16)
    space_grad_query = (
        jnp.einsum(
            "fhqk,fkhe->fqhe", space_grad_scores, key_heads, preferred_element_type=jnp.float32
        )
        * score_scale
    )
    grid_key_grad = (
        jnp.einsum(
            "fhqk,fqhe->fkhe", space_grad_scores, query_one, preferred_element_type=jnp.float32
        )
        * score_scale
    )
    grid_value_grad = jnp.einsum(
        "fhqk,fqhe->fkhe", space_probs_low, space_grad_mixed, preferred_element_type=jnp.float32
    )
    space_key_grad, space_value_grad = (
        lax.psum_scatter(
            grid_key_grad.reshape(frame_count, -1, MODEL).astype(jnp.bfloat16),
            "space",
            scatter_dimension=1,
            tiled=True,
        ).astype(jnp.float32),
        lax.psum_scatter(
            grid_value_grad.reshape(frame_count, -1, MODEL).astype(jnp.bfloat16),
            "space",
            scatter_dimension=1,
            tiled=True,
        ).astype(jnp.float32),
    )
    grad_packed_one = jnp.concatenate(
        (
            space_grad_query.reshape(rows_dev, MODEL),
            space_key_grad.reshape(rows_dev, MODEL),
            space_value_grad.reshape(rows_dev, MODEL),
        ),
        axis=1,
    ).astype(jnp.bfloat16)
    space_qkv_grad = weight_grad(normed_one, grad_packed_one)
    norm_pull = jax.vjp(layer_norm, hidden_zero, gains[0], shifts[0])[1]
    grad_hidden, gain_one, shift_one = norm_pull(back_dot(grad_packed_one, space_in_w))
    grad_zero = grad_one + grad_hidden
    input_grad = grad_zero.reshape(block_input.shape)
    frame_grad = jnp.sum(grad_zero.reshape(frame_count, half_grid, MODEL), axis=1)
    action_grad = jnp.dot(
        one_hot.astype(jnp.float32).T, frame_grad, precision=lax.Precision.HIGHEST
    )
    gain_grad = jnp.stack((gain_one, gain_two, gain_three))
    shift_grad = jnp.stack((shift_one, shift_two, shift_three))
    shares = (
        lax.psum_scatter(
            action_grad.astype(jnp.bfloat16), "tm", scatter_dimension=1, tiled=True
        ).astype(jnp.float32),
        lax.psum_scatter(
            gain_grad.astype(jnp.bfloat16), "tm", scatter_dimension=1, tiled=True
        ).astype(jnp.float32),
        lax.psum_scatter(
            shift_grad.astype(jnp.bfloat16), "tm", scatter_dimension=1, tiled=True
        ).astype(jnp.float32),
        lax.psum_scatter(
            space_qkv_grad.astype(jnp.bfloat16), "tm", scatter_dimension=0, tiled=True
        ).astype(jnp.float32),
        lax.psum_scatter(
            space_out_grad.astype(jnp.bfloat16), "tm", scatter_dimension=0, tiled=True
        ).astype(jnp.float32),
        lax.psum_scatter(
            time_qkv_grad.astype(jnp.bfloat16), "tm", scatter_dimension=0, tiled=True
        ).astype(jnp.float32),
        lax.psum_scatter(
            time_out_grad.astype(jnp.bfloat16), "tm", scatter_dimension=0, tiled=True
        ).astype(jnp.float32),
        lax.psum_scatter(
            ffn_in_grad.astype(jnp.bfloat16), "tm", scatter_dimension=0, tiled=True
        ).astype(jnp.float32),
        lax.psum_scatter(
            bias_in_grad.astype(jnp.bfloat16), "tm", scatter_dimension=0, tiled=True
        ).astype(jnp.float32),
        lax.psum_scatter(
            ffn_out_grad.astype(jnp.bfloat16), "tm", scatter_dimension=0, tiled=True
        ).astype(jnp.float32),
        lax.psum_scatter(
            bias_out_grad.astype(jnp.bfloat16), "tm", scatter_dimension=0, tiled=True
        ).astype(jnp.float32),
    )
    summed = (
        lax.psum(shares[0].astype(jnp.bfloat16), ("row", "space")).astype(jnp.float32),
        lax.psum(shares[1].astype(jnp.bfloat16), ("row", "space")).astype(jnp.float32),
        lax.psum(shares[2].astype(jnp.bfloat16), ("row", "space")).astype(jnp.float32),
        lax.psum(shares[3].astype(jnp.bfloat16), ("row", "space")).astype(jnp.float32),
        lax.psum(shares[4].astype(jnp.bfloat16), ("row", "space")).astype(jnp.float32),
        lax.psum(shares[5].astype(jnp.bfloat16), ("row", "space")).astype(jnp.float32),
        lax.psum(shares[6].astype(jnp.bfloat16), ("row", "space")).astype(jnp.float32),
        lax.psum(shares[7].astype(jnp.bfloat16), ("row", "space")).astype(jnp.float32),
        lax.psum(shares[8].astype(jnp.bfloat16), ("row", "space")).astype(jnp.float32),
        lax.psum(shares[9].astype(jnp.bfloat16), ("row", "space")).astype(jnp.float32),
        lax.psum(shares[10].astype(jnp.bfloat16), ("row", "space")).astype(jnp.float32),
    )
    return (
        block_output,
        input_grad,
        summed[0],
        summed[1],
        summed[2],
        summed[3],
        summed[4],
        summed[5],
        summed[6],
        summed[7],
        summed[8],
        summed[9],
        summed[10],
    )


def solution(mesh):
    placed = (
        P("row", "tm", "space", None),
        P(None, "tm"),
        P(None, "tm"),
        P(None, "tm"),
        P("tm", None),
        P("tm", None),
        P("tm", None),
        P("tm", None),
        P("tm", None),
        P("tm"),
        P("tm", None),
        P("tm"),
        P("row", "tm", "space", None),
        P("row", None),
        P("row", "tm"),
    )
    return jax.shard_map(
        body,
        mesh=mesh,
        in_specs=placed,
        out_specs=(
            P("row", "tm", "space", None),
            P("row", "tm", "space", None),
            P(None, "tm"),
            P(None, "tm"),
            P(None, "tm"),
            P("tm", None),
            P("tm", None),
            P("tm", None),
            P("tm", None),
            P("tm", None),
            P("tm"),
            P("tm", None),
            P("tm"),
        ),
        check_vma=False,
    )
```

profile of v0, /device:TPU:0, one launch (start us, length us, event | category | flops | bytes accessed | tf_op | source)
XLA Modules:
  0.0 1762.3 jit_solution(8149239046692288889)
XLA Ops:
  38.7 19.5 %all-gather.11.cloned.1.call-done = bf16[1024,3072]{1,0:T(8,128)(2,1)} async-done(((bf16[128,3072]{1,0:T(8,128)(2,1)}), bf16[1024,3072]{1,0:T(8,128)(2,1)}) %all-gather.11.cloned.1.call-update) | async-done | bytes 6291472 | tf_op jit(solution)/shard_map/all_gather | solution.py:77
  76.5 23.3 %all-gather.15.cloned.1.call-done = bf16[4,256,1024]{2,1,0:T(8,128)(2,1)} async-done(((bf16[4,128,1024]{2,1,0:T(8,128)(2,1)}), bf16[4,256,1024]{2,1,0:T(8,128)(2,1)}) %all-gather.15.cloned.1.call-update) | async-done | bytes 2097168 | tf_op jit(solution)/shard_map/all_gather | solution.py:115
  102.6 32.4 %all-gather.13.cloned.1.call-done = bf16[4,256,1024]{2,1,0:T(8,128)(2,1)} async-done(((bf16[4,128,1024]{2,1,0:T(8,128)(2,1)}), bf16[4,256,1024]{2,1,0:T(8,128)(2,1)}) %all-gather.13.cloned.1.call-update) | async-done | bytes 2097168 | tf_op jit(solution)/shard_map/all_gather | solution.py:116
  168.4 43.6 %all-gather.19.cloned.1.call-done = bf16[1024,3072]{1,0:T(8,128)(2,1)} async-done(((bf16[128,3072]{1,0:T(8,128)(2,1)}), bf16[1024,3072]{1,0:T(8,128)(2,1)}) %all-gather.19.cloned.1.call-update) | async-done | bytes 6291472 | tf_op jit(solution)/shard_map/all_gather | solution.py:79
  238.5 16.5 collective-permute-start.4
  263.4 17.1 collective-permute-done.7
  285.2 64.3 %collective-permute-done.6 = bf16[4,128,1024]{1,2,0:T(8,128)(2,1)} collective-permute-done((bf16[4,128,1024]{1,2,0:T(8,128)(2,1)}, bf16[4,128,1024]{1,2,0:T(8,128)(2,1)}, u32[]{:S(2)}, u32[]{:S(2)}) %collective-permute-start.6) | collective-permute-done | bytes 1048608 | tf_op jit(solution)/shard_map/ppermute | solution.py:22
  355.8 31.8 %collective-permute-done.5 = bf16[4,128,1024]{1,2,0:T(8,128)(2,1)} collective-permute-done((bf16[4,128,1024]{1,2,0:T(8,128)(2,1)}, bf16[4,128,1024]{1,2,0:T(8,128)(2,1)}, u32[]{:S(2)}, u32[]{:S(2)}) %collective-permute-start.5) | collective-permute-done | bytes 1048608 | tf_op jit(solution)/shard_map/ppermute | solution.py:22
  394.4 68.4 %all-gather = bf16[8,1,512]{2,1,0:T(2,128)(2,1)S(1)} all-gather(bf16[1,1,512]{2,1,0:T(2,128)(2,1)S(1)} %reshape.453), channel_id=1, replica_groups=mesh['row'=2,'tm'=8,'space'=2] {'tm'}, dimensions={0}, use_global_device_ids=true | all-gather | bytes 9216 | tf_op jit(solution)/shard_map/all_gather | solution.py:82
  527.1 55.2 %concatenate.56 = bf16[24,128,16,64]{3,0,2,1:T(8,128)(2,1)} concatenate(bf16[4,128,16,64]{3,0,2,1:T(4,128)(2,1)} %copy.114, bf16[4,128,16,64]{3,0,2,1:T(4,128)(2,1)} %copy.115, bf16[4,128,16,64]{3,0,2,1:T(4,128)(2,1)} %copy.116, bf16[4,128,16,64]{3,0,2,1:T(4,128)(2,1)} %copy.117, bf16[4,128,16,64]{3,0,2,1:T(4,128)(2,1)} %copy.118, bf16[4,128,16,64]{3,0,2,1:T(4,128)(2,1)} %copy.119), dimensions={0} | concatenate | bytes 12582912 | tf_op jit(solution)/shard_map/concatenate | solution.py:147
  582.3 55.4 %concatenate.49 = bf16[24,128,16,64]{3,0,2,1:T(8,128)(2,1)} concatenate(bf16[4,128,16,64]{3,0,2,1:T(4,128)(2,1)} %copy.101, bf16[4,128,16,64]{3,0,2,1:T(4,128)(2,1)} %copy.102, bf16[4,128,16,64]{3,0,2,1:T(4,128)(2,1)} %copy.103, bf16[4,128,16,64]{3,0,2,1:T(4,128)(2,1)} %copy.104, bf16[4,128,16,64]{3,0,2,1:T(4,128)(2,1)} %copy.105, bf16[4,128,16,64]{3,0,2,1:T(4,128)(2,1)} %copy.106), dimensions={0} | concatenate | bytes 12582912 | tf_op jit(solution)/shard_map/concatenate | solution.py:148
  680.4 14.0 fusion.82
  709.4 13.1 multiply_reduce_fusion.2
  722.5 16.0 convolution_bitcast_fusion
  738.6 21.1 %copy.128 = f32[24,128,16,64]{1,3,2,0:T(8,128)} copy(f32[24,128,16,64]{3,0,2,1:T(8,128)} %convolution_bitcast_fusion) | data formatting | bytes 25165824 | tf_op jit(solution)/shard_map/phfg,fphe->gphe/transpose | solution.py:216
  780.5 21.1 %copy.126 = f32[24,128,16,64]{1,3,2,0:T(8,128)} copy(f32[24,128,16,64]{3,0,2,1:T(8,128)} %multiply_bitcast_fusion) | data formatting | bytes 25165824 | tf_op jit(solution)/shard_map/mul | solution.py:211
  835.5 39.6 %collective-permute-done.14 = bf16[4,128,2048]{1,2,0:T(8,128)(2,1)} collective-permute-done((bf16[4,128,2048]{1,2,0:T(8,128)(2,1)}, bf16[4,128,2048]{1,2,0:T(8,128)(2,1)}, u32[]{:S(2)}, u32[]{:S(2)}) %collective-permute-start.14) | collective-permute-done | bytes 2097184 | tf_op jit(solution)/shard_map/ppermute | solution.py:22
  882.8 26.7 %collective-permute-done.11 = bf16[4,128,2048]{1,2,0:T(8,128)(2,1)} collective-permute-done((bf16[4,128,2048]{1,2,0:T(8,128)(2,1)}, bf16[4,128,2048]{1,2,0:T(8,128)(2,1)}, u32[]{:S(2)}, u32[]{:S(2)}) %collective-permute-start.11) | collective-permute-done | bytes 2097184 | tf_op jit(solution)/shard_map/ppermute | solution.py:22
  985.8 13.3 convolution_convert_fusion
  1016.4 53.7 %reduce-scatter.20.cloned.1.call-done = bf16[4,128,1024]{2,1,0:T(8,128)(2,1)} async-done(((bf16[4,256,1024]{2,1,0:T(8,128)(2,1)}), bf16[4,128,1024]{2,1,0:T(8,128)(2,1)}) %reduce-scatter.20.cloned.1.call-update) | async-done | bytes 1048592 | tf_op jit(solution)/shard_map/reduce_scatter | solution.py:277
  1071.6 32.5 %reduce-scatter.18.cloned.1.call-done = bf16[4,128,1024]{2,1,0:T(8,128)(2,1)} async-done(((bf16[4,256,1024]{2,1,0:T(8,128)(2,1)}), bf16[4,128,1024]{2,1,0:T(8,128)(2,1)}) %reduce-scatter.18.cloned.1.call-update) | async-done | bytes 1048592 | tf_op jit(solution)/shard_map/reduce_scatter | solution.py:271
  1132.9 15.7 reduce-scatter.28.cloned.1.call-done
  1148.6 45.3 %reduce-scatter.24.cloned.1.call-done = bf16[128,1024]{1,0:T(8,128)(2,1)} async-done(((bf16[1024,1024]{1,0:T(8,128)(2,1)}), bf16[128,1024]{1,0:T(8,128)(2,1)}) %reduce-scatter.24.cloned.1.call-update) | async-done | bytes 262160 | tf_op jit(solution)/shard_map/reduce_scatter | solution.py:316
  1194.0 65.2 %reduce-scatter.26.cloned.1.call-done = bf16[128,3072]{1,0:T(8,128)(2,1)} async-done(((bf16[1024,3072]{1,0:T(8,128)(2,1)}), bf16[128,3072]{1,0:T(8,128)(2,1)}) %reduce-scatter.26.cloned.1.call-update) | async-done | bytes 786448 | tf_op jit(solution)/shard_map/reduce_scatter | solution.py:319
  1259.1 75.0 %reduce-scatter.32.cloned.1.call-done = bf16[512,1024]{1,0:T(8,128)(2,1)} async-done(((bf16[4096,1024]{1,0:T(8,128)(2,1)}), bf16[512,1024]{1,0:T(8,128)(2,1)}) %reduce-scatter.32.cloned.1.call-update) | async-done | bytes 1048592 | tf_op jit(solution)/shard_map/reduce_scatter | solution.py:331
  1334.2 74.6 %reduce-scatter.30.cloned.1.call-done = bf16[128,4096]{1,0:T(8,128)(2,1)} async-done(((bf16[1024,4096]{1,0:T(8,128)(2,1)}), bf16[128,4096]{1,0:T(8,128)(2,1)}) %reduce-scatter.30.cloned.1.call-update) | async-done | bytes 1048592 | tf_op jit(solution)/shard_map/reduce_scatter | solution.py:325
  1408.8 65.4 %reduce-scatter.22.cloned.1.call-done = bf16[128,3072]{1,0:T(8,128)(2,1)} async-done(((bf16[1024,3072]{1,0:T(8,128)(2,1)}), bf16[128,3072]{1,0:T(8,128)(2,1)}) %reduce-scatter.22.cloned.1.call-update) | async-done | bytes 786448 | tf_op jit(solution)/shard_map/reduce_scatter | solution.py:313
  1485.5 24.0 %all-reduce.2 = (bf16[4096]{0:T(1024)(128)(2,1)S(1)}, bf16[1024]{0:T(1024)(128)(2,1)S(1)}) all-reduce(bf16[4096]{0:T(1024)(128)(2,1)S(1)} %copy-done.63, bf16[1024]{0:T(1024)(128)(2,1)S(1)} %reduce_sum.272), channel_id=12, replica_groups=mesh['row'=2,'tm'=8,'space'=2] {'tm'}, use_global_device_ids=true, to_apply=%region_44.45.clone | all-reduce | flops 5120 | bytes 20480
  1509.7 12.3 add_convert_fusion
  1522.8 25.8 %reduce-scatter.38.cloned.1.call-done = bf16[128,3]{1,0:T(8,128)(2,1)} async-done(((bf16[1024,3]{1,0:T(8,128)(2,1)}), bf16[128,3]{1,0:T(8,128)(2,1)}) %reduce-scatter.38.cloned.1.call-update) | async-done | bytes 784
  1549.4 36.5 %reduce-scatter.34.cloned.1.call-done = bf16[128,8]{1,0:T(8,128)(2,1)} async-done(((bf16[1024,8]{1,0:T(8,128)(2,1)}), bf16[128,8]{1,0:T(8,128)(2,1)}) %reduce-scatter.34.cloned.1.call-update) | async-done | bytes 2064
  1601.5 144.0 %all-reduce.7.cloned.1.call-done = (bf16[128,3072]{1,0:T(8,128)(2,1)}, bf16[128,1024]{1,0:T(8,128)(2,1)}, bf16[128,3072]{1,0:T(8,128)(2,1)}, bf16[128,1024]{1,0:...) async-done(((bf16[128,3072]{1,0:T(8,128)(2,1)}, bf16[128,1024]{1,0:T(8,128)(2,1)}, bf16[128,3072]{1,0:T(8,128)(2,1)}, bf16[128,1024]{1,0:T(8,128)(2,1)}, ...) | async-done | bytes 4194320 | tf_op jit(solution)/shard_map/psum | solution.py:342
  (371 shorter events, 482.7 us)
Async XLA Ops:
  7.2 51.0 %all-gather.11.cloned.1.call-start = ((), (), s32[]{:S(2)}) async-start(), calls=%async_computation.11 | async-start | bytes 7077888 | tf_op jit(solution)/shard_map/all_gather | solution.py:77
  7.9 91.8 %all-gather.15.cloned.1.call-start = ((), (), s32[]{:S(2)}) async-start(), calls=%async_computation.13 | async-start | bytes 3145728 | tf_op jit(solution)/shard_map/all_gather | solution.py:115
  66.5 68.6 %all-gather.13.cloned.1.call-start = ((), (), s32[]{:S(2)}) async-start(), calls=%async_computation.12 | async-start | bytes 3145728 | tf_op jit(solution)/shard_map/all_gather | solution.py:116
  67.2 97.5 %all-gather.17.cloned.1.call-start = ((), (), s32[]{:S(2)}) async-start(), calls=%async_computation.14 | async-start | bytes 2359296 | tf_op jit(solution)/shard_map/all_gather | solution.py:78
  67.8 144.2 %all-gather.19.cloned.1.call-start = ((), (), s32[]{:S(2)}) async-start(), calls=%async_computation.15 | async-start | bytes 7077888 | tf_op jit(solution)/shard_map/all_gather | solution.py:79
  68.4 594.8 %all-gather.21.cloned.1.call-start = ((), (), s32[]{:S(2)}) async-start(), calls=%async_computation.16 | async-start | bytes 2359296 | tf_op jit(solution)/shard_map/all_gather | solution.py:80
  69.0 599.2 %all-gather.23.cloned.1.call-start = ((), (), s32[]{:S(2)}) async-start(), calls=%async_computation.17 | async-start | bytes 9437184 | tf_op jit(solution)/shard_map/all_gather | solution.py:81
  69.7 610.6 %all-gather.25.cloned.1.call-start = ((), (), s32[]{:S(2)}) async-start(), calls=%async_computation.18 | async-start | bytes 9437184 | tf_op jit(solution)/shard_map/all_gather | solution.py:83
  70.5 999.6 %reduce-scatter.20.cloned.1.call-start = ((), (), s32[]{:S(2)}) async-start(), calls=%async_computation.20 | async-start | bytes 3145728 | tf_op jit(solution)/shard_map/reduce_scatter | solution.py:277
  229.5 51.0 %collective-permute-start.7 = (bf16[4,128,1024]{1,2,0:T(8,128)(2,1)}, bf16[4,128,1024]{1,2,0:T(8,128)(2,1)}, u32[]{:S(2)}, u32[]{:S(2)}) collective-permute-start(bf16[4,128,1024]{1,2,0:T(8,128)(2,1)} %copy.108), channel_id=1, source_target_pairs={{0,6},{2,8},{4,10},{6,12},{8,14},{1,7},{3,9},{5,11},{7,13},{9,15},... | collective-permute-start | bytes 3145736 | tf_op jit(solution)/shard_map/ppermute | solution.py:22
  232.5 117.0 %collective-permute-start.6 = (bf16[4,128,1024]{1,2,0:T(8,128)(2,1)}, bf16[4,128,1024]{1,2,0:T(8,128)(2,1)}, u32[]{:S(2)}, u32[]{:S(2)}) collective-permute-start(bf16[4,128,1024]{1,2,0:T(8,128)(2,1)} %copy.108), channel_id=1, source_target_pairs={{0,8},{2,10},{4,12},{6,14},{1,9},{3,11},{5,13},{7,15},{16,24},{18,... | collective-permute-start | bytes 3145736 | tf_op jit(solution)/shard_map/ppermute | solution.py:22
  234.8 152.8 %collective-permute-start.5 = (bf16[4,128,1024]{1,2,0:T(8,128)(2,1)}, bf16[4,128,1024]{1,2,0:T(8,128)(2,1)}, u32[]{:S(2)}, u32[]{:S(2)}) collective-permute-start(bf16[4,128,1024]{1,2,0:T(8,128)(2,1)} %copy.108), channel_id=1, source_target_pairs={{0,10},{2,12},{4,14},{1,11},{3,13},{5,15},{16,26},{18,28},{20,30},... | collective-permute-start | bytes 3145736 | tf_op jit(solution)/shard_map/ppermute | solution.py:22
  238.5 266.7 %collective-permute-start.4 = (bf16[4,128,1024]{1,2,0:T(8,128)(2,1)}, bf16[4,128,1024]{1,2,0:T(8,128)(2,1)}, u32[]{:S(2)}, u32[]{:S(2)}) collective-permute-start(bf16[4,128,1024]{1,2,0:T(8,128)(2,1)} %copy.95), channel_id=1, source_target_pairs={{0,2},{2,4},{4,6},{6,8},{8,10},{10,12},{12,14},{1,3},{3,5},{5,7},{... | collective-permute-start | bytes 3145736 | tf_op jit(solution)/shard_map/ppermute | solution.py:22
  258.0 251.6 %collective-permute-start.3 = (bf16[4,128,1024]{1,2,0:T(8,128)(2,1)}, bf16[4,128,1024]{1,2,0:T(8,128)(2,1)}, u32[]{:S(2)}, u32[]{:S(2)}) collective-permute-start(bf16[4,128,1024]{1,2,0:T(8,128)(2,1)} %copy.95), channel_id=1, source_target_pairs={{0,4},{2,6},{4,8},{6,10},{8,12},{10,14},{1,5},{3,7},{5,9},{7,11},{... | collective-permute-start | bytes 3145736 | tf_op jit(solution)/shard_map/ppermute | solution.py:22
  280.4 233.5 %collective-permute-start.2 = (bf16[4,128,1024]{1,2,0:T(8,128)(2,1)}, bf16[4,128,1024]{1,2,0:T(8,128)(2,1)}, u32[]{:S(2)}, u32[]{:S(2)}) collective-permute-start(bf16[4,128,1024]{1,2,0:T(8,128)(2,1)} %copy.95), channel_id=1, source_target_pairs={{0,6},{2,8},{4,10},{6,12},{8,14},{1,7},{3,9},{5,11},{7,13},{9,15},... | collective-permute-start | bytes 3145736 | tf_op jit(solution)/shard_map/ppermute | solution.py:22
  349.5 168.8 %collective-permute-start.1 = (bf16[4,128,1024]{1,2,0:T(8,128)(2,1)}, bf16[4,128,1024]{1,2,0:T(8,128)(2,1)}, u32[]{:S(2)}, u32[]{:S(2)}) collective-permute-start(bf16[4,128,1024]{1,2,0:T(8,128)(2,1)} %copy.95), channel_id=1, source_target_pairs={{0,8},{2,10},{4,12},{6,14},{1,9},{3,11},{5,13},{7,15},{16,24},{18,... | collective-permute-start | bytes 3145736 | tf_op jit(solution)/shard_map/ppermute | solution.py:22
  387.6 135.2 %collective-permute-start = (bf16[4,128,1024]{1,2,0:T(8,128)(2,1)}, bf16[4,128,1024]{1,2,0:T(8,128)(2,1)}, u32[]{:S(2)}, u32[]{:S(2)}) collective-permute-start(bf16[4,128,1024]{1,2,0:T(8,128)(2,1)} %copy.95), channel_id=1, source_target_pairs={{0,10},{2,12},{4,14},{1,11},{3,13},{5,15},{16,26},{18,28},{20,30},... | collective-permute-start | bytes 3145736 | tf_op jit(solution)/shard_map/ppermute | solution.py:22
  819.0 56.1 %collective-permute-start.14 = (bf16[4,128,2048]{1,2,0:T(8,128)(2,1)}, bf16[4,128,2048]{1,2,0:T(8,128)(2,1)}, u32[]{:S(2)}, u32[]{:S(2)}) collective-permute-start(bf16[4,128,2048]{1,2,0:T(8,128)(2,1)} %get-tuple-element.45), channel_id=1, source_target_pairs={{10,0},{12,2},{14,4},{11,1},{13,3},{15,5},{26,16},{28,18},{30,20},... | collective-permute-start | bytes 6291464 | tf_op jit(solution)/shard_map/ppermute | solution.py:22
  820.3 62.6 %collective-permute-start.13 = (bf16[4,128,2048]{1,2,0:T(8,128)(2,1)}, bf16[4,128,2048]{1,2,0:T(8,128)(2,1)}, u32[]{:S(2)}, u32[]{:S(2)}) collective-permute-start(bf16[4,128,2048]{1,2,0:T(8,128)(2,1)} %get-tuple-element.46), channel_id=1, source_target_pairs={{8,0},{10,2},{12,4},{14,6},{9,1},{11,3},{13,5},{15,7},{24,16},{26,... | collective-permute-start | bytes 6291464 | tf_op jit(solution)/shard_map/ppermute | solution.py:22
  821.6 61.3 %collective-permute-start.12 = (bf16[4,128,2048]{1,2,0:T(8,128)(2,1)}, bf16[4,128,2048]{1,2,0:T(8,128)(2,1)}, u32[]{:S(2)}, u32[]{:S(2)}) collective-permute-start(bf16[4,128,2048]{1,2,0:T(8,128)(2,1)} %get-tuple-element.47), channel_id=1, source_target_pairs={{6,0},{8,2},{10,4},{12,6},{14,8},{7,1},{9,3},{11,5},{13,7},{15,9},... | collective-permute-start | bytes 6291464 | tf_op jit(solution)/shard_map/ppermute | solution.py:22
  822.9 86.7 %collective-permute-start.11 = (bf16[4,128,2048]{1,2,0:T(8,128)(2,1)}, bf16[4,128,2048]{1,2,0:T(8,128)(2,1)}, u32[]{:S(2)}, u32[]{:S(2)}) collective-permute-start(bf16[4,128,2048]{1,2,0:T(8,128)(2,1)} %get-tuple-element.48), channel_id=1, source_target_pairs={{4,0},{6,2},{8,4},{10,6},{12,8},{14,10},{5,1},{7,3},{9,5},{11,7},{... | collective-permute-start | bytes 6291464 | tf_op jit(solution)/shard_map/ppermute | solution.py:22
  947.7 156.4 %reduce-scatter.18.cloned.1.call-start = ((), (), s32[]{:S(2)}) async-start(), calls=%async_computation.19 | async-start | bytes 3145728 | tf_op jit(solution)/shard_map/reduce_scatter | solution.py:271
  967.9 180.7 %reduce-scatter.28.cloned.1.call-start = ((), (), s32[]{:S(2)}) async-start(), calls=%async_computation.24 | async-start | bytes 2359296 | tf_op jit(solution)/shard_map/reduce_scatter | solution.py:322
  972.1 221.8 %reduce-scatter.24.cloned.1.call-start = ((), (), s32[]{:S(2)}) async-start(), calls=%async_computation.22 | async-start | bytes 2359296 | tf_op jit(solution)/shard_map/reduce_scatter | solution.py:316
  976.7 282.4 %reduce-scatter.26.cloned.1.call-start = ((), (), s32[]{:S(2)}) async-start(), calls=%async_computation.23 | async-start | bytes 7077888 | tf_op jit(solution)/shard_map/reduce_scatter | solution.py:319
  985.1 349.1 %reduce-scatter.32.cloned.1.call-start = ((), (), s32[]{:S(2)}) async-start(), calls=%async_computation.26 | async-start | bytes 9437184 | tf_op jit(solution)/shard_map/reduce_scatter | solution.py:331
  999.2 409.6 %reduce-scatter.30.cloned.1.call-start = ((), (), s32[]{:S(2)}) async-start(), calls=%async_computation.25 | async-start | bytes 9437184 | tf_op jit(solution)/shard_map/reduce_scatter | solution.py:325
  1009.9 464.2 %reduce-scatter.22.cloned.1.call-start = ((), (), s32[]{:S(2)}) async-start(), calls=%async_computation.21 | async-start | bytes 7077888 | tf_op jit(solution)/shard_map/reduce_scatter | solution.py:313
  1115.8 406.2 %reduce-scatter.36.cloned.1.call-start = ((), (), s32[]{:S(2)}) async-start(), calls=%async_computation.28 | async-start | bytes 294912
  1126.8 421.8 %reduce-scatter.38.cloned.1.call-start = ((), (), s32[]{:S(2)}) async-start(), calls=%async_computation.29 | async-start | bytes 294912
  1131.6 454.3 %reduce-scatter.34.cloned.1.call-start = ((), (), s32[]{:S(2)}) async-start(), calls=%async_computation.27 | async-start | bytes 294912
  1132.8 612.7 %all-reduce.7.cloned.1.call-start = ((), (), s32[]{:S(2)}) async-start(), calls=%async_computation.30 | async-start | bytes 8388608 | tf_op jit(solution)/shard_map/psum | solution.py:342
  (82 other events, 3444.1 us)
Sparse Core Ops, SparseCore 0:
  9.9 48.2 all-gather.10
  66.6 33.1 all-gather.14
  101.9 33.1 all-gather.12
  136.8 27.8 all-gather.16
  166.4 45.5 all-gather.18
  213.7 114.6 all-gather.20
  330.3 85.8 all-gather.22
  418.2 67.9 all-gather.24
  947.8 122.2 reduce-scatter.19
  1072.2 31.8 reduce-scatter.17
  1107.4 41.1 reduce-scatter.27
  1152.7 41.2 reduce-scatter.23
  1197.3 61.7 reduce-scatter.25
  1262.8 71.2 reduce-scatter.31
  1337.5 71.2 reduce-scatter.29
  1412.4 61.7 reduce-scatter.21
  1477.6 33.6 reduce-scatter.35
  1515.0 33.5 reduce-scatter.37
  1552.2 33.6 reduce-scatter.33
  1588.8 156.7 all-reduce.6
where the time goes:
time: 1780 us; the launch traced here: 1760 us
  waiting for transfers between devices  958 us (54%)
  local copies, waits for them, and re-layouts  299 us (17%)
  matrix products  233 us (13%)
  blocking collectives  140 us (8%)
  starting transfers between devices  61.4 us (3%)
  other arithmetic  53.6 us (3%)
    ppermute x15, waiting for transfers between devices, passed_along(): return lax.ppermute(block, axis, route)  190 us
    psum x1, waiting for transfers between devices, body(): lax.psum(shares[3].astype(jnp.bfloat16), ('row', 'space'))  144 us
    concatenate x8, local copies, waits for them, and re-layouts, body(): jnp.concatenate(key_pieces, axis=0)  87.1 us
    concatenate x8, local copies, waits for them, and re-layouts, body(): jnp.concatenate(value_pieces, axis=0)  83.6 us
    reduce_scatter x1, waiting for transfers between devices, body(): lax.psum_scatter(ffn_out_grad.astype(jnp.bfloat16), 'tm', scatter_dimensi...  75 us
    reduce_scatter x1, waiting for transfers between devices, body(): lax.psum_scatter(ffn_in_grad.astype(jnp.bfloat16), 'tm', scatter_dimensio...  74.6 us
    all_gather x1, blocking collectives, body(): lax.all_gather(ffn_bias_in, 'tm', axis=0, tiled=True)  68.4 us
    unnamed x23, waiting for transfers between devices  66.8 us
  transfers between devices with their start and end apart: 35, of which 23 were waited for; matrix products, arithmetic and copies ran while one was open for 22% of the time, Pallas kernels for 0%

commit v1 on v0

v1 whole, which is shorter than its diff:
```python
import math

import jax
import jax.numpy as jnp
from jax import lax
from jax.experimental import pallas as pl
from jax.experimental.pallas import tpu as pltpu
from jax.sharding import PartitionSpec as P

MODEL = 1024
HEADS = 16
HEAD_DIM = 64
ACTIONS = 8
TILE = 256
PAIR = 2 * HEAD_DIM
PAIRS = HEADS // 2
SCALE = 1.0 / math.sqrt(HEAD_DIM)

EPSILON = 1e-05
NEG_FILL = -1e30
BF = jnp.bfloat16
F32 = jnp.float32


def layer_norm(values, gain_row, shift_row):
    row_mean = jnp.mean(values, axis=-1, keepdims=True)
    centred = values - row_mean
    spread = jnp.mean(centred * centred, axis=-1, keepdims=True)
    return centred * lax.rsqrt(spread + EPSILON) * gain_row + shift_row


def forward_dot(values, weight):
    return jnp.dot(values, weight, preferred_element_type=F32)


def weight_grad(left_rows, right_rows):
    return lax.dot_general(
        left_rows, right_rows, (((0,), (0,)), ((), ())), preferred_element_type=F32
    )


def back_dot(grad_rows, weight):
    return lax.dot_general(
        grad_rows, weight, (((1,), (1,)), ((), ())), preferred_element_type=F32
    )


def dot_nt(a, b):
    return lax.dot_general(a, b, (((1,), (1,)), ((), ())), preferred_element_type=F32)


def dot_nn(a, b):
    return lax.dot_general(a, b, (((1,), (0,)), ((), ())), preferred_element_type=F32)


def dot_tn(a, b):
    return lax.dot_general(a, b, (((0,), (0,)), ((), ())), preferred_element_type=F32)


def of_head(half, values):
    lane = lax.broadcasted_iota(jnp.int32, values.shape, 1)
    keep = (lane < HEAD_DIM) if half == 0 else (lane >= HEAD_DIM)
    return jnp.where(keep, values, jnp.zeros_like(values))


def join_heads(first, second):
    lane = lax.broadcasted_iota(jnp.int32, first.shape, 1)
    return jnp.where(lane < HEAD_DIM, first, second)


def pair_cols(pair, part):
    return pl.ds(pl.multiple_of(part * MODEL + pair * PAIR, PAIR), PAIR)


def attn_fwd_kernel(tiles, masked, packed_ref, *refs):
    if masked:
        col_ref, row_ref, mixed_ref, probs_ref = refs
    else:
        mixed_ref, probs_ref = refs

    def one_pair(pair, carry):
        for t in range(tiles):
            mine = pl.ds(t * TILE, TILE)
            width = (t + 1) * TILE
            seen = pl.ds(0, width)
            query = packed_ref[mine, pair_cols(pair, 0)] * jnp.asarray(SCALE, BF)
            key = packed_ref[seen, pair_cols(pair, 1)]
            value = packed_ref[seen, pair_cols(pair, 2)]
            if masked:
                same = col_ref[mine, :] == row_ref[:, seen]
                order = lax.broadcasted_iota(
                    jnp.int32, (TILE, width), 0
                ) + t * TILE >= lax.broadcasted_iota(jnp.int32, (TILE, width), 1)
                allowed = same & order
            outs = []
            for half in range(2):
                scores = dot_nt(of_head(half, query), key)
                if masked:
                    scores = jnp.where(allowed, scores, NEG_FILL)
                top = jnp.max(scores, axis=1, keepdims=True)
                raised = jnp.exp(scores - top)
                total = jnp.sum(raised, axis=1, keepdims=True)
                probs = (raised * (1.0 / total)).astype(BF)
                probs_ref[2 * pair + half, mine, seen] = probs
                outs.append(dot_nn(probs, value))
            mixed_ref[mine, pair_cols(pair, 0)] = join_heads(*outs).astype(BF)
        return carry

    lax.fori_loop(0, PAIRS, one_pair, 0, unroll=2)


def attn_bwd_kernel(tiles, packed_ref, probs_ref, grad_ref, out_ref, key_acc, value_acc):
    def one_pair(pair, carry):
        for t in reversed(range(tiles)):
            mine = pl.ds(t * TILE, TILE)
            seen = pl.ds(0, (t + 1) * TILE)
            query = packed_ref[mine, pair_cols(pair, 0)] * jnp.asarray(SCALE, BF)
            key = packed_ref[seen, pair_cols(pair, 1)]
            value = packed_ref[seen, pair_cols(pair, 2)]
            grad = grad_ref[mine, pair_cols(pair, 0)]
            dqs, dks, dvs = [], [], []
            for half in range(2):
                probs_low = probs_ref[2 * pair + half, mine, seen]
                probs = probs_low.astype(F32)
                dprobs = dot_nt(of_head(half, grad), value)
                delta = jnp.sum(dprobs * probs, axis=1, keepdims=True)
                dscores = (probs * (dprobs - delta)).astype(BF)
                dqs.append(dot_nn(dscores, key))
                dks.append(dot_tn(dscores, query))
                dvs.append(dot_tn(probs_low, grad))
            out_ref[mine, pair_cols(pair, 0)] = (join_heads(*dqs) * SCALE).astype(BF)
            dkey, dvalue = join_heads(*dks), join_heads(*dvs)
            if tiles == 1:
                out_ref[seen, pair_cols(pair, 1)] = dkey.astype(BF)
                out_ref[seen, pair_cols(pair, 2)] = dvalue.astype(BF)
            elif t == tiles - 1:
                key_acc[...] = dkey
                value_acc[...] = dvalue
            else:
                key_acc[seen, :] += dkey
                value_acc[seen, :] += dvalue
        if tiles > 1:
            out_ref[:, pair_cols(pair, 1)] = key_acc[...].astype(BF)
            out_ref[:, pair_cols(pair, 2)] = value_acc[...].astype(BF)
        return carry

    lax.fori_loop(0, PAIRS, one_pair, 0, unroll=2)


def blocks(rows, span):
    return {
        "packed": pl.BlockSpec((span, 3 * MODEL), lambda t: (t, 0)),
        "mixed": pl.BlockSpec((span, MODEL), lambda t: (t, 0)),
        "probs": pl.BlockSpec((HEADS, span, span), lambda t: (0, t, 0)),
        "col": pl.BlockSpec((span, 1), lambda t: (t, 0)),
        "row": pl.BlockSpec((1, span), lambda t: (0, t)),
    }


def attention(packed, span, groups=None):
    rows = packed.shape[0]
    at = blocks(rows, span)
    masked = groups is not None
    extra = (groups[:, None], groups[None, :]) if masked else ()
    specs = [at["packed"]] + ([at["col"], at["row"]] if masked else [])
    return pl.pallas_call(
        lambda *refs: attn_fwd_kernel(span // TILE, masked, *refs),
        grid=(rows // span,),
        in_specs=specs,
        out_specs=[at["mixed"], at["probs"]],
        out_shape=[
            jax.ShapeDtypeStruct((rows, MODEL), BF),
            jax.ShapeDtypeStruct((HEADS, rows, span), BF),
        ],
        compiler_params=pltpu.CompilerParams(vmem_limit_bytes=48 * 2**20),
        cost_estimate=pl.CostEstimate(
            flops=8 * HEADS * rows * span * HEAD_DIM,
            bytes_accessed=rows * (8 * MODEL + 2 * HEADS * span),
            transcendentals=HEADS * rows * span,
        ),
        name="attention_forward",
    )(packed, *extra)


def attention_back(packed, probs, grad, span):
    rows = packed.shape[0]
    at = blocks(rows, span)
    return pl.pallas_call(
        lambda *refs: attn_bwd_kernel(span // TILE, *refs),
        grid=(rows // span,),
        in_specs=[at["packed"], at["probs"], at["mixed"]],
        out_specs=at["packed"],
        out_shape=jax.ShapeDtypeStruct((rows, 3 * MODEL), BF),
        scratch_shapes=[pltpu.VMEM((span, PAIR), F32), pltpu.VMEM((span, PAIR), F32)],
        compiler_params=pltpu.CompilerParams(vmem_limit_bytes=48 * 2**20),
        cost_estimate=pl.CostEstimate(
            flops=16 * HEADS * rows * span * HEAD_DIM,
            bytes_accessed=rows * (14 * MODEL + 2 * HEADS * span),
            transcendentals=0,
        ),
        name="attention_backward",
    )(packed, probs, grad)


def hop(block, axis, flip):
    size = lax.axis_size(axis)
    return lax.ppermute(block, axis, [(i, i ^ flip) for i in range(size)])


def add_low(one, other):
    return (one.astype(F32) + other.astype(F32)).astype(BF)


def lay_kernel(rows, places, *refs):
    parts, whole_ref, done = refs[: len(places)], refs[-2], refs[-1]
    me = lax.axis_index("tm")
    copies = []
    for i, (flip, start) in enumerate(places):
        at = pl.multiple_of((me ^ flip) * rows + start, 32)
        target = whole_ref.at[pl.ds(at, parts[i].shape[0]), :]
        copies.append(pltpu.make_async_copy(parts[i], target, done.at[i]))
        copies[-1].start()
    for copy in copies:
        copy.wait()


def gather_rows(block):
    if lax.axis_size("tm") != 8:
        return lax.all_gather(block, "tm", axis=0, tiled=True)
    rows = block.shape[0]
    half = rows // 2
    me = lax.axis_index("tm")
    by_two, by_four = hop(block, "tm", 2), hop(block, "tm", 4)
    low_six, high_six = hop(by_two[:half], "tm", 4), hop(by_four[half:], "tm", 2)
    pieces = ((block, 0, 0), (by_two, 2, 0), (by_four, 4, 0), (low_six, 6, 0), (high_six, 6, half))
    parts, places = [], []
    for piece, flip, start in pieces:
        for core in range(2):
            parts.append(hop(piece, "tm", 1) if core else piece)
            places.append((flip + core, start))
    return pl.pallas_call(
        lambda *refs: lay_kernel(rows, places, *refs),
        in_specs=[pl.BlockSpec(memory_space=pl.ANY)] * len(parts),
        out_specs=pl.BlockSpec(memory_space=pl.ANY),
        out_shape=jax.ShapeDtypeStruct((8 * rows,) + block.shape[1:], block.dtype),
        scratch_shapes=[pltpu.SemaphoreType.DMA((len(parts),))],
        cost_estimate=pl.CostEstimate(
            flops=0, bytes_accessed=32 * rows * block.shape[1], transcendentals=0
        ),
        name="lay_rows",
    )(*parts)


def scatter_rows(whole):
    size = lax.axis_size("tm")
    whole = whole.astype(BF)
    if size != 8:
        return lax.psum_scatter(whole, "tm", scatter_dimension=0, tiled=True)
    rows = whole.shape[0] // 8
    half = rows // 2
    me = lax.axis_index("tm")

    def share(flip):
        return lax.dynamic_slice(whole, ((me ^ flip) * rows, 0), (rows, whole.shape[1]))

    chip = {flip: add_low(share(flip), hop(share(flip + 1), "tm", 1)) for flip in (0, 2, 4, 6)}
    two, two_six = hop(chip[2][:half], "tm", 2), hop(chip[6][:half], "tm", 2)
    four, four_six = hop(chip[4][half:], "tm", 4), hop(chip[6][half:], "tm", 4)
    top = add_low(chip[0][:half], two)
    top_far = add_low(chip[4][:half], two_six)
    low = add_low(chip[0][half:], four)
    low_far = add_low(chip[2][half:], four_six)
    return jnp.concatenate(
        (add_low(top, hop(top_far, "tm", 4)), add_low(low, hop(low_far, "tm", 2))), axis=0
    )


def sum_planes(block):
    rows = block.shape[0]
    half, quarter = rows // 2, rows // 4
    cols = block.shape[1]
    mine, ours = lax.axis_index("space"), lax.axis_index("row")

    def cut(array, start, length):
        return lax.dynamic_slice(array, (start, 0), (length, cols))

    one = add_low(
        cut(block, mine * half, half), hop(cut(block, (1 - mine) * half, half), "space", 1)
    )
    two = add_low(
        cut(one, ours * quarter, quarter), hop(cut(one, (1 - ours) * quarter, quarter), "row", 1)
    )
    other = hop(two, "row", 1)
    both = jnp.where(
        ours == 0, jnp.concatenate((two, other), axis=0), jnp.concatenate((other, two), axis=0)
    )
    far = hop(both, "space", 1)
    return jnp.where(
        mine == 0, jnp.concatenate((both, far), axis=0), jnp.concatenate((far, both), axis=0)
    ).astype(F32)


def reduce_grad(whole):
    return sum_planes(scatter_rows(whole))


def gather_small(flat):
    size = lax.axis_size("tm")
    if size != 8:
        return lax.all_gather(flat, "tm", axis=0)
    me = lax.axis_index("tm")
    whole = jnp.zeros((size,) + flat.shape, flat.dtype)
    for flip in range(size):
        part = hop(flat, "tm", flip) if flip else flat
        whole = lax.dynamic_update_slice(whole, part[None], (me ^ flip,) + (0,) * flat.ndim)
    return whole


def scatter_small(shares):
    size = lax.axis_size("tm")
    if size != 8:
        own = lax.psum_scatter(shares, "tm", scatter_dimension=0, tiled=True)[0]
        return lax.psum(own, ("row", "space"))
    me = lax.axis_index("tm")
    own = lax.dynamic_index_in_dim(shares, me, 0, keepdims=False)
    for flip in range(1, size):
        own = own + hop(
            lax.dynamic_index_in_dim(shares, me ^ flip, 0, keepdims=False), "tm", flip
        )
    own = own + hop(own, "space", 1)
    return own + hop(own, "row", 1)


def body(
    block_input,
    action_table,
    norm_gain,
    norm_bias,
    space_qkv,
    space_out,
    time_qkv,
    time_out,
    ffn_in,
    ffn_bias_in,
    ffn_out,
    ffn_bias_out,
    out_grad,
    frame_segment,
    frame_action,
):
    tm, halves = lax.axis_size("tm"), lax.axis_size("space")
    slot, side = lax.axis_index("tm"), lax.axis_index("space")
    frame_count, half_grid = block_input.shape[1], block_input.shape[2]
    own_frames = frame_count // halves
    grid_all = half_grid * halves
    cut = half_grid // tm
    all_frames = frame_count * tm
    rows_dev = frame_count * half_grid
    width = MODEL // tm
    hidden_units = ffn_bias_in.shape[0]

    small = gather_small(
        jnp.concatenate(
            [a.reshape(-1, width) for a in (action_table, norm_gain, norm_bias)]
            + [ffn_bias_out.reshape(1, width), ffn_bias_in.reshape(-1, width)]
        )
    )
    lines = ACTIONS + 7
    by_row = small[:, :lines].transpose(1, 0, 2).reshape(lines, MODEL)
    table_full = by_row[:ACTIONS]
    gains = by_row[ACTIONS : ACTIONS + 3].astype(F32)
    shifts = by_row[ACTIONS + 3 : ACTIONS + 6].astype(F32)
    bias_out = by_row[ACTIONS + 6].astype(F32)
    bias_in = small[:, lines:].reshape(-1).astype(F32)

    inputs = lax.all_to_all(block_input[0], "space", 0, 1, tiled=True)
    actions = lax.dynamic_slice(frame_action[0], (side * own_frames,), (own_frames,))
    one_hot = (actions[:, None] == jnp.arange(ACTIONS)[None, :]).astype(BF)
    embedded = forward_dot(one_hot, table_full)

    space_in_w = gather_rows(space_qkv)
    space_out_w = gather_rows(space_out)
    time_in_w = gather_rows(time_qkv)
    time_out_w = gather_rows(time_out)
    ffn_in_w = gather_rows(ffn_in)
    ffn_out_w = gather_rows(ffn_out)

    hidden_zero = (inputs.astype(F32) + embedded[:, None, :]).reshape(rows_dev, MODEL)
    normed_one = layer_norm(hidden_zero, gains[0], shifts[0]).astype(BF)
    packed_one = forward_dot(normed_one, space_in_w).astype(BF)
    space_mixed, space_probs = attention(packed_one, grid_all)
    hidden_one_own = (hidden_zero + forward_dot(space_mixed, space_out_w)).astype(BF)

    sent = hidden_one_own.reshape(own_frames, halves * tm, cut, MODEL)
    came = lax.all_to_all(sent, ("space", "tm"), 1, 0)
    hidden_one = (
        came.reshape(halves, tm, own_frames, cut, MODEL)
        .transpose(1, 0, 2, 3, 4)
        .reshape(rows_dev, MODEL)
        .astype(F32)
    )
    grad_out_low = lax.all_to_all(out_grad[0], "tm", 1, 0, tiled=True).reshape(rows_dev, MODEL)
    grad_out = grad_out_low.astype(F32)
    groups = (
        frame_segment[0].astype(jnp.int32)[:, None] * cut + jnp.arange(cut, dtype=jnp.int32)
    ).reshape(rows_dev)

    normed_two = layer_norm(hidden_one, gains[1], shifts[1]).astype(BF)
    packed_two = forward_dot(normed_two, time_in_w).astype(BF)
    time_mixed, time_probs = attention(packed_two, rows_dev, groups)
    hidden_two = hidden_one + forward_dot(time_mixed, time_out_w)
    normed_three = layer_norm(hidden_two, gains[2], shifts[2]).astype(BF)
    pre_act = forward_dot(normed_three, ffn_in_w) + bias_in
    activated, gelu_pull = jax.vjp(jax.nn.gelu, pre_act)
    act_low = activated.astype(BF)
    block_out = (hidden_two + forward_dot(act_low, ffn_out_w) + bias_out).astype(BF)
    block_output = lax.all_to_all(
        block_out.reshape(all_frames, cut, MODEL), "tm", 0, 1, tiled=True
    )[None]

    ffn_out_grad = reduce_grad(weight_grad(act_low, grad_out_low))
    bias_out_grad = jnp.sum(grad_out, axis=0)
    grad_pre = gelu_pull(back_dot(grad_out_low, ffn_out_w))[0]
    grad_pre_low = grad_pre.astype(BF)
    ffn_in_grad = reduce_grad(weight_grad(normed_three, grad_pre_low))
    bias_in_grad = jnp.sum(grad_pre_low.astype(F32), axis=0)
    norm_pull = jax.vjp(layer_norm, hidden_two, gains[2], shifts[2])[1]
    grad_hidden, gain_three, shift_three = norm_pull(back_dot(grad_pre_low, ffn_in_w))
    grad_two = grad_out + grad_hidden
    time_branch = grad_two.astype(BF)
    time_out_grad = reduce_grad(weight_grad(time_mixed, time_branch))
    time_grad_mixed = back_dot(time_branch, time_out_w).astype(BF)
    grad_packed_two = attention_back(packed_two, time_probs, time_grad_mixed, rows_dev)
    time_qkv_grad = reduce_grad(weight_grad(normed_two, grad_packed_two))
    norm_pull = jax.vjp(layer_norm, hidden_one, gains[1], shifts[1])[1]
    grad_hidden, gain_two, shift_two = norm_pull(back_dot(grad_packed_two, time_in_w))
    grad_one_low = (grad_two + grad_hidden).astype(BF)

    sent = (
        grad_one_low.reshape(tm, halves, own_frames, cut, MODEL)
        .transpose(1, 0, 2, 3, 4)
        .reshape(halves * tm, own_frames, cut, MODEL)
    )
    space_branch = lax.all_to_all(sent, ("space", "tm"), 0, 1).reshape(rows_dev, MODEL)
    space_out_grad = reduce_grad(weight_grad(space_mixed, space_branch))
    space_grad_mixed = back_dot(space_branch, space_out_w).astype(BF)
    grad_packed_one = attention_back(packed_one, space_probs, space_grad_mixed, grid_all)
    space_qkv_grad = reduce_grad(weight_grad(normed_one, grad_packed_one))
    norm_pull = jax.vjp(layer_norm, hidden_zero, gains[0], shifts[0])[1]
    grad_hidden, gain_one, shift_one = norm_pull(back_dot(grad_packed_one, space_in_w))
    grad_zero = space_branch.astype(F32) + grad_hidden
    frame_grad = jnp.sum(grad_zero.reshape(own_frames, grid_all, MODEL), axis=1)
    action_grad = jnp.dot(one_hot.astype(F32).T, frame_grad, precision=lax.Precision.HIGHEST)
    input_grad = lax.all_to_all(
        grad_zero.astype(BF).reshape(own_frames, grid_all, MODEL), "space", 1, 0, tiled=True
    ).astype(F32)[None]

    by_row = jnp.concatenate(
        (
            action_grad,
            jnp.stack((gain_one, gain_two, gain_three, shift_one, shift_two, shift_three)),
            bias_out_grad[None],
        )
    )
    shares = jnp.concatenate(
        (
            by_row.reshape(lines, tm, width).transpose(1, 0, 2),
            bias_in_grad.reshape(tm, -1, width),
        ),
        axis=1,
    )
    small_grads = scatter_small(shares)
    return (
        block_output,
        input_grad,
        small_grads[:ACTIONS],
        small_grads[ACTIONS : ACTIONS + 3],
        small_grads[ACTIONS + 3 : ACTIONS + 6],
        space_qkv_grad,
        space_out_grad,
        time_qkv_grad,
        time_out_grad,
        ffn_in_grad,
        small_grads[lines:].reshape(hidden_units),
        ffn_out_grad,
        small_grads[ACTIONS + 6],
    )


def solution(mesh):
    placed = (
        P("row", "tm", "space", None),
        P(None, "tm"),
        P(None, "tm"),
        P(None, "tm"),
        P("tm", None),
        P("tm", None),
        P("tm", None),
        P("tm", None),
        P("tm", None),
        P("tm"),
        P("tm", None),
        P("tm"),
        P("row", "tm", "space", None),
        P("row", None),
        P("row", "tm"),
    )
    return jax.shard_map(
        body,
        mesh=mesh,
        in_specs=placed,
        out_specs=(
            P("row", "tm", "space", None),
            P("row", "tm", "space", None),
            P(None, "tm"),
            P(None, "tm"),
            P(None, "tm"),
            P("tm", None),
            P("tm", None),
            P("tm", None),
            P("tm", None),
            P("tm", None),
            P("tm"),
            P("tm", None),
            P("tm"),
        ),
        check_vma=False,
    )
```

time: 1780 us -> 1770 us (level)
  Pallas kernels: 0 us -> 1090 us
  waiting for transfers between devices: 958 us -> 290 us
  local copies, waits for them, and re-layouts: 299 us -> 65.8 us
  blocking collectives: 140 us -> 0 us
  matrix products: 233 us -> 116 us
  starting transfers between devices: 61.4 us -> 156 us
    pallas_call x0 -> x10, Pallas kernels: none -> 1090 us  [the longest x6 1020 us: gather_rows(): pl.pallas_call(lambda *refs: lay_kernel(rows, places, *refs), in_specs=[p...]
    reduce_scatter x8 -> x0, waiting for transfers between devices: 427 us -> none  [the longest x1 75 us: body(): lax.psum_scatter(ffn_out_grad.astype(jnp.bfloat16), 'tm', scatter_dimensi...]
    concatenate x17 -> x2, local copies, waits for them, and re-layouts: 171 us -> 4.94 us  [the longest x1 2.75 us: body(): jnp.concatenate((action_grad, jnp.stack((gain_one, gain_two, gain_three,...]
    psum x1 -> x0, waiting for transfers between devices: 144 us -> none  [body(): lax.psum(shares[3].astype(jnp.bfloat16), ('row', 'space'))]
    all_gather x8 -> x0, waiting for transfers between devices: 130 us -> none  [the longest x1 43.6 us: body(): lax.all_gather(time_qkv, 'tm', axis=0, tiled=True)]
    all_gather x5 -> x0, blocking collectives: 104 us -> none  [the longest x1 68.4 us: body(): lax.all_gather(ffn_bias_in, 'tm', axis=0, tiled=True)]
    ppermute x15 -> x154, waiting for transfers between devices: 190 us -> 290 us  [hop(): return lax.ppermute(block, axis, [(i, i ^ flip) for i in range(size)])]
    dot_general x18 -> x8, matrix products: 126 us -> 41 us  [the longest x7 40.1 us: forward_dot(): return jnp.dot(values, weight, preferred_element_type=F32)]
  transfers between devices with their start and end apart: 35 -> 160, of which waited for: 23 -> 46; matrix products, arithmetic and copies ran while one was open for 22% -> 7% of each run, Pallas kernels for 0% -> 60%
where the time goes in v1:
time: 1770 us
  Pallas kernels  1090 us (62%)
  waiting for transfers between devices  290 us (16%)
  starting transfers between devices  156 us (9%)
  matrix products  116 us (7%)
  local copies, waits for them, and re-layouts  65.8 us (4%)
  other arithmetic  47.9 us (3%)
    pallas_call x6, Pallas kernels, gather_rows(): pl.pallas_call(lambda *refs: lay_kernel(rows, places, *refs), in_specs=[p...  1020 us
    ppermute x154, waiting for transfers between devices, hop(): return lax.ppermute(block, axis, [(i, i ^ flip) for i in range(size)])  290 us
    ppermute x154, starting transfers between devices, hop(): return lax.ppermute(block, axis, [(i, i ^ flip) for i in range(size)])  130 us
    dot_general x7, matrix products, forward_dot(): return jnp.dot(values, weight, preferred_element_type=F32)  40.1 us
    dot_general x6, matrix products, back_dot(): lax.dot_general(grad_rows, weight, (((1,), (1,)), ((), ())), preferred_el...  38.5 us
    dot_general x6, matrix products, weight_grad(): lax.dot_general(left_rows, right_rows, (((0,), (0,)), ((), ())), preferre...  36.8 us
    pallas_call x2, Pallas kernels, attention_back(): pl.pallas_call(lambda *refs: attn_bwd_kernel(span // TILE, *refs), grid=(...  35.9 us
  transfers between devices with their start and end apart: 160, of which 46 were waited for; matrix products, arithmetic and copies ran while one was open for 7% of the time, Pallas kernels for 60%

profile of v1, /device:TPU:0, one launch (start us, length us, event | category | flops | bytes accessed | tf_op | source)
XLA Modules:
  0.0 1765.0 jit_solution(1097326651847637100)
XLA Ops:
  50.7 13.4 collective-permute-done.8.refs_2_
  67.8 13.2 collective-permute-done.26.refs_2_
  87.3 16.1 collective-permute-done.44.refs_2_
  104.2 21.7 %collective-permute-done.53.refs_2_ = bf16[512,1024]{1,0:T(8,128)(2,1)} collective-permute-done((bf16[512,1024]{1,0:T(8,128)(2,1)}, bf16[512,1024]{1,0:T(8,128)(2,1)}, u32[]{:S(2)}, u32[]{:S(2)}) %collective-permute-start.53) | collective-permute-done | bytes 1048608 | tf_op jit(solution)/shard_map/ppermute | solution.py:207
  125.9 8.7 collective-permute-done.12.refs_6_
  135.4 64.7 %lay_rows.7 = bf16[1024,1024]{1,0:T(8,128)(2,1)} custom-call(bf16[128,1024]{1,0:T(8,128)(2,1)} %refs_0_.7, bf16[128,1024]{1,0:T(8,128)(2,1)} %collective-permute-done.16.refs_1_, bf16[128,1024]{1,0:T(8,128)(2,1)} %copy-done.42, bf16[128,1024]{1,0:T(8,128)(2,1)} %collective-permute-done.18.refs_3_, bf16[128,1024]{1,0:T(8,128)(2,1)} %copy-done.43, ...), custom_call_target="tpu_custom_call" | custom-call | bytes 4194304 | tf_op jit(solution)/shard_map/lay_rows/pallas_call | solution.py:241
  222.9 191.8 %lay_rows.6 = bf16[1024,3072]{1,0:T(8,128)(2,1)} custom-call(bf16[128,3072]{1,0:T(8,128)(2,1)} %refs_0_.6, bf16[128,3072]{1,0:T(8,128)(2,1)} %copy-done.39, bf16[128,3072]{1,0:T(8,128)(2,1)} %collective-permute-done.8.refs_2_, bf16[128,3072]{1,0:T(8,128)(2,1)} %collective-permute-done.9.refs_3_, bf16[128,3072]{1,0:T(8,128)(2,1)} %collective-permute-done.10.refs_4_, ...), custom_call_target="tpu_custom_call" | custom-call | bytes 12582912 | tf_op jit(solution)/shard_map/lay_rows/pallas_call | solution.py:241
  424.3 10.4 attention_forward.2
  452.5 64.7 %lay_rows.9 = bf16[1024,1024]{1,0:T(8,128)(2,1)} custom-call(bf16[128,1024]{1,0:T(8,128)(2,1)} %refs_0_.9, bf16[128,1024]{1,0:T(8,128)(2,1)} %copy-done.60, bf16[128,1024]{1,0:T(8,128)(2,1)} %copy-done.40, bf16[128,1024]{1,0:T(8,128)(2,1)} %copy-done.61, bf16[128,1024]{1,0:T(8,128)(2,1)} %copy-done.41, bf16[128,1024]{1,0:T(8,128)(2,1)} %copy-done.62, ...), custom_call_target="tpu_custom_call" | custom-call | bytes 4194304 | tf_op jit(solution)/shard_map/lay_rows/pallas_call | solution.py:241
  519.5 191.8 %lay_rows.8 = bf16[1024,3072]{1,0:T(8,128)(2,1)} custom-call(bf16[128,3072]{1,0:T(8,128)(2,1)} %refs_0_.8, bf16[128,3072]{1,0:T(8,128)(2,1)} %collective-permute-done.25.refs_1_, bf16[128,3072]{1,0:T(8,128)(2,1)} %collective-permute-done.26.refs_2_, bf16[128,3072]{1,0:T(8,128)(2,1)} %collective-permute-done.27.refs_3_, bf16[128,3072]{1,0:T(8,128)(2,1)} %copy-done.31, ...), custom_call_target="tpu_custom_call" | custom-call | bytes 12582912 | tf_op jit(solution)/shard_map/lay_rows/pallas_call | solution.py:241
  711.3 255.3 %lay_rows.10 = bf16[1024,4096]{1,0:T(8,128)(2,1)} custom-call(bf16[128,4096]{1,0:T(8,128)(2,1)} %refs_0_.10, bf16[128,4096]{1,0:T(8,128)(2,1)} %collective-permute-done.43.refs_1_, bf16[128,4096]{1,0:T(8,128)(2,1)} %copy-done.26, bf16[128,4096]{1,0:T(8,128)(2,1)} %collective-permute-done.45.refs_3_, bf16[128,4096]{1,0:T(8,128)(2,1)} %collective-permute-done.46.refs_4_, ...), custom_call_target="tpu_custom_call" | custom-call | bytes 16777216 | tf_op jit(solution)/shard_map/lay_rows/pallas_call | solution.py:241
  966.6 255.3 %lay_rows.11 = bf16[4096,1024]{1,0:T(8,128)(2,1)} custom-call(bf16[512,1024]{1,0:T(8,128)(2,1)} %refs_0_.11, bf16[512,1024]{1,0:T(8,128)(2,1)} %collective-permute-done.52.refs_1_, bf16[512,1024]{1,0:T(8,128)(2,1)} %collective-permute-done.53.refs_2_, bf16[512,1024]{1,0:T(8,128)(2,1)} %collective-permute-done.54.refs_3_, bf16[512,1024]{1,0:T(8,128)(2,1)} %copy-done.23, ...), custom_call_target="tpu_custom_call" | custom-call | bytes 16777216 | tf_op jit(solution)/shard_map/lay_rows/pallas_call | solution.py:241
  1233.4 15.9 attention_forward.3
  1251.4 11.0 fusion.69
  1262.4 13.2 convolution_convert_fusion
  1275.7 13.8 convert_reduce_fusion
  1289.5 9.5 multiply_reduce_fusion
  1306.6 7.3 convolution_convert_fusion.1
  1313.9 19.6 %attention_backward.2 = bf16[512,3072]{1,0:T(8,128)(2,1)S(1)} custom-call(bf16[512,3072]{1,0:T(8,128)(2,1)} %copy-done.5, bf16[16,512,512]{2,1,0:T(8,128)(2,1)} %get-tuple-element.19.refs_1_, bf16[512,1024]{1,0:T(8,128)(2,1)S(1)} %convolution_convert_fusion.9.refs_2_), custom_call_target="tpu_custom_call" | custom-call | flops 4294967296 | bytes 15728640 | tf_op jit(solution)/shard_map/attention_backward/pallas_call | solution.py:188
  1333.5 8.7 multiply_reduce_fusion.1
  1347.7 12.2 add_convert_fusion.9
  1441.0 11.2 collective-permute-done.106
  1454.7 8.7 collective-permute-done.134
  1488.3 16.3 attention_backward.3
  1559.1 19.0 %collective-permute-done.135 = bf16[64,4096]{1,0:T(8,128)(2,1)S(1)} collective-permute-done((bf16[64,4096]{1,0:T(8,128)(2,1)S(1)}, bf16[64,4096]{1,0:T(8,128)(2,1)S(1)}, u32[]{:S(2)}, u32[]{:S(2)}) %collective-permute-start.135) | collective-permute-done | bytes 524320 | tf_op jit(solution)/shard_map/ppermute | solution.py:207
  1581.0 7.1 collective-permute-done.149
  1619.5 12.2 collective-permute-done.150
  1654.6 14.1 collective-permute-done.75
  1679.2 9.0 collective-permute-done.137
  1688.4 15.9 collective-permute-done.151
  1726.8 23.6 %collective-permute-done.153 = bf16[256,1024]{1,0:T(8,128)(2,1)S(1)} collective-permute-done((bf16[256,1024]{1,0:T(8,128)(2,1)S(1)}, bf16[256,1024]{1,0:T(8,128)(2,1)S(1)}, u32[]{:S(2)}, u32[]{:S(2)}) %collective-permute-start.153) | collective-permute-done | bytes 524320 | tf_op jit(solution)/shard_map/ppermute | solution.py:207
  1753.9 9.3 collective-permute-done.83
  (711 shorter events, 396.9 us)
Async XLA Ops:
  27.0 177.3 %all-to-all-start = ((bf16[4,128,1024]{2,1,0:T(8,128)(2,1)}), bf16[4,128,1024]{2,1,0:T(8,128)(2,1)S(1)}, u32[]{:S(2)}, u32[]{:S(2)}) async-start(bf16[4,128,1024]{2,1,0:T(8,128)(2,1)} %bitcast.270), calls=%async_computation | async-start | bytes 2097152 | tf_op jit(solution)/shard_map/all_to_all | solution.py:376
  48.9 34.8 %collective-permute-start.28 = (bf16[128,3072]{1,0:T(8,128)(2,1)}, bf16[128,3072]{1,0:T(8,128)(2,1)S(1)}, u32[]{:S(2)}, u32[]{:S(2)}) collective-permute-start(bf16[128,3072]{1,0:T(8,128)(2,1)} %refs_0_.8), channel_id=1, source_target_pairs={{0,8},{2,10},{4,12},{6,14},{8,0},{10,2},{12,4},{14,6},{1,9},{3,11}... | collective-permute-start | bytes 2359304 | tf_op jit(solution)/shard_map/ppermute | solution.py:207
  64.1 39.2 %collective-permute-start.44 = (bf16[128,4096]{1,0:T(8,128)(2,1)}, bf16[128,4096]{1,0:T(8,128)(2,1)S(1)}, u32[]{:S(2)}, u32[]{:S(2)}) collective-permute-start(bf16[128,4096]{1,0:T(8,128)(2,1)} %refs_0_.10), channel_id=1, source_target_pairs={{0,4},{2,6},{4,0},{6,2},{8,12},{10,14},{12,8},{14,10},{1,5},{3,7},... | collective-permute-start | bytes 3145736 | tf_op jit(solution)/shard_map/ppermute | solution.py:207
  64.9 39.4 %collective-permute-start.46 = (bf16[128,4096]{1,0:T(8,128)(2,1)}, bf16[128,4096]{1,0:T(8,128)(2,1)}, u32[]{:S(2)}, u32[]{:S(2)}) collective-permute-start(bf16[128,4096]{1,0:T(8,128)(2,1)} %refs_0_.10), channel_id=1, source_target_pairs={{0,8},{2,10},{4,12},{6,14},{8,0},{10,2},{12,4},{14,6},{1,9},{3,11}... | collective-permute-start | bytes 3145736 | tf_op jit(solution)/shard_map/ppermute | solution.py:207
  66.3 59.6 %collective-permute-start.53 = (bf16[512,1024]{1,0:T(8,128)(2,1)}, bf16[512,1024]{1,0:T(8,128)(2,1)}, u32[]{:S(2)}, u32[]{:S(2)}) collective-permute-start(bf16[512,1024]{1,0:T(8,128)(2,1)} %refs_0_.11), channel_id=1, source_target_pairs={{0,4},{2,6},{4,0},{6,2},{8,12},{10,14},{12,8},{14,10},{1,5},{3,7},... | collective-permute-start | bytes 3145736 | tf_op jit(solution)/shard_map/ppermute | solution.py:207
  81.0 122.8 %collective-permute-start.55 = (bf16[512,1024]{1,0:T(8,128)(2,1)}, bf16[512,1024]{1,0:T(8,128)(2,1)S(1)}, u32[]{:S(2)}, u32[]{:S(2)}) collective-permute-start(bf16[512,1024]{1,0:T(8,128)(2,1)} %refs_0_.11), channel_id=1, source_target_pairs={{0,8},{2,10},{4,12},{6,14},{8,0},{10,2},{12,4},{14,6},{1,9},{3,11}... | collective-permute-start | bytes 3145736 | tf_op jit(solution)/shard_map/ppermute | solution.py:207
  83.7 50.8 %collective-permute-start.12 = (bf16[64,3072]{1,0:T(8,128)(2,1)S(1)}, bf16[64,3072]{1,0:T(8,128)(2,1)S(1)}, u32[]{:S(2)}, u32[]{:S(2)}) collective-permute-start(bf16[64,3072]{1,0:T(8,128)(2,1)S(1)} %slice.330), channel_id=1, source_target_pairs={{0,8},{2,10},{4,12},{6,14},{8,0},{10,2},{12,4},{14,6},{1,9},{3,11}... | collective-permute-start | bytes 1179656 | tf_op jit(solution)/shard_map/ppermute | solution.py:207
  103.3 105.5 %collective-permute-start.14 = (bf16[64,3072]{1,0:T(8,128)(2,1)}, bf16[64,3072]{1,0:T(8,128)(2,1)}, u32[]{:S(2)}, u32[]{:S(2)}) collective-permute-start(bf16[64,3072]{1,0:T(8,128)(2,1)} %slice.331), channel_id=1, source_target_pairs={{0,4},{2,6},{4,0},{6,2},{8,12},{10,14},{12,8},{14,10},{1,5},{3,7},... | collective-permute-start | bytes 1179656 | tf_op jit(solution)/shard_map/ppermute | solution.py:207
  104.2 106.4 %collective-permute-start.9 = (bf16[128,3072]{1,0:T(8,128)(2,1)}, bf16[128,3072]{1,0:T(8,128)(2,1)}, u32[]{:S(2)}, u32[]{:S(2)}) collective-permute-start(bf16[128,3072]{1,0:T(8,128)(2,1)} %collective-permute-done.8.refs_2_), channel_id=1, source_target_pairs={{0,2},{2,0},{4,6},{6,4},{8,10},{10,8},{12,14},{14,12},{1,3},{3,1},... | collective-permute-start | bytes 2359304 | tf_op jit(solution)/shard_map/ppermute | solution.py:207
  125.9 88.3 %collective-permute-start.11 = (bf16[128,3072]{1,0:T(8,128)(2,1)}, bf16[128,3072]{1,0:T(8,128)(2,1)}, u32[]{:S(2)}, u32[]{:S(2)}) collective-permute-start(bf16[128,3072]{1,0:T(8,128)(2,1)} %collective-permute-done.10.refs_4_), channel_id=1, source_target_pairs={{0,2},{2,0},{4,6},{6,4},{8,10},{10,8},{12,14},{14,12},{1,3},{3,1},... | collective-permute-start | bytes 2359304 | tf_op jit(solution)/shard_map/ppermute | solution.py:207
  134.6 74.7 %collective-permute-start.13 = (bf16[64,3072]{1,0:T(8,128)(2,1)S(1)}, bf16[64,3072]{1,0:T(8,128)(2,1)}, u32[]{:S(2)}, u32[]{:S(2)}) collective-permute-start(bf16[64,3072]{1,0:T(8,128)(2,1)S(1)} %collective-permute-done.12.refs_6_), channel_id=1, source_target_pairs={{0,2},{2,0},{4,6},{6,4},{8,10},{10,8},{12,14},{14,12},{1,3},{3,1},... | collective-permute-start | bytes 1179656 | tf_op jit(solution)/shard_map/ppermute | solution.py:207
  203.8 211.0 %collective-permute-start.43 = (bf16[128,4096]{1,0:T(8,128)(2,1)}, bf16[128,4096]{1,0:T(8,128)(2,1)}, u32[]{:S(2)}, u32[]{:S(2)}) collective-permute-start(bf16[128,4096]{1,0:T(8,128)(2,1)} %refs_0_.10), channel_id=1, source_target_pairs={{0,2},{2,0},{4,6},{6,4},{8,10},{10,8},{12,14},{14,12},{1,3},{3,1},... | collective-permute-start | bytes 3145736 | tf_op jit(solution)/shard_map/ppermute | solution.py:207
  204.7 233.2 %all-to-all-start.3 = ((bf16[4,128,1024]{2,0,1:T(4,128)(2,1)}), bf16[4,128,1024]{2,0,1:T(4,128)(2,1)S(1)}, u32[]{:S(2)}, u32[]{:S(2)}) async-start(bf16[4,128,1024]{2,0,1:T(4,128)(2,1)} %bitcast.240), calls=%async_computation.3 | async-start | bytes 2097152 | tf_op jit(solution)/shard_map/all_to_all | solution.py:402
  208.8 205.9 %collective-permute-start.25 = (bf16[128,3072]{1,0:T(8,128)(2,1)}, bf16[128,3072]{1,0:T(8,128)(2,1)}, u32[]{:S(2)}, u32[]{:S(2)}) collective-permute-start(bf16[128,3072]{1,0:T(8,128)(2,1)} %refs_0_.8), channel_id=1, source_target_pairs={{0,2},{2,0},{4,6},{6,4},{8,10},{10,8},{12,14},{14,12},{1,3},{3,1},... | collective-permute-start | bytes 2359304 | tf_op jit(solution)/shard_map/ppermute | solution.py:207
  210.7 204.7 %collective-permute-start.30 = (bf16[64,3072]{1,0:T(8,128)(2,1)}, bf16[64,3072]{1,0:T(8,128)(2,1)S(1)}, u32[]{:S(2)}, u32[]{:S(2)}) collective-permute-start(bf16[64,3072]{1,0:T(8,128)(2,1)} %slice.336), channel_id=1, source_target_pairs={{0,8},{2,10},{4,12},{6,14},{8,0},{10,2},{12,4},{14,6},{1,9},{3,11}... | collective-permute-start | bytes 1179656 | tf_op jit(solution)/shard_map/ppermute | solution.py:207
  212.7 203.5 %collective-permute-start.32 = (bf16[64,3072]{1,0:T(8,128)(2,1)}, bf16[64,3072]{1,0:T(8,128)(2,1)}, u32[]{:S(2)}, u32[]{:S(2)}) collective-permute-start(bf16[64,3072]{1,0:T(8,128)(2,1)} %slice.337), channel_id=1, source_target_pairs={{0,4},{2,6},{4,0},{6,2},{8,12},{10,14},{12,8},{14,10},{1,5},{3,7},... | collective-permute-start | bytes 1179656 | tf_op jit(solution)/shard_map/ppermute | solution.py:207
  214.2 203.5 %collective-permute-start.48 = (bf16[64,4096]{1,0:T(8,128)(2,1)}, bf16[64,4096]{1,0:T(8,128)(2,1)}, u32[]{:S(2)}, u32[]{:S(2)}) collective-permute-start(bf16[64,4096]{1,0:T(8,128)(2,1)} %slice.342), channel_id=1, source_target_pairs={{0,8},{2,10},{4,12},{6,14},{8,0},{10,2},{12,4},{14,6},{1,9},{3,11}... | collective-permute-start | bytes 1572872 | tf_op jit(solution)/shard_map/ppermute | solution.py:207
  437.9 784.1 %all-to-all-start.1 = ((bf16[1,2,16,16,1024]{4,3,1,0,2:T(8,128)(2,1)}), bf16[1,2,16,16,1024]{4,3,1,0,2:T(8,128)(2,1)S(1)}, u32[]{:S(2)}, u32[]{:S(2)}) async-start(bf16[1,2,16,16,1024]{4,3,1,0,2:T(8,128)(2,1)} %copy.45), calls=%async_computation.1 | async-start | bytes 2097152 | tf_op jit(solution)/shard_map/all_to_all | solution.py:395
  448.2 518.4 %collective-permute-start.52 = (bf16[512,1024]{1,0:T(8,128)(2,1)}, bf16[512,1024]{1,0:T(8,128)(2,1)}, u32[]{:S(2)}, u32[]{:S(2)}) collective-permute-start(bf16[512,1024]{1,0:T(8,128)(2,1)} %refs_0_.11), channel_id=1, source_target_pairs={{0,2},{2,0},{4,6},{6,4},{8,10},{10,8},{12,14},{14,12},{1,3},{3,1},... | collective-permute-start | bytes 3145736 | tf_op jit(solution)/shard_map/ppermute | solution.py:207
  448.4 518.2 %collective-permute-start.54 = (bf16[512,1024]{1,0:T(8,128)(2,1)}, bf16[512,1024]{1,0:T(8,128)(2,1)}, u32[]{:S(2)}, u32[]{:S(2)}) collective-permute-start(bf16[512,1024]{1,0:T(8,128)(2,1)} %collective-permute-done.53.refs_2_), channel_id=1, source_target_pairs={{0,2},{2,0},{4,6},{6,4},{8,10},{10,8},{12,14},{14,12},{1,3},{3,1},... | collective-permute-start | bytes 3145736 | tf_op jit(solution)/shard_map/ppermute | solution.py:207
  449.3 517.3 %collective-permute-start.56 = (bf16[512,1024]{1,0:T(8,128)(2,1)S(1)}, bf16[512,1024]{1,0:T(8,128)(2,1)}, u32[]{:S(2)}, u32[]{:S(2)}) collective-permute-start(bf16[512,1024]{1,0:T(8,128)(2,1)S(1)} %copy-done.25), channel_id=1, source_target_pairs={{0,2},{2,0},{4,6},{6,4},{8,10},{10,8},{12,14},{14,12},{1,3},{3,1},... | collective-permute-start | bytes 3145736 | tf_op jit(solution)/shard_map/ppermute | solution.py:207
  450.1 516.5 %collective-permute-start.58 = (bf16[256,1024]{1,0:T(8,128)(2,1)}, bf16[256,1024]{1,0:T(8,128)(2,1)}, u32[]{:S(2)}, u32[]{:S(2)}) collective-permute-start(bf16[256,1024]{1,0:T(8,128)(2,1)} %collective-permute-done.57.refs_6_), channel_id=1, source_target_pairs={{0,2},{2,0},{4,6},{6,4},{8,10},{10,8},{12,14},{14,12},{1,3},{3,1},... | collective-permute-start | bytes 1572872 | tf_op jit(solution)/shard_map/ppermute | solution.py:207
  450.5 516.1 %collective-permute-start.60 = (bf16[256,1024]{1,0:T(8,128)(2,1)}, bf16[256,1024]{1,0:T(8,128)(2,1)}, u32[]{:S(2)}, u32[]{:S(2)}) collective-permute-start(bf16[256,1024]{1,0:T(8,128)(2,1)} %collective-permute-done.59.refs_8_), channel_id=1, source_target_pairs={{0,2},{2,0},{4,6},{6,4},{8,10},{10,8},{12,14},{14,12},{1,3},{3,1},... | collective-permute-start | bytes 1572872 | tf_op jit(solution)/shard_map/ppermute | solution.py:207
  1359.9 51.8 %all-to-all-start.2 = ((bf16[32,16,1024]{2,1,0:T(8,128)(2,1)}), bf16[32,16,1024]{2,1,0:T(8,128)(2,1)}, u32[]{:S(2)}, u32[]{:S(2)}) async-start(bf16[32,16,1024]{2,1,0:T(8,128)(2,1)} %bitcast.272), calls=%async_computation.2 | async-start | bytes 2097152 | tf_op jit(solution)/shard_map/all_to_all | solution.py:417
  1411.7 75.2 %all-to-all-start.4 = ((bf16[16,2,1,16,1024]{4,3,1,2,0:T(8,128)(2,1)}), bf16[16,2,1,16,1024]{4,3,1,2,0:T(8,128)(2,1)S(1)}, u32[]{:S(2)}, u32[]{:S(2)}) async-start(bf16[16,2,1,16,1024]{4,3,1,2,0:T(8,128)(2,1)} %bitcast.50), calls=%async_computation.4 | async-start | bytes 2097152 | tf_op jit(solution)/shard_map/all_to_all | solution.py:444
  1421.8 57.5 %collective-permute-start.100 = (bf16[64,3072]{1,0:T(8,128)(2,1)}, bf16[64,3072]{1,0:T(8,128)(2,1)S(1)}, u32[]{:S(2)}, u32[]{:S(2)}) collective-permute-start(bf16[64,3072]{1,0:T(8,128)(2,1)} %slice.368), channel_id=1, source_target_pairs={{0,4},{2,6},{4,0},{6,2},{8,12},{10,14},{12,8},{14,10},{1,5},{3,7},... | collective-permute-start | bytes 1179656 | tf_op jit(solution)/shard_map/ppermute | solution.py:207
  1431.8 47.5 %collective-permute-start.105 = (bf16[64,3072]{1,0:T(8,128)(2,1)S(1)}, bf16[64,3072]{1,0:T(8,128)(2,1)S(1)}, u32[]{:S(2)}, u32[]{:S(2)}) collective-permute-start(bf16[64,3072]{1,0:T(8,128)(2,1)S(1)} %slice.372), channel_id=1, source_target_pairs={{0,8},{2,10},{4,12},{6,14},{8,0},{10,2},{12,4},{14,6},{1,9},{3,11}... | collective-permute-start | bytes 1179656 | tf_op jit(solution)/shard_map/ppermute | solution.py:207
  1485.4 60.0 %collective-permute-start.108 = (bf16[64,3072]{1,0:T(8,128)(2,1)}, bf16[64,3072]{1,0:T(8,128)(2,1)}, u32[]{:S(2)}, u32[]{:S(2)}) collective-permute-start(bf16[64,3072]{1,0:T(8,128)(2,1)} %fusion.28), channel_id=1, source_target_pairs={{0,1},{1,0},{2,3},{3,2},{4,5},{5,4},{6,7},{7,6},{8,9},{9,8},{10,11... | collective-permute-start | bytes 1179656 | tf_op jit(solution)/shard_map/ppermute | solution.py:207
  1526.6 197.6 %all-to-all-start.5 = ((bf16[2,256,1024]{2,0,1:T(2,128)(2,1)}), bf16[2,256,1024]{2,0,1:T(2,128)(2,1)S(1)}, u32[]{:S(2)}, u32[]{:S(2)}) async-start(bf16[2,256,1024]{2,0,1:T(2,128)(2,1)} %copy.53), calls=%async_computation.5 | async-start | bytes 2097152 | tf_op jit(solution)/shard_map/all_to_all | solution.py:454
  1542.6 37.8 %collective-permute-start.142 = (bf16[256,1024]{1,0:T(8,128)(2,1)S(1)}, bf16[256,1024]{1,0:T(8,128)(2,1)S(1)}, u32[]{:S(2)}, u32[]{:S(2)}) collective-permute-start(bf16[256,1024]{1,0:T(8,128)(2,1)S(1)} %copy-done.53), channel_id=1, source_target_pairs={{0,4},{2,6},{4,0},{6,2},{8,12},{10,14},{12,8},{14,10},{1,5},{3,7},... | collective-permute-start | bytes 1572872 | tf_op jit(solution)/shard_map/ppermute | solution.py:207
  1637.1 34.9 %collective-permute-start.111 = (bf16[64,3072]{1,0:T(8,128)(2,1)S(1)}, bf16[64,3072]{1,0:T(8,128)(2,1)S(1)}, u32[]{:S(2)}, u32[]{:S(2)}) collective-permute-start(bf16[64,3072]{1,0:T(8,128)(2,1)S(1)} %maximum_select_fusion.7), channel_id=1, source_target_pairs={{0,1},{1,0},{2,3},{3,2},{4,5},{5,4},{6,7},{7,6},{8,9},{9,8},{10,11... | collective-permute-start | bytes 1179656 | tf_op jit(solution)/shard_map/ppermute | solution.py:207
  1715.1 37.3 %collective-permute-start.139 = (bf16[64,4096]{1,0:T(8,128)(2,1)S(1)}, bf16[64,4096]{1,0:T(8,128)(2,1)S(1)}, u32[]{:S(2)}, u32[]{:S(2)}) collective-permute-start(bf16[64,4096]{1,0:T(8,128)(2,1)S(1)} %maximum_select_fusion.4), channel_id=1, source_target_pairs={{0,1},{1,0},{2,3},{3,2},{4,5},{5,4},{6,7},{7,6},{8,9},{9,8},{10,11... | collective-permute-start | bytes 1572872 | tf_op jit(solution)/shard_map/ppermute | solution.py:207
  (235 other events, 3757.7 us)

commit v2 on v1

--- a/solution.py
+++ b/solution.py
@@ -211,26 +211,47 @@
     return (one.astype(F32) + other.astype(F32)).astype(BF)
 
 
-def lay_kernel(rows, places, *refs):
-    parts, whole_ref, done = refs[: len(places)], refs[-2], refs[-1]
+def lay_kernel(rows, places, splits, *refs):
+    count, outs = len(places), len(splits)
+    parts, whole = refs[:count], refs[count : count + outs]
+    stage = refs[count + outs : 2 * count + outs]
+    came, left = refs[-2:]
     me = lax.axis_index("tm")
-    copies = []
+    inward = [pltpu.make_async_copy(parts[i], stage[i], came.at[i]) for i in range(count)]
+    for copy in inward:
+        copy.start()
+    outward = []
     for i, (flip, start) in enumerate(places):
         at = pl.multiple_of((me ^ flip) * rows + start, 32)
-        target = whole_ref.at[pl.ds(at, parts[i].shape[0]), :]
-        copies.append(pltpu.make_async_copy(parts[i], target, done.at[i]))
-        copies[-1].start()
-    for copy in copies:
+        inward[i].wait()
+        first = 0
+        for j, columns in enumerate(splits):
+            outward.append(
+                pltpu.make_async_copy(
+                    stage[i].at[:, pl.ds(first, columns)],
+                    whole[j].at[pl.ds(at, parts[i].shape[0]), :],
+                    left.at[i, j],
+                )
+            )
+            outward[-1].start()
+            first += columns
+    for copy in outward:
         copy.wait()
 
 
-def gather_rows(block):
+def first_hops(block):
     if lax.axis_size("tm") != 8:
-        return lax.all_gather(block, "tm", axis=0, tiled=True)
+        return None
+    return hop(block, "tm", 2), hop(block, "tm", 4)
+
+
+def gather_rows(block, came, splits):
+    if came is None:
+        whole = lax.all_gather(block, "tm", axis=0, tiled=True)
+        return jnp.split(whole, [sum(splits[:i]) for i in range(1, len(splits))], axis=1)
     rows = block.shape[0]
     half = rows // 2
-    me = lax.axis_index("tm")
-    by_two, by_four = hop(block, "tm", 2), hop(block, "tm", 4)
+    by_two, by_four = came
     low_six, high_six = hop(by_two[:half], "tm", 4), hop(by_four[half:], "tm", 2)
     pieces = ((block, 0, 0), (by_two, 2, 0), (by_four, 4, 0), (low_six, 6, 0), (high_six, 6, half))
     parts, places = [], []
@@ -239,11 +260,16 @@
             parts.append(hop(piece, "tm", 1) if core else piece)
             places.append((flip + core, start))
     return pl.pallas_call(
-        lambda *refs: lay_kernel(rows, places, *refs),
+        lambda *refs: lay_kernel(rows, places, splits, *refs),
         in_specs=[pl.BlockSpec(memory_space=pl.ANY)] * len(parts),
-        out_specs=pl.BlockSpec(memory_space=pl.ANY),
-        out_shape=jax.ShapeDtypeStruct((8 * rows,) + block.shape[1:], block.dtype),
-        scratch_shapes=[pltpu.SemaphoreType.DMA((len(parts),))],
+        out_specs=[pl.BlockSpec(memory_space=pl.ANY)] * len(splits),
+        out_shape=[jax.ShapeDtypeStruct((8 * rows, n), block.dtype) for n in splits],
+        scratch_shapes=[pltpu.VMEM(part.shape, part.dtype) for part in parts]
+        + [
+            pltpu.SemaphoreType.DMA((len(parts),)),
+            pltpu.SemaphoreType.DMA((len(parts), len(splits))),
+        ],
+        compiler_params=pltpu.CompilerParams(vmem_limit_bytes=20 * 2**20),
         cost_estimate=pl.CostEstimate(
             flops=0, bytes_accessed=32 * rows * block.shape[1], transcendentals=0
         ),
@@ -251,57 +277,254 @@
     )(*parts)
 
 
-def scatter_rows(whole):
-    size = lax.axis_size("tm")
-    whole = whole.astype(BF)
-    if size != 8:
-        return lax.psum_scatter(whole, "tm", scatter_dimension=0, tiled=True)
-    rows = whole.shape[0] // 8
-    half = rows // 2
-    me = lax.axis_index("tm")
-
-    def share(flip):
-        return lax.dynamic_slice(whole, ((me ^ flip) * rows, 0), (rows, whole.shape[1]))
-
-    chip = {flip: add_low(share(flip), hop(share(flip + 1), "tm", 1)) for flip in (0, 2, 4, 6)}
-    two, two_six = hop(chip[2][:half], "tm", 2), hop(chip[6][:half], "tm", 2)
-    four, four_six = hop(chip[4][half:], "tm", 4), hop(chip[6][half:], "tm", 4)
-    top = add_low(chip[0][:half], two)
-    top_far = add_low(chip[4][:half], two_six)
-    low = add_low(chip[0][half:], four)
-    low_far = add_low(chip[2][half:], four_six)
-    return jnp.concatenate(
-        (add_low(top, hop(top_far, "tm", 4)), add_low(low, hop(low_far, "tm", 2))), axis=0
-    )
-
-
-def sum_planes(block):
-    rows = block.shape[0]
-    half, quarter = rows // 2, rows // 4
-    cols = block.shape[1]
-    mine, ours = lax.axis_index("space"), lax.axis_index("row")
-
-    def cut(array, start, length):
-        return lax.dynamic_slice(array, (start, 0), (length, cols))
-
-    one = add_low(
-        cut(block, mine * half, half), hop(cut(block, (1 - mine) * half, half), "space", 1)
-    )
-    two = add_low(
-        cut(one, ours * quarter, quarter), hop(cut(one, (1 - ours) * quarter, quarter), "row", 1)
-    )
-    other = hop(two, "row", 1)
-    both = jnp.where(
-        ours == 0, jnp.concatenate((two, other), axis=0), jnp.concatenate((other, two), axis=0)
-    )
-    far = hop(both, "space", 1)
-    return jnp.where(
-        mine == 0, jnp.concatenate((both, far), axis=0), jnp.concatenate((far, both), axis=0)
-    ).astype(F32)
-
-
-def reduce_grad(whole):
-    return sum_planes(scatter_rows(whole))
+def after(value, *others):
+    return lax.optimization_barrier((value,) + others)[0]
+
+
+UNIT = 128
+WIDE = 256
+ORDERS = ((3, 7, 1, 5), (5, 7, 1, 3), (2, 6, 0, 4), (4, 6, 0, 2))
+
+
+def product_kernel(order_ref, *refs):
+    lefts, right_ref, out_ref, turned = refs[:4], refs[4], refs[5], refs[6]
+
+    @pl.when(pl.program_id(2) == 0)
+    def _():
+        for i in range(4):
+            turned[pl.ds(i * UNIT, UNIT), :] = lefts[i][...].T
+
+    out_ref[...] = dot_nn(turned[...], right_ref[...]).astype(BF)
+
+
+def product(left, right):
+    tokens, width = left.shape
+    subs = width // (8 * UNIT)
+    half = right.shape[1] // 2
+    tiles = half // WIDE
+    flips = jnp.array(sum(ORDERS, ()), jnp.int32)
+    order = (lax.axis_index("tm").astype(jnp.int32) ^ flips) * subs
+    specs = [
+        pl.BlockSpec((tokens, UNIT), lambda g, u, j, order, i=i: (0, order[4 * g + i] + u))
+        for i in range(4)
+    ]
+    specs.append(pl.BlockSpec((tokens, WIDE), lambda g, u, j, order: (0, (g % 2) * tiles + j)))
+    return pl.pallas_call(
+        product_kernel,
+        grid_spec=pltpu.PrefetchScalarGridSpec(
+            num_scalar_prefetch=1,
+            grid=(4, subs, tiles),
+            in_specs=specs,
+            out_specs=pl.BlockSpec(
+                (None, None, 4 * UNIT, WIDE), lambda g, u, j, order: (g, u * tiles + j, 0, 0)
+            ),
+            scratch_shapes=[pltpu.VMEM((4 * UNIT, tokens), BF)],
+        ),
+        out_shape=jax.ShapeDtypeStruct((4, subs * tiles, 4 * UNIT, WIDE), BF),
+        compiler_params=pltpu.CompilerParams(vmem_limit_bytes=32 * 2**20),
+        cost_estimate=pl.CostEstimate(
+            flops=2 * tokens * width * right.shape[1],
+            bytes_accessed=2 * (4 * tokens * width + 2 * tokens * right.shape[1])
+            + 2 * width * right.shape[1],
+            transcendentals=0,
+        ),
+        name="weight_product",
+    )(order, *([left] * 4), right)
+
+
+def reduce_kernel(counts, places, *refs):
+    chunks, outs = len(counts), len(set(place[0] for place in places))
+    tiles_ref, out_refs = refs[:chunks], refs[chunks : chunks + outs]
+    (own, from_core, from_chip, from_owner, share, from_space, from_row, final) = refs[
+        chunks + outs : chunks + outs + 8
+    ]
+    (load_sem, core_sem, chip_sem, owner_sem, space_sem, row_sem, back_sem, last_sem) = refs[
+        chunks + outs + 8 :
+    ]
+    me, side, level = lax.axis_index("tm"), lax.axis_index("space"), lax.axis_index("row")
+    total = sum(counts)
+    source = [(c, k) for c in range(chunks) for k in range(counts[c])]
+    r = UNIT
+
+    def tm_at(flip):
+        return {"tm": me ^ flip}
+
+    barrier = pltpu.get_barrier_semaphore()
+    for device in (tm_at(1), tm_at(2), tm_at(4), {"space": 1 - side}, {"row": 1 - level}):
+        pl.semaphore_signal(barrier, inc=1, device_id=device, device_id_type=pl.DeviceIdType.MESH)
+    pl.semaphore_wait(barrier, 5)
+
+    def remote(src, dst, sems, device):
+        return pltpu.make_async_remote_copy(
+            src_ref=src,
+            dst_ref=dst,
+            send_sem=sems.at[0],
+            recv_sem=sems.at[1],
+            device_id=device,
+            device_id_type=pl.DeviceIdType.MESH,
+        )
+
+    sent = []
+
+    def start(copy):
+        copy.start()
+        sent.append(copy)
+        return copy
+
+    loads, cores, chips, owners, spaces, rows, backs, lasts = ({} for _ in range(8))
+
+    def stage_core(t):
+        c, k = source[t]
+        for h in range(2):
+            cores[t, h] = start(
+                remote(tiles_ref[c].at[h, k], from_core.at[t, h], core_sem.at[t, h], tm_at(1))
+            )
+            loads[t, h] = pltpu.make_async_copy(
+                tiles_ref[c].at[2 + h, k], own.at[t, h], load_sem.at[t, h]
+            )
+            loads[t, h].start()
+
+    def stage_chip(t):
+        for h in range(2):
+            loads[t, h].wait()
+            cores[t, h].wait_recv()
+            own[t, h] = add_low(own[t, h], from_core[t, h])
+            chips[t, h] = start(
+                remote(
+                    own.at[t, h, pl.ds(0, 2 * r)],
+                    from_chip.at[t, h],
+                    chip_sem.at[t, h],
+                    tm_at(4 if h else 2),
+                )
+            )
+
+    def stage_owner(t):
+        for h in range(2):
+            chips[t, h].wait_recv()
+            own[t, h, pl.ds(2 * r, 2 * r)] = add_low(
+                own[t, h, pl.ds(2 * r, 2 * r)], from_chip[t, h]
+            )
+            owners[t, h] = start(
+                remote(
+                    own.at[t, h, pl.ds(3 * r, r)],
+                    from_owner.at[t, h],
+                    owner_sem.at[t, h],
+                    tm_at(2 if h else 4),
+                )
+            )
+
+    def stage_space(t):
+        for h in range(2):
+            owners[t, h].wait_recv()
+            share[t, h] = add_low(own[t, h, pl.ds(2 * r, r)], from_owner[t, h])
+        spaces[t] = start(
+            remote(share.at[t, 1 - side], from_space.at[t], space_sem.at[t], {"space": 1 - side})
+        )
+
+    def stage_row(t):
+        spaces[t].wait_recv()
+        share[t, side] = add_low(share[t, side], from_space[t])
+        other = pl.multiple_of((1 - level) * (r // 2), r // 2)
+        rows[t] = start(
+            remote(
+                share.at[t, side, pl.ds(other, r // 2)],
+                from_row.at[t],
+                row_sem.at[t],
+                {"row": 1 - level},
+            )
+        )
+
+    def stage_back(t):
+        rows[t].wait_recv()
+        mine = pl.ds(pl.multiple_of(level * (r // 2), r // 2), r // 2)
+        final[t, side, mine] = add_low(share[t, side, mine], from_row[t])
+        backs[t] = start(
+            remote(
+                final.at[t, side, mine], final.at[t, side, mine], back_sem.at[t], {"row": 1 - level}
+            )
+        )
+
+    def stage_last(t):
+        backs[t].wait_recv()
+        lasts[t] = start(
+            remote(final.at[t, side], final.at[t, side], last_sem.at[t], {"space": 1 - side})
+        )
+
+    def stage_out(t):
+        lasts[t].wait_recv()
+        out, row, column, half = places[t]
+        for h in range(2):
+            out_refs[out][pl.ds(row, r), pl.ds(column + h * half, WIDE)] = final[t, h].astype(F32)
+
+    stages = (
+        stage_core,
+        stage_chip,
+        stage_owner,
+        stage_space,
+        stage_row,
+        stage_back,
+        stage_last,
+        stage_out,
+    )
+    for step in range(total + len(stages) - 1):
+        for number, stage in enumerate(stages):
+            if 0 <= step - number < total:
+                stage(step - number)
+    for copy in sent:
+        copy.wait_send()
+
+
+def reduce_products(pairs, number):
+    if lax.axis_size("tm") != 8:
+        result = []
+        for left, right in pairs:
+            whole = weight_grad(left, right).astype(BF)
+            block = lax.psum_scatter(whole, "tm", scatter_dimension=0, tiled=True)
+            result.append(lax.psum(block, ("row", "space")).astype(F32))
+        return result
+    tiles = [product(left, right) for left, right in pairs]
+    counts = [block.shape[1] for block in tiles]
+    places, shapes = [], []
+    for which, (left, right) in enumerate(pairs):
+        half = right.shape[1] // 2
+        shapes.append((left.shape[1] // 8, right.shape[1]))
+        for sub in range(left.shape[1] // (8 * UNIT)):
+            for j in range(half // WIDE):
+                places.append((which, sub * UNIT, j * WIDE, half))
+    n = sum(counts)
+    vmem = pltpu.VMEM
+    dma = pltpu.SemaphoreType.DMA
+    return pl.pallas_call(
+        lambda *refs: reduce_kernel(counts, places, *refs),
+        in_specs=[pl.BlockSpec(memory_space=pl.ANY)] * len(tiles),
+        out_specs=[pl.BlockSpec(memory_space=pltpu.VMEM)] * len(pairs),
+        out_shape=[jax.ShapeDtypeStruct(shape, F32) for shape in shapes],
+        scratch_shapes=[
+            vmem((n, 2, 4 * UNIT, WIDE), BF),
+            vmem((n, 2, 4 * UNIT, WIDE), BF),
+            vmem((n, 2, 2 * UNIT, WIDE), BF),
+            vmem((n, 2, UNIT, WIDE), BF),
+            vmem((n, 2, UNIT, WIDE), BF),
+            vmem((n, UNIT, WIDE), BF),
+            vmem((n, UNIT // 2, WIDE), BF),
+            vmem((n, 2, UNIT, WIDE), BF),
+            dma((n, 2)),
+            dma((n, 2, 2)),
+            dma((n, 2, 2)),
+            dma((n, 2, 2)),
+            dma((n, 2)),
+            dma((n, 2)),
+            dma((n, 2)),
+            dma((n, 2)),
+        ],
+        compiler_params=pltpu.CompilerParams(
+            vmem_limit_bytes=56 * 2**20, collective_id=number, has_side_effects=True
+        ),
+        cost_estimate=pl.CostEstimate(
+            flops=1024, bytes_accessed=n * 8 * UNIT * WIDE, transcendentals=0
+        ),
+        name="reduce_tiles",
+    )(*tiles)
 
 
 def gather_small(flat):
@@ -378,12 +601,21 @@
     one_hot = (actions[:, None] == jnp.arange(ACTIONS)[None, :]).astype(BF)
     embedded = forward_dot(one_hot, table_full)
 
-    space_in_w = gather_rows(space_qkv)
-    space_out_w = gather_rows(space_out)
-    time_in_w = gather_rows(time_qkv)
-    time_out_w = gather_rows(time_out)
-    ffn_in_w = gather_rows(ffn_in)
-    ffn_out_w = gather_rows(ffn_out)
+    blocks_in = [
+        jnp.concatenate((space_qkv, space_out), axis=1),
+        jnp.concatenate((time_qkv, time_out), axis=1),
+        ffn_in,
+        ffn_out,
+    ]
+    came = []
+    for i, block in enumerate(blocks_in):
+        if i and came[-1] is not None:
+            blocks_in[i] = after(block, *came[-1])
+        came.append(first_hops(blocks_in[i]))
+    space_in_w, space_out_w = gather_rows(blocks_in[0], came[0], (3 * MODEL, MODEL))
+    time_in_w, time_out_w = gather_rows(blocks_in[1], came[1], (3 * MODEL, MODEL))
+    (ffn_in_w,) = gather_rows(blocks_in[2], came[2], (ffn_in.shape[1],))
+    (ffn_out_w,) = gather_rows(blocks_in[3], came[3], (MODEL,))
 
     hidden_zero = (inputs.astype(F32) + embedded[:, None, :]).reshape(rows_dev, MODEL)
     normed_one = layer_norm(hidden_zero, gains[0], shifts[0]).astype(BF)
@@ -412,26 +644,26 @@
     normed_three = layer_norm(hidden_two, gains[2], shifts[2]).astype(BF)
     pre_act = forward_dot(normed_three, ffn_in_w) + bias_in
     activated, gelu_pull = jax.vjp(jax.nn.gelu, pre_act)
-    act_low = activated.astype(BF)
+    act_low, slope = lax.optimization_barrier(
+        (activated.astype(BF), gelu_pull(jnp.ones_like(pre_act))[0].astype(BF))
+    )
     block_out = (hidden_two + forward_dot(act_low, ffn_out_w) + bias_out).astype(BF)
     block_output = lax.all_to_all(
         block_out.reshape(all_frames, cut, MODEL), "tm", 0, 1, tiled=True
     )[None]
 
-    ffn_out_grad = reduce_grad(weight_grad(act_low, grad_out_low))
     bias_out_grad = jnp.sum(grad_out, axis=0)
-    grad_pre = gelu_pull(back_dot(grad_out_low, ffn_out_w))[0]
-    grad_pre_low = grad_pre.astype(BF)
-    ffn_in_grad = reduce_grad(weight_grad(normed_three, grad_pre_low))
+    grad_pre_low = (back_dot(grad_out_low, ffn_out_w) * slope.astype(F32)).astype(BF)
     bias_in_grad = jnp.sum(grad_pre_low.astype(F32), axis=0)
     norm_pull = jax.vjp(layer_norm, hidden_two, gains[2], shifts[2])[1]
     grad_hidden, gain_three, shift_three = norm_pull(back_dot(grad_pre_low, ffn_in_w))
     grad_two = grad_out + grad_hidden
     time_branch = grad_two.astype(BF)
-    time_out_grad = reduce_grad(weight_grad(time_mixed, time_branch))
+    ffn_out_grad, ffn_in_grad = reduce_products(
+        ((act_low, grad_out_low), (normed_three, grad_pre_low)), 1
+    )
     time_grad_mixed = back_dot(time_branch, time_out_w).astype(BF)
     grad_packed_two = attention_back(packed_two, time_probs, time_grad_mixed, rows_dev)
-    time_qkv_grad = reduce_grad(weight_grad(normed_two, grad_packed_two))
     norm_pull = jax.vjp(layer_norm, hidden_one, gains[1], shifts[1])[1]
     grad_hidden, gain_two, shift_two = norm_pull(back_dot(grad_packed_two, time_in_w))
     grad_one_low = (grad_two + grad_hidden).astype(BF)
@@ -442,12 +674,19 @@
         .reshape(halves * tm, own_frames, cut, MODEL)
     )
     space_branch = lax.all_to_all(sent, ("space", "tm"), 0, 1).reshape(rows_dev, MODEL)
-    space_out_grad = reduce_grad(weight_grad(space_mixed, space_branch))
     space_grad_mixed = back_dot(space_branch, space_out_w).astype(BF)
     grad_packed_one = attention_back(packed_one, space_probs, space_grad_mixed, grid_all)
-    space_qkv_grad = reduce_grad(weight_grad(normed_one, grad_packed_one))
     norm_pull = jax.vjp(layer_norm, hidden_zero, gains[0], shifts[0])[1]
     grad_hidden, gain_one, shift_one = norm_pull(back_dot(grad_packed_one, space_in_w))
+    time_qkv_grad, time_out_grad, space_out_grad, space_qkv_grad = reduce_products(
+        (
+            (normed_two, grad_packed_two),
+            (time_mixed, time_branch),
+            (space_mixed, space_branch),
+            (normed_one, grad_packed_one),
+        ),
+        2,
+    )
     grad_zero = space_branch.astype(F32) + grad_hidden
     frame_grad = jnp.sum(grad_zero.reshape(own_frames, grid_all, MODEL), axis=1)
     action_grad = jnp.dot(one_hot.astype(F32).T, frame_grad, precision=lax.Precision.HIGHEST)

time: 1770 us -> 663 us (0.37)
  Pallas kernels: 1090 us -> 337 us
  waiting for transfers between devices: 290 us -> 88.8 us
  starting transfers between devices: 156 us -> 69.9 us
  matrix products: 116 us -> 59.5 us
  other arithmetic: 47.9 us -> 25.5 us
    pallas_call x6 -> x12, Pallas kernels: 1020 us -> 275 us  [the longest x2 197 us: reduce_products(): pl.pallas_call(lambda *refs: reduce_kernel(counts, places, *refs), in_spe...]
    ppermute x154 -> x52, waiting for transfers between devices: 290 us -> 88.8 us  [hop(): return lax.ppermute(block, axis, [(i, i ^ flip) for i in range(size)])]
    ppermute x154 -> x52, starting transfers between devices: 130 us -> 43.1 us  [hop(): return lax.ppermute(block, axis, [(i, i ^ flip) for i in range(size)])]
    dot_general x6 -> x0, matrix products: 36.8 us -> none  [weight_grad(): lax.dot_general(left_rows, right_rows, (((0,), (0,)), ((), ())), preferre...]
    unnamed x215 -> x148, local copies, waits for them, and re-layouts: 8.1 us -> 41.7 us
    convert_element_type x42 -> x1, other arithmetic: 29.3 us -> 0.41 us  [body(): normed_three = layer_norm(hidden_two, gains[2], shifts[2]).astype(BF)]
  transfers between devices with their start and end apart: 160 -> 58, of which waited for: 46 -> 10; matrix products, arithmetic and copies ran while one was open for 7% -> 13% of each run, Pallas kernels for 60% -> 48%
where the time goes in v2:
time: 663 us; the launch traced here: 655 us
  Pallas kernels  337 us (51%)
  waiting for transfers between devices  88.8 us (13%)
  local copies, waits for them, and re-layouts  71.6 us (11%)
  starting transfers between devices  69.9 us (11%)
  matrix products  59.5 us (9%)
  other arithmetic  25.5 us (4%)
    pallas_call x2, Pallas kernels, reduce_products(): pl.pallas_call(lambda *refs: reduce_kernel(counts, places, *refs), in_spe...  197 us
    ppermute x52, waiting for transfers between devices, hop(): return lax.ppermute(block, axis, [(i, i ^ flip) for i in range(size)])  88.8 us
    pallas_call x6, Pallas kernels, product(): pl.pallas_call(product_kernel, grid_spec=pltpu.PrefetchScalarGridSpec(num...  66.5 us
    ppermute x52, starting transfers between devices, hop(): return lax.ppermute(block, axis, [(i, i ^ flip) for i in range(size)])  43.1 us
    unnamed x148, local copies, waits for them, and re-layouts  41.7 us
    pallas_call x2, Pallas kernels, attention_back(): pl.pallas_call(lambda *refs: attn_bwd_kernel(span // TILE, *refs), grid=(...  35.9 us
    dot_general x7, matrix products, forward_dot(): return jnp.dot(values, weight, preferred_element_type=F32)  33.8 us
    pallas_call x2, Pallas kernels, attention(): pl.pallas_call(lambda *refs: attn_fwd_kernel(span // TILE, masked, *refs)...  26.4 us
  transfers between devices with their start and end apart: 58, of which 10 were waited for; matrix products, arithmetic and copies ran while one was open for 13% of the time, Pallas kernels for 48%

profile of v2, /device:TPU:0, one launch (start us, length us, event | category | flops | bytes accessed | tf_op | source)
XLA Modules:
  0.0 654.8 jit_solution(16097976386819778127)
XLA Ops:
  3.0 3.4 collective-permute-start.6
  8.8 4.5 all-to-all-start
  26.8 22.1 %collective-permute-done.10.refs_4_ = bf16[128,4096]{1,0:T(8,128)(2,1)} collective-permute-done((bf16[128,4096]{1,0:T(8,128)(2,1)S(1)}, bf16[128,4096]{1,0:T(8,128)(2,1)}, u32[]{:S(2)}, u32[]{:S(2)}) %collective-permute-start.10) | collective-permute-done | bytes 1048608 | tf_op jit(solution)/shard_map/ppermute | solution.py:207
  56.0 4.2 all-to-all-start.3
  65.2 6.8 %collective-permute-done.12.refs_6_ = bf16[64,4096]{1,0:T(8,128)(2,1)} collective-permute-done((bf16[64,4096]{1,0:T(8,128)(2,1)}, bf16[64,4096]{1,0:T(8,128)(2,1)}, u32[]{:S(2)}, u32[]{:S(2)}) %collective-permute-start.12) | collective-permute-done | bytes 524320 | tf_op jit(solution)/shard_map/ppermute | solution.py:207
  87.1 3.7 convolution_convert_fusion.1.refs_0_
  90.7 10.4 %attention_forward.2 = (bf16[512,1024]{1,0:T(8,128)(2,1)S(1)}, bf16[16,512,256]{2,1,0:T(8,128)(2,1)}) custom-call(bf16[512,3072]{1,0:T(8,128)(2,1)S(1)} %convolution_convert_fusion.1.refs_0_), custom_call_target="tpu_custom_call" | custom-call | flops 1073741824 | bytes 8388608 | tf_op jit(solution)/shard_map/attention_forward/pallas_call | solution.py:166
  103.5 4.7 all-to-all-start.1
  113.6 43.5 %collective-permute-done.23.refs_8_ = bf16[64,4096]{1,0:T(8,128)(2,1)} collective-permute-done((bf16[64,4096]{1,0:T(8,128)(2,1)S(1)}, bf16[64,4096]{1,0:T(8,128)(2,1)}, u32[]{:S(2)}, u32[]{:S(2)}) %collective-permute-start.23) | collective-permute-done | bytes 524320 | tf_op jit(solution)/shard_map/ppermute | solution.py:207
  189.2 6.5 convolution_convert_fusion.refs_0_
  195.8 16.0 %attention_forward.3 = (bf16[512,1024]{1,0:T(8,128)(2,1)S(1)}, bf16[16,512,512]{2,1,0:T(8,128)(2,1)}) custom-call(bf16[512,3072]{1,0:T(8,128)(2,1)S(1)} %convolution_convert_fusion.refs_0_, s32[512,1]{1,0:T(8,128)S(1)} %add.283.refs_1_, s32[1,512]{1,0:T(1,128)S(1)} %add.258.refs_2_), custom_call_target="tpu_custom_call" | custom-call | flops 2147483648 | bytes 12582912 | tf_op jit(solution)/shard_map/attention_forward/pallas_call | solution.py:166
  221.7 8.6 %collective-permute-done.41.refs_8_ = bf16[256,1024]{1,0:T(8,128)(2,1)S(1)} collective-permute-done((bf16[256,1024]{1,0:T(8,128)(2,1)S(1)}, bf16[256,1024]{1,0:T(8,128)(2,1)S(1)}, u32[]{:S(2)}, u32[]{:S(2)}) %collective-permute-start.41) | collective-permute-done | bytes 524320 | tf_op jit(solution)/shard_map/ppermute | solution.py:207
  230.9 11.9 %fusion.6 = (bf16[512,4096]{1,0:T(8,128)(2,1)}, bf16[512,4096]{1,0:T(8,128)(2,1)S(1)}) fusion(f32[4096]{0:T(1024)S(1)} %copy-done.63, bf16[512,1024]{1,0:T(8,128)(2,1)S(1)} %add_convert_fusion.2.refs_0_.refs_1_.refs_2_.refs_3_, bf16[1024,4096]{1,0:T(8,128)(2,1)S(1)} %lay_rows.6), kind=kOutput, calls=%fused_computation.8 | convolution fusion | flops 4339007488 | bytes 17842176 | tf_op jit(solution)/shard_map/dot_general | solution.py:33
  242.9 19.0 %weight_product.10.refs_0_ = bf16[4,8,512,256]{3,2,1,0:T(8,128)(2,1)S(1)} custom-call(s32[16]{0:T(128)S(1)} %get-tuple-element.84.order_ref, bf16[512,4096]{1,0:T(8,128)(2,1)S(1)} %get-tuple-element.40.refs_0_.refs_1_.refs_2_.refs_3_, bf16[512,4096]{1,0:T(8,128)(2,1)S(1)} %get-tuple-element.40.refs_0_.refs_1_.refs_2_.refs_3_, ...), custom_call_target="tpu_custom_call" | custom-call | flops 4294967296 | bytes 27262976 | tf_op jit(solution)/shard_map/weight_product/pallas_call | solution.py:312
  261.9 3.3 copy-done.5
  267.5 8.6 %convert_reduce_fusion = (f32[4096]{0:T(1024)S(1)}, bf16[512,4096]{1,0:T(8,128)(2,1)S(1)}) fusion(bf16[512,4096]{1,0:T(8,128)(2,1)} %get-tuple-element.42, bf16[4096,1024]{1,0:T(8,128)(2,1)S(1)} %lay_rows.7, bf16[512,1024]{1,0:T(8,128)(2,1)S(1)} %bitcast.222), kind=kOutput, calls=%fused_computation.11 | convolution fusion | flops 4305448960 | bytes 17842176 | tf_op jit(solution)/shard_map/dot_general | solution.py:43
  276.1 6.3 multiply_reduce_fusion
  288.4 19.9 %attention_backward.2.refs_4_ = bf16[512,3072]{1,0:T(8,128)(2,1)S(1)} custom-call(bf16[512,3072]{1,0:T(8,128)(2,1)} %copy-done.40, bf16[16,512,512]{2,1,0:T(8,128)(2,1)} %get-tuple-element.43.refs_1_, bf16[512,1024]{1,0:T(8,128)(2,1)S(1)} %convolution_convert_fusion.3.refs_2_), custom_call_target="tpu_custom_call" | custom-call | flops 4294967296 | bytes 15728640 | tf_op jit(solution)/shard_map/attention_backward/pallas_call | solution.py:188
  308.4 3.9 multiply_reduce_fusion.1
  315.5 4.4 all-to-all-start.4
  322.1 14.5 %weight_product.11.refs_1_ = bf16[4,8,512,256]{3,2,1,0:T(8,128)(2,1)S(1)} custom-call(s32[16]{0:T(128)S(1)} %get-tuple-element.85.order_ref, bf16[512,1024]{1,0:T(8,128)(2,1)S(1)} %add_convert_fusion.2.refs_0_.refs_1_.refs_2_.refs_3_, bf16[512,1024]{1,0:T(8,128)(2,1)S(1)} %add_convert_fusion.2.refs_0_.refs_1_.refs_2_.refs_3_, ...), custom_call_target="tpu_custom_call" | custom-call | flops 4294967296 | bytes 20971520 | tf_op jit(solution)/shard_map/weight_product/pallas_call | solution.py:312
  339.9 11.3 %weight_product.6.refs_0_ = bf16[4,6,512,256]{3,2,1,0:T(8,128)(2,1)S(1)} custom-call(s32[16]{0:T(128)S(1)} %get-tuple-element.85.order_ref, bf16[512,1024]{1,0:T(8,128)(2,1)S(1)} %add_convert_fusion.3.refs_0_.refs_1_.refs_2_.refs_3_, bf16[512,1024]{1,0:T(8,128)(2,1)S(1)} %add_convert_fusion.3.refs_0_.refs_1_.refs_2_.refs_3_, ...), custom_call_target="tpu_custom_call" | custom-call | flops 3221225472 | bytes 16777216 | tf_op jit(solution)/shard_map/weight_product/pallas_call | solution.py:312
  353.9 8.9 %add_convert_fusion.1 = bf16[512,1024]{1,0:T(8,128)(2,1)} fusion(f32[512,1024]{1,0:T(8,128)S(1)} %copy-done.47, bf16[512,4096]{1,0:T(8,128)(2,1)S(1)} %copy-done.3, bf16[4096,1024]{1,0:T(8,128)(2,1)} %copy-done.17, f32[1024]{0:T(1024)S(1)} %bitcast.272), kind=kOutput, calls=%fused_computation.40 | convolution fusion | flops 4296540160 | bytes 15732736 | tf_op jit(solution)/shard_map/dot_general | solution.py:33
  363.8 4.6 all-to-all-start.2
  371.1 16.1 %attention_backward.3.refs_4_ = bf16[512,3072]{1,0:T(8,128)(2,1)S(1)} custom-call(bf16[512,3072]{1,0:T(8,128)(2,1)} %copy-done.25, bf16[16,512,256]{2,1,0:T(8,128)(2,1)} %get-tuple-element.44.refs_1_, bf16[512,1024]{1,0:T(8,128)(2,1)S(1)} %convolution_convert_fusion.2.refs_2_), custom_call_target="tpu_custom_call" | custom-call | flops 2147483648 | bytes 11534336 | tf_op jit(solution)/shard_map/attention_backward/pallas_call | solution.py:188
  387.2 3.9 multiply_reduce_fusion.2
  399.2 5.2 weight_product.7.refs_1_
  405.8 97.7 %reduce_tiles.3 = (f32[512,1024]{1,0:T(8,128)}, f32[128,4096]{1,0:T(8,128)}) custom-call(bf16[4,8,512,256]{3,2,1,0:T(8,128)(2,1)} %copy-done.5, bf16[4,8,512,256]{3,2,1,0:T(8,128)(2,1)} %copy-done.4), custom_call_target="tpu_custom_call" | custom-call | flops 1024 | bytes 4194304 | tf_op jit(solution)/shard_map/reduce_tiles/pallas_call | solution.py:497
  514.4 4.4 all-to-all-start.5
  520.1 11.6 %weight_product.9.refs_3_ = bf16[4,6,512,256]{3,2,1,0:T(8,128)(2,1)S(1)} custom-call(s32[16]{0:T(128)S(1)} %get-tuple-element.85.order_ref, bf16[512,1024]{1,0:T(8,128)(2,1)S(1)} %copy-done.7, bf16[512,1024]{1,0:T(8,128)(2,1)S(1)} %copy-done.7, bf16[512,1024]{1,0:T(8,128)(2,1)S(1)} %copy-done.7, bf16[512,1024]{1,0:T(8,128)(2,1)S(1)} %copy-done.7, ...), custom_call_target="tpu_custom_call" | custom-call | flops 3221225472 | bytes 16777216 | tf_op jit(solution)/shard_map/weight_product/pallas_call | solution.py:312
  531.8 5.0 weight_product.8.refs_2_
  540.4 99.5 %reduce_tiles.2 = (f32[128,3072]{1,0:T(8,128)}, f32[128,1024]{1,0:T(8,128)}, f32[128,1024]{1,0:T(8,128)}, f32[128,3072]{1,0:T(8,128)}) custom-call(bf16[4,6,512,256]{3,2,1,0:T(8,128)(2,1)} %copy-done.10, bf16[4,2,512,256]{3,2,1,0:T(8,128)(2,1)} %copy-done.18, bf16[4,2,512,256]{3,2,1,0:T(8,128)(2,1)} %copy-done.19, bf16[4,6,512,256]{3,2,1,0:T(8,128)(2,1)} %copy-done.11), custom_call_target="tpu_custom_call" | custom-call | flops 1024 | bytes 4194304 | tf_op jit(solution)/shard_map/reduce_tiles/pallas_call | solution.py:497
  (355 shorter events, 157.9 us)
Async XLA Ops:
  3.0 23.6 %collective-permute-start.6 = (bf16[19,128]{1,0:T(8,128)(2,1)S(1)}, bf16[19,128]{1,0:T(8,128)(2,1)S(1)}, u32[]{:S(2)}, u32[]{:S(2)}) collective-permute-start(bf16[19,128]{1,0:T(8,128)(2,1)S(1)} %concatenate.30), channel_id=1, source_target_pairs={{0,14},{2,12},{4,10},{6,8},{8,6},{10,4},{12,2},{14,0},{1,15},{3,13... | collective-permute-start | bytes 14600 | tf_op jit(solution)/shard_map/ppermute | solution.py:207
  8.8 47.2 %all-to-all-start = ((bf16[4,128,1024]{2,1,0:T(8,128)(2,1)}), bf16[4,128,1024]{2,1,0:T(8,128)(2,1)}, u32[]{:S(2)}, u32[]{:S(2)}) async-start(bf16[4,128,1024]{2,1,0:T(8,128)(2,1)} %bitcast.239), calls=%async_computation | async-start | bytes 2097152 | tf_op jit(solution)/shard_map/all_to_all | solution.py:599
  23.4 25.5 %collective-permute-start.10 = (bf16[128,4096]{1,0:T(8,128)(2,1)S(1)}, bf16[128,4096]{1,0:T(8,128)(2,1)}, u32[]{:S(2)}, u32[]{:S(2)}) collective-permute-start(bf16[128,4096]{1,0:T(8,128)(2,1)S(1)} %constant_dynamic-update-slice_fusion.8.refs_0_), channel_id=1, source_target_pairs={{0,8},{2,10},{4,12},{6,14},{8,0},{10,2},{12,4},{14,6},{1,9},{3,11}... | collective-permute-start | bytes 3145736 | tf_op jit(solution)/shard_map/ppermute | solution.py:207
  25.0 27.1 %collective-permute-start.8 = (bf16[128,4096]{1,0:T(8,128)(2,1)S(1)}, bf16[128,4096]{1,0:T(8,128)(2,1)}, u32[]{:S(2)}, u32[]{:S(2)}) collective-permute-start(bf16[128,4096]{1,0:T(8,128)(2,1)S(1)} %constant_dynamic-update-slice_fusion.8.refs_0_), channel_id=1, source_target_pairs={{0,4},{2,6},{4,0},{6,2},{8,12},{10,14},{12,8},{14,10},{1,5},{3,7},... | collective-permute-start | bytes 3145736 | tf_op jit(solution)/shard_map/ppermute | solution.py:207
  26.5 47.7 %collective-permute-start.7 = (bf16[128,4096]{1,0:T(8,128)(2,1)S(1)}, bf16[128,4096]{1,0:T(8,128)(2,1)S(1)}, u32[]{:S(2)}, u32[]{:S(2)}) collective-permute-start(bf16[128,4096]{1,0:T(8,128)(2,1)S(1)} %constant_dynamic-update-slice_fusion.8.refs_0_), channel_id=1, source_target_pairs={{0,2},{2,0},{4,6},{6,4},{8,10},{10,8},{12,14},{14,12},{1,3},{3,1},... | collective-permute-start | bytes 3145736 | tf_op jit(solution)/shard_map/ppermute | solution.py:207
  55.5 24.6 %collective-permute-start.11 = (bf16[128,4096]{1,0:T(8,128)(2,1)}, bf16[128,4096]{1,0:T(8,128)(2,1)}, u32[]{:S(2)}, u32[]{:S(2)}) collective-permute-start(bf16[128,4096]{1,0:T(8,128)(2,1)} %collective-permute-done.10.refs_4_), channel_id=1, source_target_pairs={{0,2},{2,0},{4,6},{6,4},{8,10},{10,8},{12,14},{14,12},{1,3},{3,1},... | collective-permute-start | bytes 3145736 | tf_op jit(solution)/shard_map/ppermute | solution.py:207
  55.5 24.6 %collective-permute-start.9 = (bf16[128,4096]{1,0:T(8,128)(2,1)}, bf16[128,4096]{1,0:T(8,128)(2,1)}, u32[]{:S(2)}, u32[]{:S(2)}) collective-permute-start(bf16[128,4096]{1,0:T(8,128)(2,1)} %collective-permute-done.8.refs_2_), channel_id=1, source_target_pairs={{0,2},{2,0},{4,6},{6,4},{8,10},{10,8},{12,14},{14,12},{1,3},{3,1},... | collective-permute-start | bytes 3145736 | tf_op jit(solution)/shard_map/ppermute | solution.py:207
  56.0 47.5 %all-to-all-start.3 = ((bf16[4,128,1024]{2,0,1:T(4,128)(2,1)}), bf16[4,128,1024]{2,0,1:T(4,128)(2,1)}, u32[]{:S(2)}, u32[]{:S(2)}) async-start(bf16[4,128,1024]{2,0,1:T(4,128)(2,1)} %bitcast.232), calls=%async_computation.3 | async-start | bytes 2097152 | tf_op jit(solution)/shard_map/all_to_all | solution.py:634
  75.4 32.8 %collective-permute-start.19 = (bf16[128,4096]{1,0:T(8,128)(2,1)S(1)}, bf16[128,4096]{1,0:T(8,128)(2,1)S(1)}, u32[]{:S(2)}, u32[]{:S(2)}) collective-permute-start(bf16[128,4096]{1,0:T(8,128)(2,1)S(1)} %pad_maximum_fusion.refs_0_), channel_id=1, source_target_pairs={{0,8},{2,10},{4,12},{6,14},{8,0},{10,2},{12,4},{14,6},{1,9},{3,11}... | collective-permute-start | bytes 3145736 | tf_op jit(solution)/shard_map/ppermute | solution.py:207
  77.0 31.2 %collective-permute-start.17 = (bf16[128,4096]{1,0:T(8,128)(2,1)S(1)}, bf16[128,4096]{1,0:T(8,128)(2,1)}, u32[]{:S(2)}, u32[]{:S(2)}) collective-permute-start(bf16[128,4096]{1,0:T(8,128)(2,1)S(1)} %pad_maximum_fusion.refs_0_), channel_id=1, source_target_pairs={{0,4},{2,6},{4,0},{6,2},{8,12},{10,14},{12,8},{14,10},{1,5},{3,7},... | collective-permute-start | bytes 3145736 | tf_op jit(solution)/shard_map/ppermute | solution.py:207
  103.5 73.8 %all-to-all-start.1 = ((bf16[1,2,16,16,1024]{4,3,1,0,2:T(8,128)(2,1)}), bf16[1,2,16,16,1024]{4,3,1,0,2:T(8,128)(2,1)}, u32[]{:S(2)}, u32[]{:S(2)}) async-start(bf16[1,2,16,16,1024]{4,3,1,0,2:T(8,128)(2,1)} %copy.79), calls=%async_computation.1 | async-start | bytes 2097152 | tf_op jit(solution)/shard_map/all_to_all | solution.py:627
  108.2 49.8 %collective-permute-start.28 = (bf16[128,4096]{1,0:T(8,128)(2,1)}, bf16[128,4096]{1,0:T(8,128)(2,1)}, u32[]{:S(2)}, u32[]{:S(2)}) collective-permute-start(bf16[128,4096]{1,0:T(8,128)(2,1)} %refs_0_), channel_id=1, source_target_pairs={{0,8},{2,10},{4,12},{6,14},{8,0},{10,2},{12,4},{14,6},{1,9},{3,11}... | collective-permute-start | bytes 3145736 | tf_op jit(solution)/shard_map/ppermute | solution.py:207
  110.2 47.9 %collective-permute-start.26 = (bf16[128,4096]{1,0:T(8,128)(2,1)}, bf16[128,4096]{1,0:T(8,128)(2,1)}, u32[]{:S(2)}, u32[]{:S(2)}) collective-permute-start(bf16[128,4096]{1,0:T(8,128)(2,1)} %refs_0_), channel_id=1, source_target_pairs={{0,4},{2,6},{4,0},{6,2},{8,12},{10,14},{12,8},{14,10},{1,5},{3,7},... | collective-permute-start | bytes 3145736 | tf_op jit(solution)/shard_map/ppermute | solution.py:207
  111.7 45.4 %collective-permute-start.23 = (bf16[64,4096]{1,0:T(8,128)(2,1)S(1)}, bf16[64,4096]{1,0:T(8,128)(2,1)}, u32[]{:S(2)}, u32[]{:S(2)}) collective-permute-start(bf16[64,4096]{1,0:T(8,128)(2,1)S(1)} %slice.127), channel_id=1, source_target_pairs={{0,4},{2,6},{4,0},{6,2},{8,12},{10,14},{12,8},{14,10},{1,5},{3,7},... | collective-permute-start | bytes 1572872 | tf_op jit(solution)/shard_map/ppermute | solution.py:207
  113.4 43.7 %collective-permute-start.21 = (bf16[64,4096]{1,0:T(8,128)(2,1)S(1)}, bf16[64,4096]{1,0:T(8,128)(2,1)}, u32[]{:S(2)}, u32[]{:S(2)}) collective-permute-start(bf16[64,4096]{1,0:T(8,128)(2,1)S(1)} %slice.126), channel_id=1, source_target_pairs={{0,8},{2,10},{4,12},{6,14},{8,0},{10,2},{12,4},{14,6},{1,9},{3,11}... | collective-permute-start | bytes 1572872 | tf_op jit(solution)/shard_map/ppermute | solution.py:207
  113.6 52.5 %collective-permute-start.16 = (bf16[128,4096]{1,0:T(8,128)(2,1)S(1)}, bf16[128,4096]{1,0:T(8,128)(2,1)}, u32[]{:S(2)}, u32[]{:S(2)}) collective-permute-start(bf16[128,4096]{1,0:T(8,128)(2,1)S(1)} %pad_maximum_fusion.refs_0_), channel_id=1, source_target_pairs={{0,2},{2,0},{4,6},{6,4},{8,10},{10,8},{12,14},{14,12},{1,3},{3,1},... | collective-permute-start | bytes 3145736 | tf_op jit(solution)/shard_map/ppermute | solution.py:207
  166.2 49.8 %collective-permute-start.25 = (bf16[128,4096]{1,0:T(8,128)(2,1)}, bf16[128,4096]{1,0:T(8,128)(2,1)}, u32[]{:S(2)}, u32[]{:S(2)}) collective-permute-start(bf16[128,4096]{1,0:T(8,128)(2,1)} %refs_0_), channel_id=1, source_target_pairs={{0,2},{2,0},{4,6},{6,4},{8,10},{10,8},{12,14},{14,12},{1,3},{3,1},... | collective-permute-start | bytes 3145736 | tf_op jit(solution)/shard_map/ppermute | solution.py:207
  166.3 46.1 %collective-permute-start.37 = (bf16[512,1024]{1,0:T(8,128)(2,1)}, bf16[512,1024]{1,0:T(8,128)(2,1)S(1)}, u32[]{:S(2)}, u32[]{:S(2)}) collective-permute-start(bf16[512,1024]{1,0:T(8,128)(2,1)} %refs_0_.1), channel_id=1, source_target_pairs={{0,8},{2,10},{4,12},{6,14},{8,0},{10,2},{12,4},{14,6},{1,9},{3,11}... | collective-permute-start | bytes 3145736 | tf_op jit(solution)/shard_map/ppermute | solution.py:207
  167.1 47.2 %collective-permute-start.35 = (bf16[512,1024]{1,0:T(8,128)(2,1)}, bf16[512,1024]{1,0:T(8,128)(2,1)}, u32[]{:S(2)}, u32[]{:S(2)}) collective-permute-start(bf16[512,1024]{1,0:T(8,128)(2,1)} %refs_0_.1), channel_id=1, source_target_pairs={{0,4},{2,6},{4,0},{6,2},{8,12},{10,14},{12,8},{14,10},{1,5},{3,7},... | collective-permute-start | bytes 3145736 | tf_op jit(solution)/shard_map/ppermute | solution.py:207
  167.9 43.9 %collective-permute-start.32 = (bf16[64,4096]{1,0:T(8,128)(2,1)}, bf16[64,4096]{1,0:T(8,128)(2,1)}, u32[]{:S(2)}, u32[]{:S(2)}) collective-permute-start(bf16[64,4096]{1,0:T(8,128)(2,1)} %slice.131), channel_id=1, source_target_pairs={{0,4},{2,6},{4,0},{6,2},{8,12},{10,14},{12,8},{14,10},{1,5},{3,7},... | collective-permute-start | bytes 1572872 | tf_op jit(solution)/shard_map/ppermute | solution.py:207
  169.1 42.8 %collective-permute-start.30 = (bf16[64,4096]{1,0:T(8,128)(2,1)}, bf16[64,4096]{1,0:T(8,128)(2,1)}, u32[]{:S(2)}, u32[]{:S(2)}) collective-permute-start(bf16[64,4096]{1,0:T(8,128)(2,1)} %slice.130), channel_id=1, source_target_pairs={{0,8},{2,10},{4,12},{6,14},{8,0},{10,2},{12,4},{14,6},{1,9},{3,11}... | collective-permute-start | bytes 1572872 | tf_op jit(solution)/shard_map/ppermute | solution.py:207
  218.2 47.0 %collective-permute-start.34 = (bf16[512,1024]{1,0:T(8,128)(2,1)}, bf16[512,1024]{1,0:T(8,128)(2,1)S(1)}, u32[]{:S(2)}, u32[]{:S(2)}) collective-permute-start(bf16[512,1024]{1,0:T(8,128)(2,1)} %refs_0_.1), channel_id=1, source_target_pairs={{0,2},{2,0},{4,6},{6,4},{8,10},{10,8},{12,14},{14,12},{1,3},{3,1},... | collective-permute-start | bytes 3145736 | tf_op jit(solution)/shard_map/ppermute | solution.py:207
  218.3 46.9 %collective-permute-start.38 = (bf16[512,1024]{1,0:T(8,128)(2,1)S(1)}, bf16[512,1024]{1,0:T(8,128)(2,1)S(1)}, u32[]{:S(2)}, u32[]{:S(2)}) collective-permute-start(bf16[512,1024]{1,0:T(8,128)(2,1)S(1)} %copy-done.29), channel_id=1, source_target_pairs={{0,2},{2,0},{4,6},{6,4},{8,10},{10,8},{12,14},{14,12},{1,3},{3,1},... | collective-permute-start | bytes 3145736 | tf_op jit(solution)/shard_map/ppermute | solution.py:207
  218.8 46.4 %collective-permute-start.36 = (bf16[512,1024]{1,0:T(8,128)(2,1)}, bf16[512,1024]{1,0:T(8,128)(2,1)S(1)}, u32[]{:S(2)}, u32[]{:S(2)}) collective-permute-start(bf16[512,1024]{1,0:T(8,128)(2,1)} %collective-permute-done.35.refs_2_), channel_id=1, source_target_pairs={{0,2},{2,0},{4,6},{6,4},{8,10},{10,8},{12,14},{14,12},{1,3},{3,1},... | collective-permute-start | bytes 3145736 | tf_op jit(solution)/shard_map/ppermute | solution.py:207
  230.2 35.0 %collective-permute-start.42 = (bf16[256,1024]{1,0:T(8,128)(2,1)S(1)}, bf16[256,1024]{1,0:T(8,128)(2,1)S(1)}, u32[]{:S(2)}, u32[]{:S(2)}) collective-permute-start(bf16[256,1024]{1,0:T(8,128)(2,1)S(1)} %collective-permute-done.41.refs_8_), channel_id=1, source_target_pairs={{0,2},{2,0},{4,6},{6,4},{8,10},{10,8},{12,14},{14,12},{1,3},{3,1},... | collective-permute-start | bytes 1572872 | tf_op jit(solution)/shard_map/ppermute | solution.py:207
  230.9 34.3 %collective-permute-start.40 = (bf16[256,1024]{1,0:T(8,128)(2,1)S(1)}, bf16[256,1024]{1,0:T(8,128)(2,1)S(1)}, u32[]{:S(2)}, u32[]{:S(2)}) collective-permute-start(bf16[256,1024]{1,0:T(8,128)(2,1)S(1)} %collective-permute-done.39.refs_6_), channel_id=1, source_target_pairs={{0,2},{2,0},{4,6},{6,4},{8,10},{10,8},{12,14},{14,12},{1,3},{3,1},... | collective-permute-start | bytes 1572872 | tf_op jit(solution)/shard_map/ppermute | solution.py:207
  315.5 47.3 %all-to-all-start.4 = ((bf16[16,2,1,16,1024]{4,3,1,2,0:T(8,128)(2,1)}), bf16[16,2,1,16,1024]{4,3,1,2,0:T(8,128)(2,1)S(1)}, u32[]{:S(2)}, u32[]{:S(2)}) async-start(bf16[16,2,1,16,1024]{4,3,1,2,0:T(8,128)(2,1)} %bitcast.234), calls=%async_computation.4 | async-start | bytes 2097152 | tf_op jit(solution)/shard_map/all_to_all | solution.py:676
  363.8 150.6 %all-to-all-start.2 = ((bf16[32,16,1024]{2,1,0:T(8,128)(2,1)}), bf16[32,16,1024]{2,1,0:T(8,128)(2,1)}, u32[]{:S(2)}, u32[]{:S(2)}) async-start(bf16[32,16,1024]{2,1,0:T(8,128)(2,1)} %bitcast.42), calls=%async_computation.2 | async-start | bytes 2097152 | tf_op jit(solution)/shard_map/all_to_all | solution.py:651
  393.6 112.0 %collective-permute-start.49 = (f32[19,128]{1,0:T(8,128)S(1)}, f32[19,128]{1,0:T(8,128)S(1)}, u32[]{:S(2)}, u32[]{:S(2)}) collective-permute-start(f32[19,128]{1,0:T(8,128)S(1)} %fusion.19), channel_id=1, source_target_pairs={{0,14},{2,12},{4,10},{6,8},{8,6},{10,4},{12,2},{14,0},{1,15},{3,13... | collective-permute-start | bytes 29192 | tf_op jit(solution)/shard_map/ppermute | solution.py:207
  396.4 110.7 %collective-permute-start.43 = (f32[19,128]{1,0:T(8,128)S(1)}, f32[19,128]{1,0:T(8,128)S(1)}, u32[]{:S(2)}, u32[]{:S(2)}) collective-permute-start(f32[19,128]{1,0:T(8,128)S(1)} %get-tuple-element.68), channel_id=1, source_target_pairs={{0,2},{2,0},{4,6},{6,4},{8,10},{10,8},{12,14},{14,12},{1,3},{3,1},... | collective-permute-start | bytes 29192 | tf_op jit(solution)/shard_map/ppermute | solution.py:207
  514.4 127.8 %all-to-all-start.5 = ((bf16[2,256,1024]{2,0,1:T(2,128)(2,1)}), bf16[2,256,1024]{2,0,1:T(2,128)(2,1)}, u32[]{:S(2)}, u32[]{:S(2)}) async-start(bf16[2,256,1024]{2,0,1:T(2,128)(2,1)} %copy.94), calls=%async_computation.5 | async-start | bytes 2097152 | tf_op jit(solution)/shard_map/all_to_all | solution.py:693
  531.7 108.3 %collective-permute-start.51 = (f32[19,128]{1,0:T(8,128)S(1)}, f32[19,128]{1,0:T(8,128)S(1)}, u32[]{:S(2)}, u32[]{:S(2)}) collective-permute-start(f32[19,128]{1,0:T(8,128)S(1)} %add.281), channel_id=1, source_target_pairs={{0,16},{16,0},{1,17},{17,1},{2,18},{18,2},{3,19},{19,3},{4,20},{20... | collective-permute-start | bytes 29192 | tf_op jit(solution)/shard_map/ppermute | solution.py:207
  (96 other events, 1137.9 us)

commit v3 on v2

v3 whole, which is shorter than its diff:
```python
import math

import jax
import jax.numpy as jnp
from jax import lax
from jax.experimental import pallas as pl
from jax.experimental.pallas import tpu as pltpu
from jax.sharding import PartitionSpec as P

MODEL = 1024
HEADS = 16
HEAD_DIM = 64
ACTIONS = 8
TILE = 256
PAIR = 2 * HEAD_DIM
PAIRS = HEADS // 2
SCALE = 1.0 / math.sqrt(HEAD_DIM)

EPSILON = 1e-05
NEG_FILL = -1e30
BF = jnp.bfloat16
F32 = jnp.float32


def layer_norm(values, gain_row, shift_row):
    row_mean = jnp.mean(values, axis=-1, keepdims=True)
    centred = values - row_mean
    spread = jnp.mean(centred * centred, axis=-1, keepdims=True)
    return centred * lax.rsqrt(spread + EPSILON) * gain_row + shift_row


def forward_dot(values, weight):
    return jnp.dot(values, weight, preferred_element_type=F32)


def weight_grad(left_rows, right_rows):
    return lax.dot_general(
        left_rows, right_rows, (((0,), (0,)), ((), ())), preferred_element_type=F32
    )


def back_dot(grad_rows, weight):
    return lax.dot_general(
        grad_rows, weight, (((1,), (1,)), ((), ())), preferred_element_type=F32
    )


def dot_nt(a, b):
    return lax.dot_general(a, b, (((1,), (1,)), ((), ())), preferred_element_type=F32)


def dot_nn(a, b):
    return lax.dot_general(a, b, (((1,), (0,)), ((), ())), preferred_element_type=F32)


def dot_tn(a, b):
    return lax.dot_general(a, b, (((0,), (0,)), ((), ())), preferred_element_type=F32)


def of_head(half, values):
    lane = lax.broadcasted_iota(jnp.int32, values.shape, 1)
    keep = (lane < HEAD_DIM) if half == 0 else (lane >= HEAD_DIM)
    return jnp.where(keep, values, jnp.zeros_like(values))


def join_heads(first, second):
    lane = lax.broadcasted_iota(jnp.int32, first.shape, 1)
    return jnp.where(lane < HEAD_DIM, first, second)


def pair_cols(pair, part):
    if isinstance(pair, int):
        return pl.ds(part * MODEL + pair * PAIR, PAIR)
    return pl.ds(pl.multiple_of(part * MODEL + pair * PAIR, PAIR), PAIR)


def attn_fwd_kernel(tiles, masked, packed_ref, *refs):
    if masked:
        col_ref, row_ref, mixed_ref, probs_ref = refs
    else:
        mixed_ref, probs_ref = refs

    def one_pair(pair, carry):
        for t in range(tiles):
            mine = pl.ds(t * TILE, TILE)
            width = (t + 1) * TILE
            seen = pl.ds(0, width)
            query = packed_ref[mine, pair_cols(pair, 0)] * jnp.asarray(SCALE, BF)
            key = packed_ref[seen, pair_cols(pair, 1)]
            value = packed_ref[seen, pair_cols(pair, 2)]
            if masked:
                same = col_ref[mine, :] == row_ref[:, seen]
                order = lax.broadcasted_iota(
                    jnp.int32, (TILE, width), 0
                ) + t * TILE >= lax.broadcasted_iota(jnp.int32, (TILE, width), 1)
                allowed = same & order
            outs = []
            for half in range(2):
                scores = dot_nt(of_head(half, query), key)
                if masked:
                    scores = jnp.where(allowed, scores, NEG_FILL)
                top = jnp.max(scores, axis=1, keepdims=True)
                raised = jnp.exp(scores - top)
                total = jnp.sum(raised, axis=1, keepdims=True)
                probs = (raised * (1.0 / total)).astype(BF)
                probs_ref[2 * pair + half, mine, seen] = probs
                outs.append(dot_nn(probs, value))
            mixed_ref[mine, pair_cols(pair, 0)] = join_heads(*outs).astype(BF)
        return carry

    lax.fori_loop(0, PAIRS, one_pair, 0, unroll=2)


def attn_bwd_pair(base, tiles, pair, packed_ref, probs_ref, grad_ref, out_ref, accs=None):
    for t in reversed(range(tiles)):
        mine = pl.ds(base + t * TILE, TILE)
        seen = pl.ds(base, (t + 1) * TILE)
        query = packed_ref[mine, pair_cols(pair, 0)] * jnp.asarray(SCALE, BF)
        key = packed_ref[seen, pair_cols(pair, 1)]
        value = packed_ref[seen, pair_cols(pair, 2)]
        grad = grad_ref[mine, pair_cols(pair, 0)]
        dqs, dks, dvs = [], [], []
        for half in range(2):
            probs_low = probs_ref[2 * pair + half, mine, pl.ds(0, (t + 1) * TILE)]
            probs = probs_low.astype(F32)
            dprobs = dot_nt(of_head(half, grad), value)
            delta = jnp.sum(dprobs * probs, axis=1, keepdims=True)
            dscores = (probs * (dprobs - delta)).astype(BF)
            dqs.append(dot_nn(dscores, key))
            dks.append(dot_tn(dscores, query))
            dvs.append(dot_tn(probs_low, grad))
        out_ref[mine, pair_cols(pair, 0)] = (join_heads(*dqs) * SCALE).astype(BF)
        dkey, dvalue = join_heads(*dks), join_heads(*dvs)
        if tiles == 1:
            out_ref[seen, pair_cols(pair, 1)] = dkey.astype(BF)
            out_ref[seen, pair_cols(pair, 2)] = dvalue.astype(BF)
        elif t == tiles - 1:
            accs[0][...] = dkey
            accs[1][...] = dvalue
        else:
            accs[0][pl.ds(0, (t + 1) * TILE), :] += dkey
            accs[1][pl.ds(0, (t + 1) * TILE), :] += dvalue
    if tiles > 1:
        out_ref[:, pair_cols(pair, 1)] = accs[0][...].astype(BF)
        out_ref[:, pair_cols(pair, 2)] = accs[1][...].astype(BF)


def attn_bwd_kernel(tiles, packed_ref, probs_ref, grad_ref, out_ref, key_acc, value_acc):
    def one_pair(pair, carry):
        attn_bwd_pair(
            0, tiles, pair, packed_ref, probs_ref, grad_ref, out_ref, (key_acc, value_acc)
        )
        return carry

    lax.fori_loop(0, PAIRS, one_pair, 0, unroll=2)


def blocks(rows, span):
    return {
        "packed": pl.BlockSpec((span, 3 * MODEL), lambda t: (t, 0)),
        "mixed": pl.BlockSpec((span, MODEL), lambda t: (t, 0)),
        "probs": pl.BlockSpec((HEADS, span, span), lambda t: (0, t, 0)),
        "col": pl.BlockSpec((span, 1), lambda t: (t, 0)),
        "row": pl.BlockSpec((1, span), lambda t: (0, t)),
    }


def attention(packed, span, groups=None):
    rows = packed.shape[0]
    at = blocks(rows, span)
    masked = groups is not None
    extra = (groups[:, None], groups[None, :]) if masked else ()
    specs = [at["packed"]] + ([at["col"], at["row"]] if masked else [])
    return pl.pallas_call(
        lambda *refs: attn_fwd_kernel(span // TILE, masked, *refs),
        grid=(rows // span,),
        in_specs=specs,
        out_specs=[at["mixed"], at["probs"]],
        out_shape=[
            jax.ShapeDtypeStruct((rows, MODEL), BF),
            jax.ShapeDtypeStruct((HEADS, rows, span), BF),
        ],
        compiler_params=pltpu.CompilerParams(vmem_limit_bytes=48 * 2**20),
        cost_estimate=pl.CostEstimate(
            flops=8 * HEADS * rows * span * HEAD_DIM,
            bytes_accessed=rows * (8 * MODEL + 2 * HEADS * span),
            transcendentals=HEADS * rows * span,
        ),
        name="attention_forward",
    )(packed, *extra)


def attention_back(packed, probs, grad, span):
    rows = packed.shape[0]
    at = blocks(rows, span)
    return pl.pallas_call(
        lambda *refs: attn_bwd_kernel(span // TILE, *refs),
        grid=(rows // span,),
        in_specs=[at["packed"], at["probs"], at["mixed"]],
        out_specs=at["packed"],
        out_shape=jax.ShapeDtypeStruct((rows, 3 * MODEL), BF),
        scratch_shapes=[pltpu.VMEM((span, PAIR), F32), pltpu.VMEM((span, PAIR), F32)],
        compiler_params=pltpu.CompilerParams(vmem_limit_bytes=48 * 2**20),
        cost_estimate=pl.CostEstimate(
            flops=16 * HEADS * rows * span * HEAD_DIM,
            bytes_accessed=rows * (14 * MODEL + 2 * HEADS * span),
            transcendentals=0,
        ),
        name="attention_backward",
    )(packed, probs, grad)


def hop(block, axis, flip):
    size = lax.axis_size(axis)
    return lax.ppermute(block, axis, [(i, i ^ flip) for i in range(size)])


def add_low(one, other):
    return (one.astype(F32) + other.astype(F32)).astype(BF)


def lay_kernel(rows, places, splits, *refs):
    count, outs = len(places), len(splits)
    parts, whole = refs[:count], refs[count : count + outs]
    stage = refs[count + outs : 2 * count + outs]
    came, left = refs[-2:]
    me = lax.axis_index("tm")
    inward = [pltpu.make_async_copy(parts[i], stage[i], came.at[i]) for i in range(count)]
    for copy in inward:
        copy.start()
    outward = []
    for i, (flip, start) in enumerate(places):
        at = pl.multiple_of((me ^ flip) * rows + start, 32)
        inward[i].wait()
        first = 0
        for j, columns in enumerate(splits):
            outward.append(
                pltpu.make_async_copy(
                    stage[i].at[:, pl.ds(first, columns)],
                    whole[j].at[pl.ds(at, parts[i].shape[0]), :],
                    left.at[i, j],
                )
            )
            outward[-1].start()
            first += columns
    for copy in outward:
        copy.wait()


def first_hops(block):
    if lax.axis_size("tm") != 8:
        return None
    return hop(block, "tm", 2), hop(block, "tm", 4)


def second_hops(came):
    if came is None:
        return None
    half = came[0].shape[0] // 2
    return hop(came[0][:half], "tm", 4), hop(came[1][half:], "tm", 2)


def gather_rows(block, came, passed, splits):
    if came is None:
        whole = lax.all_gather(block, "tm", axis=0, tiled=True)
        return jnp.split(whole, [sum(splits[:i]) for i in range(1, len(splits))], axis=1)
    rows = block.shape[0]
    half = rows // 2
    by_two, by_four = came
    low_six, high_six = passed
    pieces = ((block, 0, 0), (by_two, 2, 0), (by_four, 4, 0), (low_six, 6, 0), (high_six, 6, half))
    parts, places = [], []
    for piece, flip, start in pieces:
        for core in range(2):
            parts.append(hop(piece, "tm", 1) if core else piece)
            places.append((flip + core, start))
    return pl.pallas_call(
        lambda *refs: lay_kernel(rows, places, splits, *refs),
        in_specs=[pl.BlockSpec(memory_space=pl.ANY)] * len(parts),
        out_specs=[pl.BlockSpec(memory_space=pl.ANY)] * len(splits),
        out_shape=[jax.ShapeDtypeStruct((8 * rows, n), block.dtype) for n in splits],
        scratch_shapes=[pltpu.VMEM(part.shape, part.dtype) for part in parts]
        + [
            pltpu.SemaphoreType.DMA((len(parts),)),
            pltpu.SemaphoreType.DMA((len(parts), len(splits))),
        ],
        compiler_params=pltpu.CompilerParams(vmem_limit_bytes=20 * 2**20),
        cost_estimate=pl.CostEstimate(
            flops=0, bytes_accessed=32 * rows * block.shape[1], transcendentals=0
        ),
        name="lay_rows",
    )(*parts)


def after(value, *others):
    return lax.optimization_barrier((value,) + others)[0]


def first_kernel(*refs):
    blocks, small_ref, tokens_ref = refs[:2], refs[2], refs[3]
    wholes, smalls_ref, frames_ref = refs[4:6], refs[6], refs[7]
    local, small_sem, frame_sem, near, far, core = refs[8:]
    me, side = lax.axis_index("tm"), lax.axis_index("space")
    rows = blocks[0].shape[0]
    half = rows // 2
    half_grid, own_frames = tokens_ref.shape[1], tokens_ref.shape[0] // 2

    barrier = pltpu.get_barrier_semaphore()
    for flip in range(1, 8):
        pl.semaphore_signal(
            barrier, inc=1, device_id={"tm": me ^ flip}, device_id_type=pl.DeviceIdType.MESH
        )
    pl.semaphore_signal(
        barrier, inc=1, device_id={"space": 1 - side}, device_id_type=pl.DeviceIdType.MESH
    )
    pl.semaphore_wait(barrier, 8)

    sent = []

    def send(src, dst, sems, device):
        copy = pltpu.make_async_remote_copy(
            src_ref=src,
            dst_ref=dst,
            send_sem=sems.at[0],
            recv_sem=sems.at[1],
            device_id=device,
            device_id_type=pl.DeviceIdType.MESH,
        )
        copy.start()
        sent.append(copy)
        return copy

    def place(w, flip, start, length):
        at = pl.multiple_of((me ^ flip) * rows + start, half)
        return wholes[w].at[pl.ds(at, length), :]

    arrived = {}
    for w in range(2):
        for number, (flip, start) in enumerate(((2, 0), (4, half), (2, half), (4, 0))):
            arrived[w, flip, start] = send(
                blocks[w].at[pl.ds(start, half), :],
                place(w, 0, start, half),
                near.at[w, number],
                {"tm": me ^ flip},
            )
    small_copies = [
        send(small_ref, smalls_ref.at[me], small_sem.at[flip], {"tm": me ^ flip})
        for flip in range(1, 8)
    ]
    columns = pl.ds(pl.multiple_of(side * half_grid, half_grid), half_grid)
    frame_copy = send(
        tokens_ref.at[pl.ds((1 - side) * own_frames, own_frames)],
        frames_ref.at[:, columns, :],
        frame_sem,
        {"space": 1 - side},
    )
    core_copies = [
        send(blocks[w], place(w, 0, 0, rows), core.at[w, 0], {"tm": me ^ 1}) for w in range(2)
    ]
    own = [
        pltpu.make_async_copy(small_ref, smalls_ref.at[me], local.at[0]),
        pltpu.make_async_copy(
            tokens_ref.at[pl.ds(side * own_frames, own_frames)],
            frames_ref.at[:, columns, :],
            local.at[1],
        ),
    ] + [pltpu.make_async_copy(blocks[w], place(w, 0, 0, rows), local.at[2 + w]) for w in range(2)]
    for copy in own:
        copy.start()
    for w in range(2):
        for number, (flip, start) in enumerate(((2, 0), (4, half), (2, half), (4, 0))):
            arrived[w, flip, start].wait_recv()
            block = place(w, flip, start, half)
            if number < 2:
                arrived[w, 6, start] = send(
                    block, block, far.at[w, number], {"tm": me ^ (6 - flip)}
                )
            core_copies.append(send(block, block, core.at[w, 1 + number], {"tm": me ^ 1}))
    for w in range(2):
        for number, start in enumerate((0, half)):
            arrived[w, 6, start].wait_recv()
            block = place(w, 6, start, half)
            core_copies.append(send(block, block, core.at[w, 5 + number], {"tm": me ^ 1}))
    for copy in small_copies + [frame_copy] + core_copies:
        copy.wait_recv()
    for copy in own:
        copy.wait()
    for copy in sent:
        copy.wait_send()


def first_gather(weights, small, tokens):
    if lax.axis_size("tm") != 8:
        return (
            *[lax.all_gather(weight, "tm", axis=0, tiled=True) for weight in weights],
            lax.all_gather(small, "tm", axis=0),
            lax.all_to_all(tokens, "space", 0, 1, tiled=True),
        )
    used = small.shape[0]
    small = jnp.pad(small, ((0, -used % 16), (0, 0)))
    frames, half_grid, model = tokens.shape
    dma = pltpu.SemaphoreType.DMA
    first, second, smalls, whole_frames = pl.pallas_call(
        first_kernel,
        in_specs=[pl.BlockSpec(memory_space=pltpu.VMEM)] * 4,
        out_specs=[pl.BlockSpec(memory_space=pl.ANY)] * 4,
        out_shape=[
            jax.ShapeDtypeStruct((8 * weight.shape[0], weight.shape[1]), weight.dtype)
            for weight in weights
        ]
        + [
            jax.ShapeDtypeStruct((8,) + small.shape, small.dtype),
            jax.ShapeDtypeStruct((frames // 2, 2 * half_grid, model), tokens.dtype),
        ],
        scratch_shapes=[
            dma((4,)),
            dma((8, 2)),
            dma((2,)),
            dma((2, 4, 2)),
            dma((2, 2, 2)),
            dma((2, 7, 2)),
        ],
        compiler_params=pltpu.CompilerParams(
            vmem_limit_bytes=16 * 2**20, collective_id=3, has_side_effects=True
        ),
        cost_estimate=pl.CostEstimate(flops=0, bytes_accessed=2**24, transcendentals=0),
        name="first_gather",
    )(*weights, small, tokens)
    return first, second, smalls[:, :used], whole_frames


UNIT = 128
WIDE = 256
SLOTS = 6
FINALS = 10
DELAYS = (0, 1, 3, 5, 7, 9, 11, 13)
ORDERS = ((3, 7, 1, 5), (5, 7, 1, 3), (2, 6, 0, 4), (4, 6, 0, 2))


def reduce_kernel(chunks, places, with_small, units, *refs):
    refs = list(refs)

    def take(count):
        taken = refs[:count]
        del refs[:count]
        return taken

    lefts, rights = take(chunks), take(chunks)
    small_ref = take(1)[0] if with_small else None
    packed_ref, probs_ref, grad_ref = take(3) if units else (None,) * 3
    out_refs = take(chunks)
    small_out = take(1)[0] if with_small else None
    packed_out = take(1)[0] if units else None
    (far, own, from_core, from_chip, from_owner, share, from_space, from_row, final) = take(9)
    (core_sem, chip_sem, owner_sem, space_sem, row_sem, back_sem, last_sem) = take(7)
    turned = take(len(refs))
    me, side, level = lax.axis_index("tm"), lax.axis_index("space"), lax.axis_index("row")
    total = len(places)
    r = UNIT

    def tm_at(flip):
        return {"tm": me ^ flip}

    barrier = pltpu.get_barrier_semaphore()
    for device in (tm_at(1), tm_at(2), tm_at(4), {"space": 1 - side}, {"row": 1 - level}):
        pl.semaphore_signal(barrier, inc=1, device_id=device, device_id_type=pl.DeviceIdType.MESH)
    pl.semaphore_wait(barrier, 5)

    def start(src, dst, sems, device):
        copy = pltpu.make_async_remote_copy(
            src_ref=src,
            dst_ref=dst,
            send_sem=sems.at[0],
            recv_sem=sems.at[1],
            device_id=device,
            device_id_type=pl.DeviceIdType.MESH,
        )
        copy.start()
        return copy

    cores, chips, owners, spaces, rows, backs, lasts = ({} for _ in range(7))

    def buffer_of(which):
        wide = lefts[which].shape[1] > 8 * UNIT
        return turned[1] if wide else turned[0]

    def part(t, h, order):
        which, row, column, half = places[t]
        if which == chunks:
            return jnp.concatenate([small_ref[me ^ flip] for flip in order], axis=0)
        rows_each = lefts[which].shape[1] // 8
        picked = [
            buffer_of(which)[pl.ds(pl.multiple_of((me ^ flip) * rows_each + row, r), r), :]
            for flip in order
        ]
        return dot_nn(
            jnp.concatenate(picked, axis=0), rights[which][:, pl.ds(column + h * half, WIDE)]
        )

    mine = {}

    def stage_core(t):
        which, slot = places[t][0], t % SLOTS
        if which < chunks and (t == 0 or places[t - 1][0] != which):
            buffer_of(which)[...] = lefts[which][...].T
        for h in range(2):
            if t >= SLOTS:
                cores[t - SLOTS, h].wait_send()
            far[slot, h] = part(t, h, ORDERS[h]).astype(BF)
            cores[t, h] = start(
                far.at[slot, h], from_core.at[slot, h], core_sem.at[slot, h], tm_at(1)
            )
        for h in range(2):
            if t >= SLOTS:
                chips[t - SLOTS, h].wait_send()
                owners[t - SLOTS, h].wait_send()
            own[slot, h] = part(t, h, ORDERS[2 + h]).astype(BF)

    def stage_chip(t):
        slot = t % SLOTS
        for h in range(2):
            cores[t, h].wait_recv()
            own[slot, h] = add_low(own[slot, h], from_core[slot, h])
            chips[t, h] = start(
                own.at[slot, h, pl.ds(0, 2 * r)],
                from_chip.at[slot, h],
                chip_sem.at[slot, h],
                tm_at(4 if h else 2),
            )

    def stage_owner(t):
        slot = t % SLOTS
        for h in range(2):
            chips[t, h].wait_recv()
            own[slot, h, pl.ds(2 * r, 2 * r)] = add_low(
                own[slot, h, pl.ds(2 * r, 2 * r)], from_chip[slot, h]
            )
            owners[t, h] = start(
                own.at[slot, h, pl.ds(3 * r, r)],
                from_owner.at[slot, h],
                owner_sem.at[slot, h],
                tm_at(2 if h else 4),
            )

    def stage_space(t):
        slot = t % SLOTS
        if t >= SLOTS:
            spaces[t - SLOTS].wait_send()
            rows[t - SLOTS].wait_send()
        for h in range(2):
            owners[t, h].wait_recv()
            share[slot, h] = add_low(own[slot, h, pl.ds(2 * r, r)], from_owner[slot, h])
        spaces[t] = start(
            share.at[slot, 1 - side], from_space.at[slot], space_sem.at[slot], {"space": 1 - side}
        )

    def stage_row(t):
        slot = t % SLOTS
        spaces[t].wait_recv()
        share[slot, side] = add_low(share[slot, side], from_space[slot])
        other = pl.multiple_of((1 - level) * (r // 2), r // 2)
        rows[t] = start(
            share.at[slot, side, pl.ds(other, r // 2)],
            from_row.at[slot],
            row_sem.at[slot],
            {"row": 1 - level},
        )

    def stage_back(t):
        slot = t % SLOTS
        rows[t].wait_recv()
        here = pl.ds(pl.multiple_of(level * (r // 2), r // 2), r // 2)
        last = t % FINALS
        final[last, side, here] = add_low(share[slot, side, here], from_row[slot])
        place = final.at[last, side, here]
        backs[t] = start(place, place, back_sem.at[last], {"row": 1 - level})

    def stage_last(t):
        slot = t % FINALS
        backs[t].wait_recv()
        place = final.at[slot, side]
        lasts[t] = start(place, place, last_sem.at[slot], {"space": 1 - side})

    def stage_out(t):
        slot = t % FINALS
        lasts[t].wait_recv()
        out, row, column, half = places[t]
        if out == chunks:
            small_out[...] = final[slot, 0].astype(F32)
        else:
            for h in range(2):
                out_refs[out][pl.ds(row, r), pl.ds(column + h * half, WIDE)] = final[
                    slot, h
                ].astype(F32)
        backs[t].wait_send()
        lasts[t].wait_send()

    stages = (
        stage_core,
        stage_chip,
        stage_owner,
        stage_space,
        stage_row,
        stage_back,
        stage_last,
        stage_out,
    )
    for step in range(total + DELAYS[-1]):
        for delay, stage in zip(DELAYS, stages):
            if 0 <= step - delay < total:
                stage(step - delay)
        if 0 < step <= units:
            frame, pair = divmod(step - 1, PAIRS)
            attn_bwd_pair(frame * TILE, 1, pair, packed_ref, probs_ref, grad_ref, packed_out)
    for t in range(max(0, total - SLOTS), total):
        for h in range(2):
            cores[t, h].wait_send()
            chips[t, h].wait_send()
            owners[t, h].wait_send()
        spaces[t].wait_send()
        rows[t].wait_send()


def reduce_products(pairs, number, small=None, attend=None):
    if lax.axis_size("tm") != 8:
        result = []
        for left, right in pairs:
            whole = weight_grad(left, right).astype(BF)
            block = lax.psum_scatter(whole, "tm", scatter_dimension=0, tiled=True)
            result.append(lax.psum(block, ("row", "space")).astype(F32))
        if small is not None:
            block = lax.psum_scatter(small, "tm", scatter_dimension=0, tiled=True)[0]
            result.append(lax.psum(block, ("row", "space")))
        if attend is not None:
            result.append(attention_back(*attend, TILE))
        return result
    places, shapes = [], []
    for which, (left, right) in enumerate(pairs):
        half = right.shape[1] // 2
        shapes.append((left.shape[1] // 8, right.shape[1]))
        for sub in range(left.shape[1] // (8 * UNIT)):
            for j in range(half // WIDE):
                places.append((which, sub * UNIT, j * WIDE, half))
    operands = [left for left, _ in pairs] + [right for _, right in pairs]
    outs = [jax.ShapeDtypeStruct(shape, F32) for shape in shapes]
    if small is not None:
        places.append((len(pairs), 0, 0, 0))
        padding = ((0, 0), (0, UNIT - small.shape[1]), (0, WIDE - small.shape[2]))
        operands.append(jnp.pad(small, padding))
        outs.append(jax.ShapeDtypeStruct((UNIT, WIDE), F32))
    units = 0
    if attend is not None:
        units = attend[0].shape[0] // TILE * PAIRS
        operands += list(attend)
        outs.append(jax.ShapeDtypeStruct(attend[0].shape, BF))
    widths = sorted({left.shape[1] for left, _ in pairs})
    tokens = pairs[0][0].shape[0]
    vmem = pltpu.VMEM
    dma = pltpu.SemaphoreType.DMA
    result = pl.pallas_call(
        lambda *refs: reduce_kernel(len(pairs), places, small is not None, units, *refs),
        in_specs=[pl.BlockSpec(memory_space=pltpu.VMEM)] * len(operands),
        out_specs=[pl.BlockSpec(memory_space=pltpu.VMEM)] * len(outs),
        out_shape=outs,
        scratch_shapes=[
            vmem((SLOTS, 2, 4 * UNIT, WIDE), BF),
            vmem((SLOTS, 2, 4 * UNIT, WIDE), BF),
            vmem((SLOTS, 2, 4 * UNIT, WIDE), BF),
            vmem((SLOTS, 2, 2 * UNIT, WIDE), BF),
            vmem((SLOTS, 2, UNIT, WIDE), BF),
            vmem((SLOTS, 2, UNIT, WIDE), BF),
            vmem((SLOTS, UNIT, WIDE), BF),
            vmem((SLOTS, UNIT // 2, WIDE), BF),
            vmem((FINALS, 2, UNIT, WIDE), BF),
            dma((SLOTS, 2, 2)),
            dma((SLOTS, 2, 2)),
            dma((SLOTS, 2, 2)),
            dma((SLOTS, 2)),
            dma((SLOTS, 2)),
            dma((FINALS, 2)),
            dma((FINALS, 2)),
        ]
        + [vmem((width, tokens), BF) for width in widths],
        compiler_params=pltpu.CompilerParams(
            vmem_limit_bytes=58 * 2**20, collective_id=number, has_side_effects=True
        ),
        cost_estimate=pl.CostEstimate(
            flops=1024, bytes_accessed=len(places) * 8 * UNIT * WIDE, transcendentals=0
        ),
        name="reduce_products",
    )(*operands)
    if small is not None:
        result = list(result)
        result[len(pairs)] = result[len(pairs)][: small.shape[1], : small.shape[2]]
    return result


def body(
    block_input,
    action_table,
    norm_gain,
    norm_bias,
    space_qkv,
    space_out,
    time_qkv,
    time_out,
    ffn_in,
    ffn_bias_in,
    ffn_out,
    ffn_bias_out,
    out_grad,
    frame_segment,
    frame_action,
):
    tm, halves = lax.axis_size("tm"), lax.axis_size("space")
    slot, side = lax.axis_index("tm"), lax.axis_index("space")
    frame_count, half_grid = block_input.shape[1], block_input.shape[2]
    own_frames = frame_count // halves
    grid_all = half_grid * halves
    cut = half_grid // tm
    all_frames = frame_count * tm
    rows_dev = frame_count * half_grid
    width = MODEL // tm
    hidden_units = ffn_bias_in.shape[0]

    space_in_w, space_out_w, small, inputs = first_gather(
        (space_qkv, space_out),
        jnp.concatenate(
            [a.reshape(-1, width) for a in (action_table, norm_gain, norm_bias)]
            + [ffn_bias_out.reshape(1, width), ffn_bias_in.reshape(-1, width)]
        ),
        block_input[0],
    )
    lines = ACTIONS + 7
    by_row = small[:, :lines].transpose(1, 0, 2).reshape(lines, MODEL)
    table_full = by_row[:ACTIONS]
    gains = by_row[ACTIONS : ACTIONS + 3].astype(F32)
    shifts = by_row[ACTIONS + 3 : ACTIONS + 6].astype(F32)
    bias_out = by_row[ACTIONS + 6].astype(F32)
    bias_in = small[:, lines:].reshape(-1).astype(F32)

    actions = lax.dynamic_slice(frame_action[0], (side * own_frames,), (own_frames,))
    one_hot = (actions[:, None] == jnp.arange(ACTIONS)[None, :]).astype(BF)
    embedded = forward_dot(one_hot, table_full)

    blocks_in = [jnp.concatenate((time_qkv, time_out), axis=1), ffn_in, ffn_out]
    came, passed = [], []
    for i, block in enumerate(blocks_in):
        if tm == 8:
            earlier = (passed[0] if i == 1 else came[1]) if i else (space_out_w,)
            blocks_in[i] = after(block, *earlier)
        came.append(first_hops(blocks_in[i]))
        passed.append(second_hops(came[i]))
    split = ((3 * MODEL, MODEL), (ffn_in.shape[1],), (MODEL,))
    gathered = [gather_rows(*all_of) for all_of in zip(blocks_in, came, passed, split)]
    time_in_w, time_out_w = gathered[0]
    (ffn_in_w,), (ffn_out_w,) = gathered[1:]
    if passed[1] is not None:
        out_grad = after(out_grad, *passed[1])

    hidden_zero = (inputs.astype(F32) + embedded[:, None, :]).reshape(rows_dev, MODEL)
    normed_one = layer_norm(hidden_zero, gains[0], shifts[0]).astype(BF)
    packed_one = forward_dot(normed_one, space_in_w).astype(BF)
    space_mixed, space_probs = attention(packed_one, grid_all)
    hidden_one_own = (hidden_zero + forward_dot(space_mixed, space_out_w)).astype(BF)

    sent = hidden_one_own.reshape(own_frames, halves * tm, cut, MODEL)
    blocks_t = lax.all_to_all(sent, ("space", "tm"), 1, 0)
    hidden_one = lax.optimization_barrier(
        blocks_t.reshape(halves, tm, own_frames, cut, MODEL)
        .transpose(1, 0, 2, 3, 4)
        .reshape(rows_dev, MODEL)
    ).astype(F32)
    grad_out_low = lax.all_to_all(out_grad[0], "tm", 1, 0, tiled=True).reshape(rows_dev, MODEL)
    grad_out = grad_out_low.astype(F32)
    groups = (
        frame_segment[0].astype(jnp.int32)[:, None] * cut + jnp.arange(cut, dtype=jnp.int32)
    ).reshape(rows_dev)

    normed_two = layer_norm(hidden_one, gains[1], shifts[1]).astype(BF)
    packed_two = forward_dot(normed_two, time_in_w).astype(BF)
    if came[1] is not None:
        packed_two = after(packed_two, *came[1])
    time_mixed, time_probs = attention(packed_two, rows_dev, groups)
    hidden_two = hidden_one + forward_dot(time_mixed, time_out_w)
    normed_three = layer_norm(hidden_two, gains[2], shifts[2]).astype(BF)
    pre_act = forward_dot(normed_three, ffn_in_w) + bias_in
    activated, gelu_pull = jax.vjp(jax.nn.gelu, pre_act)
    act_low, slope = lax.optimization_barrier(
        (activated.astype(BF), gelu_pull(jnp.ones_like(pre_act))[0].astype(BF))
    )
    block_out = (hidden_two + forward_dot(act_low, ffn_out_w) + bias_out).astype(BF)
    block_output = lax.all_to_all(
        block_out.reshape(all_frames, cut, MODEL), "tm", 0, 1, tiled=True
    )[None]

    bias_out_grad = jnp.sum(grad_out, axis=0)
    grad_pre_low = (back_dot(grad_out_low, ffn_out_w) * slope.astype(F32)).astype(BF)
    bias_in_grad = jnp.sum(grad_pre_low.astype(F32), axis=0)
    norm_pull = jax.vjp(layer_norm, hidden_two, gains[2], shifts[2])[1]
    grad_hidden, gain_three, shift_three = norm_pull(back_dot(grad_pre_low, ffn_in_w))
    grad_two = grad_out + grad_hidden
    time_branch = grad_two.astype(BF)
    time_grad_mixed = back_dot(time_branch, time_out_w).astype(BF)
    grad_packed_two = attention_back(packed_two, time_probs, time_grad_mixed, rows_dev)
    norm_pull = jax.vjp(layer_norm, hidden_one, gains[1], shifts[1])[1]
    grad_hidden, gain_two, shift_two = norm_pull(back_dot(grad_packed_two, time_in_w))
    grad_one_low = (grad_two + grad_hidden).astype(BF)

    sent = (
        grad_one_low.reshape(tm, halves, own_frames, cut, MODEL)
        .transpose(1, 0, 2, 3, 4)
        .reshape(halves * tm, own_frames, cut, MODEL)
    )
    space_branch = lax.all_to_all(sent, ("space", "tm"), 0, 1).reshape(rows_dev, MODEL)
    space_grad_mixed = back_dot(space_branch, space_out_w).astype(BF)
    ffn_out_grad, ffn_in_grad, time_qkv_grad, time_out_grad, grad_packed_one = reduce_products(
        (
            (act_low, grad_out_low),
            (normed_three, grad_pre_low),
            (normed_two, grad_packed_two),
            (time_mixed, time_branch),
        ),
        1,
        attend=(packed_one, space_probs, space_grad_mixed),
    )
    norm_pull = jax.vjp(layer_norm, hidden_zero, gains[0], shifts[0])[1]
    grad_hidden, gain_one, shift_one = norm_pull(back_dot(grad_packed_one, space_in_w))
    grad_zero = space_branch.astype(F32) + grad_hidden
    frame_grad = jnp.sum(grad_zero.reshape(own_frames, grid_all, MODEL), axis=1)
    action_grad = jnp.dot(one_hot.astype(F32).T, frame_grad, precision=lax.Precision.HIGHEST)
    input_grad = lax.all_to_all(
        grad_zero.astype(BF).reshape(own_frames, grid_all, MODEL), "space", 1, 0, tiled=True
    ).astype(F32)[None]

    by_row = jnp.concatenate(
        (
            action_grad,
            jnp.stack((gain_one, gain_two, gain_three, shift_one, shift_two, shift_three)),
            bias_out_grad[None],
        )
    )
    shares = jnp.concatenate(
        (
            by_row.reshape(lines, tm, width).transpose(1, 0, 2),
            bias_in_grad.reshape(tm, -1, width),
        ),
        axis=1,
    )
    space_out_grad, space_qkv_grad, small_grads = reduce_products(
        ((space_mixed, space_branch), (normed_one, grad_packed_one)), 2, small=shares
    )
    return (
        block_output,
        input_grad,
        small_grads[:ACTIONS],
        small_grads[ACTIONS : ACTIONS + 3],
        small_grads[ACTIONS + 3 : ACTIONS + 6],
        space_qkv_grad,
        space_out_grad,
        time_qkv_grad,
        time_out_grad,
        ffn_in_grad,
        small_grads[lines:].reshape(hidden_units),
        ffn_out_grad,
        small_grads[ACTIONS + 6],
    )


def solution(mesh):
    placed = (
        P("row", "tm", "space", None),
        P(None, "tm"),
        P(None, "tm"),
        P(None, "tm"),
        P("tm", None),
        P("tm", None),
        P("tm", None),
        P("tm", None),
        P("tm", None),
        P("tm"),
        P("tm", None),
        P("tm"),
        P("row", "tm", "space", None),
        P("row", None),
        P("row", "tm"),
    )
    return jax.shard_map(
        body,
        mesh=mesh,
        in_specs=placed,
        out_specs=(
            P("row", "tm", "space", None),
            P("row", "tm", "space", None),
            P(None, "tm"),
            P(None, "tm"),
            P(None, "tm"),
            P("tm", None),
            P("tm", None),
            P("tm", None),
            P("tm", None),
            P("tm", None),
            P("tm"),
            P("tm", None),
            P("tm"),
        ),
        check_vma=False,
    )
```

time: 663 us -> 558 us (0.84)
  starting transfers between devices: 69.9 us -> 40.9 us
  waiting for transfers between devices: 88.8 us -> 60.4 us
  local copies, waits for them, and re-layouts: 71.6 us -> 47 us
  Pallas kernels: 337 us -> 321 us
  other arithmetic: 25.5 us -> 14.8 us
  matrix products: 59.5 us -> 66.2 us
    ppermute x52 -> x27, waiting for transfers between devices: 88.8 us -> 54.3 us  [hop(): return lax.ppermute(block, axis, [(i, i ^ flip) for i in range(size)])]
    ppermute x52 -> x27, starting transfers between devices: 43.1 us -> 15.4 us  [hop(): return lax.ppermute(block, axis, [(i, i ^ flip) for i in range(size)])]
    unnamed x148 -> x126, local copies, waits for them, and re-layouts: 41.7 us -> 19.9 us
    pallas_call x2 -> x1, Pallas kernels: 35.9 us -> 19.7 us  [attention_back(): pl.pallas_call(lambda *refs: attn_bwd_kernel(span // TILE, *refs), grid=(...]
    dot_general x6, matrix products: 25.4 us -> 33.8 us  [back_dot(): lax.dot_general(grad_rows, weight, (((1,), (1,)), ((), ())), preferred_el...]
    slice x8 -> x6, local copies, waits for them, and re-layouts: 9.91 us -> 3.17 us  [second_hops(): return (hop(came[0][:half], 'tm', 4), hop(came[1][half:], 'tm', 2))]
    pallas_call x8 -> x3, Pallas kernels: 264 us -> 266 us  [the longest x2 225 us: reduce_products(): pl.pallas_call(lambda *refs: reduce_kernel(len(pairs), places, small is n...]
  transfers between devices with their start and end apart: 58 -> 32, of which waited for: 10 -> 8; matrix products, arithmetic and copies ran while one was open for 13% -> 13% of each run, Pallas kernels for 48% -> 47%
where the time goes in v3:
time: 558 us; the launch traced here: 552 us
  Pallas kernels  321 us (58%)
  matrix products  66.2 us (12%)
  waiting for transfers between devices  60.4 us (11%)
  local copies, waits for them, and re-layouts  47 us (8%)
  starting transfers between devices  40.9 us (7%)
  other arithmetic  14.8 us (3%)
    pallas_call x2, Pallas kernels, reduce_products(): pl.pallas_call(lambda *refs: reduce_kernel(len(pairs), places, small is n...  225 us
    ppermute x27, waiting for transfers between devices, hop(): return lax.ppermute(block, axis, [(i, i ^ flip) for i in range(size)])  54.3 us
    pallas_call x1, Pallas kernels, first_gather(): pl.pallas_call(first_kernel, in_specs=[pl.BlockSpec(memory_space=pltpu.VM...  41.7 us
    dot_general x6, matrix products, back_dot(): lax.dot_general(grad_rows, weight, (((1,), (1,)), ((), ())), preferred_el...  33.8 us
    dot_general x7, matrix products, forward_dot(): return jnp.dot(values, weight, preferred_element_type=F32)  32.1 us
    pallas_call x2, Pallas kernels, attention(): pl.pallas_call(lambda *refs: attn_fwd_kernel(span // TILE, masked, *refs)...  26.4 us
    unnamed x126, local copies, waits for them, and re-layouts  19.9 us
    pallas_call x1, Pallas kernels, attention_back(): pl.pallas_call(lambda *refs: attn_bwd_kernel(span // TILE, *refs), grid=(...  19.7 us
  transfers between devices with their start and end apart: 32, of which 8 were waited for; matrix products, arithmetic and copies ran while one was open for 13% of the time, Pallas kernels for 47%

profile of v3, /device:TPU:0, one launch (start us, length us, event | category | flops | bytes accessed | tf_op | source)
XLA Modules:
  0.0 552.0 jit_solution(2762757198619627707)
XLA Ops:
  0.7 2.3 concatenate.27
  4.4 41.7 %first_gather.1 = (bf16[1024,3072]{1,0:T(8,128)(2,1)S(1)}, bf16[1024,1024]{1,0:T(8,128)(2,1)S(1)}, bf16[8,32,128]{2,1,0:T(8,128)(2,1)S(1)}, bf16[2,256,1024]{2,1,0:T(8,128)(2,1)S(1)}) custom-call(bf16[128,3072]{1,0:T(8,128)(2,1)S(1)} %copy-done.15, bf16[128,1024]{1,0:T(8,128)(2,1)S(1)} %copy-done.22, bf16[32,128]{1,0:T(8,128)(2,1)S(1)} %pad.8.refs_2_, ...), custom_call_target="tpu_custom_call" | custom-call | bytes 16777216 | tf_op jit(solution)/shard_map/first_gather/pallas_call | solution.py:403
  46.1 2.7 copy-done.23
  57.0 3.7 convolution_convert_fusion.1.refs_0_.refs_8_
  60.7 10.4 %attention_forward.2 = (bf16[512,1024]{1,0:T(8,128)(2,1)S(1)}, bf16[16,512,256]{2,1,0:T(8,128)(2,1)}) custom-call(bf16[512,3072]{1,0:T(8,128)(2,1)S(1)} %convolution_convert_fusion.1.refs_0_.refs_8_), custom_call_target="tpu_custom_call" | custom-call | flops 1073741824 | bytes 8388608 | tf_op jit(solution)/shard_map/attention_forward/pallas_call | solution.py:174
  73.5 4.9 all-to-all-start
  83.1 22.1 %collective-permute-done.7.refs_8_ = bf16[64,4096]{1,0:T(8,128)(2,1)S(1)} collective-permute-done((bf16[64,4096]{1,0:T(8,128)(2,1)S(1)}, bf16[64,4096]{1,0:T(8,128)(2,1)S(1)}, u32[]{:S(2)}, u32[]{:S(2)}) %collective-permute-start.7) | collective-permute-done | bytes 524320 | tf_op jit(solution)/shard_map/ppermute | solution.py:215
  109.8 21.1 %collective-permute-done.10.refs_4_ = bf16[128,4096]{1,0:T(8,128)(2,1)S(1)} collective-permute-done((bf16[128,4096]{1,0:T(8,128)(2,1)}, bf16[128,4096]{1,0:T(8,128)(2,1)S(1)}, u32[]{:S(2)}, u32[]{:S(2)}) %collective-permute-start.10) | collective-permute-done | bytes 1048608 | tf_op jit(solution)/shard_map/ppermute | solution.py:215
  134.0 3.0 lay_rows.3
  138.3 3.7 convolution_convert_fusion.refs_0_
  143.7 16.0 %attention_forward.3 = (bf16[512,1024]{1,0:T(8,128)(2,1)S(1)}, bf16[16,512,512]{2,1,0:T(8,128)(2,1)}) custom-call(bf16[512,3072]{1,0:T(8,128)(2,1)S(1)} %convolution_convert_fusion.refs_0_, s32[512,1]{1,0:T(8,128)S(1)} %add.188.refs_1_, s32[1,512]{1,0:T(1,128)S(1)} %add.172.refs_2_), custom_call_target="tpu_custom_call" | custom-call | flops 2147483648 | bytes 12582912 | tf_op jit(solution)/shard_map/attention_forward/pallas_call | solution.py:174
  159.9 8.8 %collective-permute-done.14.refs_6_ = bf16[64,4096]{1,0:T(8,128)(2,1)} collective-permute-done((bf16[64,4096]{1,0:T(8,128)(2,1)S(1)}, bf16[64,4096]{1,0:T(8,128)(2,1)}, u32[]{:S(2)}, u32[]{:S(2)}) %collective-permute-start.14) | collective-permute-done | bytes 524320 | tf_op jit(solution)/shard_map/ppermute | solution.py:215
  178.9 4.4 all-to-all-start.2
  186.4 2.9 lay_rows.4
  190.1 11.8 %fusion.6 = (bf16[512,4096]{1,0:T(8,128)(2,1)}, bf16[512,4096]{1,0:T(8,128)(2,1)}) fusion(f32[4096]{0:T(1024)S(1)} %convert.5, bf16[512,1024]{1,0:T(8,128)(2,1)S(1)} %copy-done.44, bf16[1024,4096]{1,0:T(8,128)(2,1)S(1)} %lay_rows.4), kind=kOutput, calls=%fused_computation.8 | convolution fusion | flops 4339007488 | bytes 17842176 | tf_op jit(solution)/shard_map/dot_general | solution.py:33
  201.9 2.6 copy.44
  204.6 2.8 lay_rows.5
  207.4 10.6 %convert_reduce_fusion = (f32[4096]{0:T(1024)S(1)}, bf16[512,4096]{1,0:T(8,128)(2,1)}) fusion(bf16[512,4096]{1,0:T(8,128)(2,1)} %get-tuple-element.52, bf16[512,1024]{1,0:T(8,128)(2,1)} %bitcast.138, bf16[4096,1024]{1,0:T(8,128)(2,1)S(1)} %lay_rows.5), kind=kOutput, calls=%fused_computation.9 | convolution fusion | flops 4305448960 | bytes 17842176 | tf_op jit(solution)/shard_map/dot_general | solution.py:43
  218.0 9.0 %multiply_reduce_fusion = (f32[1024]{0:T(1024)S(1)}, f32[512]{0:T(512)S(1)}, f32[1024]{0:T(1024)S(1)}, f32[512,1024]{1,0:T(8,128)S(1)}) fusion(f32[512,1024]{1,0:T(8,128)S(1)} %copy-done.38, f32[512]{0:T(512)S(1)} %fusion.27, f32[512]{0:T(512)S(1)} %broadcast_multiply_fusion, f32[1024]{0:T(1024)S(1)} %bitcast.159, ...), kind=kOutput, calls=%fused_computation.37 | convolution fusion | flops 4299159040 | bytes 16795648 | tf_op jit(solution)/shard_map/dot_general | solution.py:43
  231.1 19.7 %attention_backward.1.refs_6_ = bf16[512,3072]{1,0:T(8,128)(2,1)S(1)} custom-call(bf16[512,3072]{1,0:T(8,128)(2,1)} %copy-done.31, bf16[16,512,512]{2,1,0:T(8,128)(2,1)} %get-tuple-element.53.refs_1_, bf16[512,1024]{1,0:T(8,128)(2,1)S(1)} %convolution_convert_fusion.3.refs_2_), custom_call_target="tpu_custom_call" | custom-call | flops 4294967296 | bytes 15728640 | tf_op jit(solution)/shard_map/attention_backward/pallas_call | solution.py:196
  250.9 3.7 fusion.32
  258.1 6.7 %all-to-all-start.3 = ((bf16[16,2,1,16,1024]{4,3,1,2,0:T(8,128)(2,1)}), bf16[16,2,1,16,1024]{4,3,1,2,0:T(8,128)(2,1)}, u32[]{:S(2)}, u32[]{:S(2)}) async-start(bf16[16,2,1,16,1024]{4,3,1,2,0:T(8,128)(2,1)} %bitcast.143), calls=%async_computation.3 | async-start | bytes 2097152 | tf_op jit(solution)/shard_map/all_to_all | solution.py:815
  264.8 10.1 %add_convert_fusion.1 = bf16[512,1024]{1,0:T(8,128)(2,1)} fusion(f32[512,1024]{1,0:T(8,128)S(1)} %copy-done.38, bf16[512,4096]{1,0:T(8,128)(2,1)} %get-tuple-element.49.refs_0_, bf16[4096,1024]{1,0:T(8,128)(2,1)} %copy-done.2, f32[1024]{0:T(1024)S(1)} %bitcast.178), kind=kOutput, calls=%fused_computation.44 | convolution fusion | flops 4296540160 | bytes 15732736 | tf_op jit(solution)/shard_map/dot_general | solution.py:33
  275.0 6.1 %all-to-all-done.3 = bf16[16,2,1,16,1024]{4,3,1,2,0:T(8,128)(2,1)} async-done(((bf16[16,2,1,16,1024]{4,3,1,2,0:T(8,128)(2,1)}), bf16[16,2,1,16,1024]{4,3,1,2,0:T(8,128)(2,1)}, u32[]{:S(2)}, u32[]{:S(2)}) %all-to-all-start.3) | async-done | bytes 1048608 | tf_op jit(solution)/shard_map/all_to_all | solution.py:815
  281.1 4.8 all-to-all-start.1
  287.2 2.3 convolution_convert_fusion.2.refs_10_
  289.5 148.4 %reduce_products.2 = (f32[512,1024]{1,0:T(8,128)}, f32[128,4096]{1,0:T(8,128)}, f32[128,3072]{1,0:T(8,128)}, f32[128,1024]{1,0:T(8,128)}, bf16[512,3072]{1,0:T(8,128)(2,1)}) custom-call(bf16[512,4096]{1,0:T(8,128)(2,1)} %get-tuple-element.49.refs_0_, bf16[512,1024]{1,0:T(8,128)(2,1)} %add_convert_fusion.2.refs_1_, bf16[512,1024]{1,0:T(8,128)(2,1)} %copy-done.43, ...), custom_call_target="tpu_custom_call" | custom-call | flops 1024 | bytes 6291456 | tf_op jit(solution)/shard_map/reduce_products/pallas_call | solution.py:660
  437.9 7.0 %multiply_reduce_fusion.1 = (f32[1024]{0:T(1024)S(1)}, f32[512]{0:T(512)S(1)}, f32[1024]{0:T(1024)S(1)}, f32[512,1024]{1,0:T(8,128)S(1)}) fusion(f32[2,256,1024]{2,1,0:T(8,128)S(1)} %copy-done.36, f32[512]{0:T(512)S(1)} %rsqrt.33, f32[512]{0:T(512)S(1)} %bitcast.163, f32[1024]{0:T(1024)S(1)} %bitcast.156, bf16[512,3072]{1,0:T(8,128)(2,1)} %get-tuple-element.55.refs_3_, ...), kind=kOutput, calls=%fused_computation.38 | convolution fusion | flops 3225417216 | bytes 13649920 | tf_op jit(solution)/shard_map/dot_general | solution.py:43
  446.1 2.0 copy.47
  448.2 4.6 all-to-all-start.4
  456.2 2.3 copy.42
  458.5 76.2 %reduce_products.3 = (f32[128,1024]{1,0:T(8,128)}, f32[128,3072]{1,0:T(8,128)}, f32[128,256]{1,0:T(8,128)}) custom-call(bf16[512,1024]{1,0:T(8,128)(2,1)} %copy-done.12, bf16[512,1024]{1,0:T(8,128)(2,1)} %copy-done.42, bf16[512,1024]{1,0:T(8,128)(2,1)} %bitcast.141, bf16[512,3072]{1,0:T(8,128)(2,1)} %get-tuple-element.55.refs_3_, ...), custom_call_target="tpu_custom_call" | custom-call | flops 1024 | bytes 2359296 | tf_op jit(solution)/shard_map/reduce_products/pallas_call | solution.py:660
  (247 shorter events, 72.0 us)
Async XLA Ops:
  50.1 28.3 %collective-permute-start.3 = (bf16[128,4096]{1,0:T(8,128)(2,1)S(1)}, bf16[128,4096]{1,0:T(8,128)(2,1)S(1)}, u32[]{:S(2)}, u32[]{:S(2)}) collective-permute-start(bf16[128,4096]{1,0:T(8,128)(2,1)S(1)} %pad_maximum_fusion.refs_0_), channel_id=1, source_target_pairs={{0,8},{2,10},{4,12},{6,14},{8,0},{10,2},{12,4},{14,6},{1,9},{3,11}... | collective-permute-start | bytes 3145736 | tf_op jit(solution)/shard_map/ppermute | solution.py:215
  51.6 28.8 %collective-permute-start.1 = (bf16[128,4096]{1,0:T(8,128)(2,1)S(1)}, bf16[128,4096]{1,0:T(8,128)(2,1)}, u32[]{:S(2)}, u32[]{:S(2)}) collective-permute-start(bf16[128,4096]{1,0:T(8,128)(2,1)S(1)} %pad_maximum_fusion.refs_0_), channel_id=1, source_target_pairs={{0,4},{2,6},{4,0},{6,2},{8,12},{10,14},{12,8},{14,10},{1,5},{3,7},... | collective-permute-start | bytes 3145736 | tf_op jit(solution)/shard_map/ppermute | solution.py:215
  73.5 34.7 %all-to-all-start = ((bf16[1,2,16,16,1024]{4,3,1,0,2:T(8,128)(2,1)}), bf16[1,2,16,16,1024]{4,3,1,0,2:T(8,128)(2,1)}, u32[]{:S(2)}, u32[]{:S(2)}) async-start(bf16[1,2,16,16,1024]{4,3,1,0,2:T(8,128)(2,1)} %copy.39), calls=%async_computation | async-start | bytes 2097152 | tf_op jit(solution)/shard_map/all_to_all | solution.py:768
  78.5 26.7 %collective-permute-start.7 = (bf16[64,4096]{1,0:T(8,128)(2,1)S(1)}, bf16[64,4096]{1,0:T(8,128)(2,1)S(1)}, u32[]{:S(2)}, u32[]{:S(2)}) collective-permute-start(bf16[64,4096]{1,0:T(8,128)(2,1)S(1)} %slice.125), channel_id=1, source_target_pairs={{0,4},{2,6},{4,0},{6,2},{8,12},{10,14},{12,8},{14,10},{1,5},{3,7},... | collective-permute-start | bytes 1572872 | tf_op jit(solution)/shard_map/ppermute | solution.py:215
  81.5 24.5 %collective-permute-start.5 = (bf16[64,4096]{1,0:T(8,128)(2,1)S(1)}, bf16[64,4096]{1,0:T(8,128)(2,1)}, u32[]{:S(2)}, u32[]{:S(2)}) collective-permute-start(bf16[64,4096]{1,0:T(8,128)(2,1)S(1)} %slice.124), channel_id=1, source_target_pairs={{0,8},{2,10},{4,12},{6,14},{8,0},{10,2},{12,4},{14,6},{1,9},{3,11}... | collective-permute-start | bytes 1572872 | tf_op jit(solution)/shard_map/ppermute | solution.py:215
  106.0 24.9 %collective-permute-start.10 = (bf16[128,4096]{1,0:T(8,128)(2,1)}, bf16[128,4096]{1,0:T(8,128)(2,1)S(1)}, u32[]{:S(2)}, u32[]{:S(2)}) collective-permute-start(bf16[128,4096]{1,0:T(8,128)(2,1)} %refs_0_.2), channel_id=1, source_target_pairs={{0,8},{2,10},{4,12},{6,14},{8,0},{10,2},{12,4},{14,6},{1,9},{3,11}... | collective-permute-start | bytes 3145736 | tf_op jit(solution)/shard_map/ppermute | solution.py:215
  106.4 24.6 %collective-permute-start.9 = (bf16[128,4096]{1,0:T(8,128)(2,1)}, bf16[128,4096]{1,0:T(8,128)(2,1)S(1)}, u32[]{:S(2)}, u32[]{:S(2)}) collective-permute-start(bf16[128,4096]{1,0:T(8,128)(2,1)} %refs_0_.2), channel_id=1, source_target_pairs={{0,4},{2,6},{4,0},{6,2},{8,12},{10,14},{12,8},{14,10},{1,5},{3,7},... | collective-permute-start | bytes 3145736 | tf_op jit(solution)/shard_map/ppermute | solution.py:215
  107.2 24.7 %collective-permute-start = (bf16[128,4096]{1,0:T(8,128)(2,1)S(1)}, bf16[128,4096]{1,0:T(8,128)(2,1)}, u32[]{:S(2)}, u32[]{:S(2)}) collective-permute-start(bf16[128,4096]{1,0:T(8,128)(2,1)S(1)} %pad_maximum_fusion.refs_0_), channel_id=1, source_target_pairs={{0,2},{2,0},{4,6},{6,4},{8,10},{10,8},{12,14},{14,12},{1,3},{3,1},... | collective-permute-start | bytes 3145736 | tf_op jit(solution)/shard_map/ppermute | solution.py:215
  107.5 26.4 %collective-permute-start.4 = (bf16[128,4096]{1,0:T(8,128)(2,1)}, bf16[128,4096]{1,0:T(8,128)(2,1)}, u32[]{:S(2)}, u32[]{:S(2)}) collective-permute-start(bf16[128,4096]{1,0:T(8,128)(2,1)} %copy-done.10), channel_id=1, source_target_pairs={{0,2},{2,0},{4,6},{6,4},{8,10},{10,8},{12,14},{14,12},{1,3},{3,1},... | collective-permute-start | bytes 3145736 | tf_op jit(solution)/shard_map/ppermute | solution.py:215
  108.1 25.8 %collective-permute-start.2 = (bf16[128,4096]{1,0:T(8,128)(2,1)}, bf16[128,4096]{1,0:T(8,128)(2,1)}, u32[]{:S(2)}, u32[]{:S(2)}) collective-permute-start(bf16[128,4096]{1,0:T(8,128)(2,1)} %collective-permute-done.1.refs_2_), channel_id=1, source_target_pairs={{0,2},{2,0},{4,6},{6,4},{8,10},{10,8},{12,14},{14,12},{1,3},{3,1},... | collective-permute-start | bytes 3145736 | tf_op jit(solution)/shard_map/ppermute | solution.py:215
  130.9 2.7 collective-permute-start.8
  131.0 2.9 collective-permute-start.6
  131.9 36.8 %collective-permute-start.21 = (bf16[512,1024]{1,0:T(8,128)(2,1)}, bf16[512,1024]{1,0:T(8,128)(2,1)S(1)}, u32[]{:S(2)}, u32[]{:S(2)}) collective-permute-start(bf16[512,1024]{1,0:T(8,128)(2,1)} %refs_0_.3), channel_id=1, source_target_pairs={{0,8},{2,10},{4,12},{6,14},{8,0},{10,2},{12,4},{14,6},{1,9},{3,11}... | collective-permute-start | bytes 3145736 | tf_op jit(solution)/shard_map/ppermute | solution.py:215
  133.6 40.9 %collective-permute-start.11 = (bf16[128,4096]{1,0:T(8,128)(2,1)}, bf16[128,4096]{1,0:T(8,128)(2,1)}, u32[]{:S(2)}, u32[]{:S(2)}) collective-permute-start(bf16[128,4096]{1,0:T(8,128)(2,1)} %refs_0_.2), channel_id=1, source_target_pairs={{0,2},{2,0},{4,6},{6,4},{8,10},{10,8},{12,14},{14,12},{1,3},{3,1},... | collective-permute-start | bytes 3145736 | tf_op jit(solution)/shard_map/ppermute | solution.py:215
  137.0 22.8 %collective-permute-start.16 = (bf16[64,4096]{1,0:T(8,128)(2,1)S(1)}, bf16[64,4096]{1,0:T(8,128)(2,1)S(1)}, u32[]{:S(2)}, u32[]{:S(2)}) collective-permute-start(bf16[64,4096]{1,0:T(8,128)(2,1)S(1)} %slice.129), channel_id=1, source_target_pairs={{0,4},{2,6},{4,0},{6,2},{8,12},{10,14},{12,8},{14,10},{1,5},{3,7},... | collective-permute-start | bytes 1572872 | tf_op jit(solution)/shard_map/ppermute | solution.py:215
  137.4 31.2 %collective-permute-start.14 = (bf16[64,4096]{1,0:T(8,128)(2,1)S(1)}, bf16[64,4096]{1,0:T(8,128)(2,1)}, u32[]{:S(2)}, u32[]{:S(2)}) collective-permute-start(bf16[64,4096]{1,0:T(8,128)(2,1)S(1)} %slice.128), channel_id=1, source_target_pairs={{0,8},{2,10},{4,12},{6,14},{8,0},{10,2},{12,4},{14,6},{1,9},{3,11}... | collective-permute-start | bytes 1572872 | tf_op jit(solution)/shard_map/ppermute | solution.py:215
  142.0 31.6 %collective-permute-start.19 = (bf16[512,1024]{1,0:T(8,128)(2,1)}, bf16[512,1024]{1,0:T(8,128)(2,1)S(1)}, u32[]{:S(2)}, u32[]{:S(2)}) collective-permute-start(bf16[512,1024]{1,0:T(8,128)(2,1)} %refs_0_.3), channel_id=1, source_target_pairs={{0,4},{2,6},{4,0},{6,2},{8,12},{10,14},{12,8},{14,10},{1,5},{3,7},... | collective-permute-start | bytes 3145736 | tf_op jit(solution)/shard_map/ppermute | solution.py:215
  159.8 23.5 %collective-permute-start.13 = (bf16[128,4096]{1,0:T(8,128)(2,1)S(1)}, bf16[128,4096]{1,0:T(8,128)(2,1)}, u32[]{:S(2)}, u32[]{:S(2)}) collective-permute-start(bf16[128,4096]{1,0:T(8,128)(2,1)S(1)} %collective-permute-done.10.refs_4_), channel_id=1, source_target_pairs={{0,2},{2,0},{4,6},{6,4},{8,10},{10,8},{12,14},{14,12},{1,3},{3,1},... | collective-permute-start | bytes 3145736 | tf_op jit(solution)/shard_map/ppermute | solution.py:215
  168.6 15.3 %collective-permute-start.12 = (bf16[128,4096]{1,0:T(8,128)(2,1)S(1)}, bf16[128,4096]{1,0:T(8,128)(2,1)}, u32[]{:S(2)}, u32[]{:S(2)}) collective-permute-start(bf16[128,4096]{1,0:T(8,128)(2,1)S(1)} %collective-permute-done.9.refs_2_), channel_id=1, source_target_pairs={{0,2},{2,0},{4,6},{6,4},{8,10},{10,8},{12,14},{14,12},{1,3},{3,1},... | collective-permute-start | bytes 3145736 | tf_op jit(solution)/shard_map/ppermute | solution.py:215
  168.6 6.2 %collective-permute-start.17 = (bf16[64,4096]{1,0:T(8,128)(2,1)S(1)}, bf16[64,4096]{1,0:T(8,128)(2,1)S(1)}, u32[]{:S(2)}, u32[]{:S(2)}) collective-permute-start(bf16[64,4096]{1,0:T(8,128)(2,1)S(1)} %collective-permute-done.16.refs_8_), channel_id=1, source_target_pairs={{0,2},{2,0},{4,6},{6,4},{8,10},{10,8},{12,14},{14,12},{1,3},{3,1},... | collective-permute-start | bytes 1572872 | tf_op jit(solution)/shard_map/ppermute | solution.py:215
  173.6 10.2 %collective-permute-start.15 = (bf16[64,4096]{1,0:T(8,128)(2,1)}, bf16[64,4096]{1,0:T(8,128)(2,1)}, u32[]{:S(2)}, u32[]{:S(2)}) collective-permute-start(bf16[64,4096]{1,0:T(8,128)(2,1)} %collective-permute-done.14.refs_6_), channel_id=1, source_target_pairs={{0,2},{2,0},{4,6},{6,4},{8,10},{10,8},{12,14},{14,12},{1,3},{3,1},... | collective-permute-start | bytes 1572872 | tf_op jit(solution)/shard_map/ppermute | solution.py:215
  174.5 15.0 %collective-permute-start.25 = (bf16[256,1024]{1,0:T(8,128)(2,1)}, bf16[256,1024]{1,0:T(8,128)(2,1)}, u32[]{:S(2)}, u32[]{:S(2)}) collective-permute-start(bf16[256,1024]{1,0:T(8,128)(2,1)} %slice.131), channel_id=1, source_target_pairs={{0,4},{2,6},{4,0},{6,2},{8,12},{10,14},{12,8},{14,10},{1,5},{3,7},... | collective-permute-start | bytes 1572872 | tf_op jit(solution)/shard_map/ppermute | solution.py:215
  174.8 15.1 %collective-permute-start.23 = (bf16[256,1024]{1,0:T(8,128)(2,1)}, bf16[256,1024]{1,0:T(8,128)(2,1)}, u32[]{:S(2)}, u32[]{:S(2)}) collective-permute-start(bf16[256,1024]{1,0:T(8,128)(2,1)} %slice.130), channel_id=1, source_target_pairs={{0,8},{2,10},{4,12},{6,14},{8,0},{10,2},{12,4},{14,6},{1,9},{3,11}... | collective-permute-start | bytes 1572872 | tf_op jit(solution)/shard_map/ppermute | solution.py:215
  178.9 23.0 %all-to-all-start.2 = ((bf16[4,128,1024]{2,0,1:T(4,128)(2,1)}), bf16[4,128,1024]{2,0,1:T(4,128)(2,1)}, u32[]{:S(2)}, u32[]{:S(2)}) async-start(bf16[4,128,1024]{2,0,1:T(4,128)(2,1)} %bitcast.142), calls=%async_computation.2 | async-start | bytes 2097152 | tf_op jit(solution)/shard_map/all_to_all | solution.py:774
  183.3 21.2 %collective-permute-start.18 = (bf16[512,1024]{1,0:T(8,128)(2,1)}, bf16[512,1024]{1,0:T(8,128)(2,1)}, u32[]{:S(2)}, u32[]{:S(2)}) collective-permute-start(bf16[512,1024]{1,0:T(8,128)(2,1)} %refs_0_.3), channel_id=1, source_target_pairs={{0,2},{2,0},{4,6},{6,4},{8,10},{10,8},{12,14},{14,12},{1,3},{3,1},... | collective-permute-start | bytes 3145736 | tf_op jit(solution)/shard_map/ppermute | solution.py:215
  183.8 20.7 %collective-permute-start.22 = (bf16[512,1024]{1,0:T(8,128)(2,1)S(1)}, bf16[512,1024]{1,0:T(8,128)(2,1)}, u32[]{:S(2)}, u32[]{:S(2)}) collective-permute-start(bf16[512,1024]{1,0:T(8,128)(2,1)S(1)} %copy-done.7), channel_id=1, source_target_pairs={{0,2},{2,0},{4,6},{6,4},{8,10},{10,8},{12,14},{14,12},{1,3},{3,1},... | collective-permute-start | bytes 3145736 | tf_op jit(solution)/shard_map/ppermute | solution.py:215
  183.9 20.6 %collective-permute-start.20 = (bf16[512,1024]{1,0:T(8,128)(2,1)}, bf16[512,1024]{1,0:T(8,128)(2,1)}, u32[]{:S(2)}, u32[]{:S(2)}) collective-permute-start(bf16[512,1024]{1,0:T(8,128)(2,1)} %copy-done.8), channel_id=1, source_target_pairs={{0,2},{2,0},{4,6},{6,4},{8,10},{10,8},{12,14},{14,12},{1,3},{3,1},... | collective-permute-start | bytes 3145736 | tf_op jit(solution)/shard_map/ppermute | solution.py:215
  189.6 15.0 %collective-permute-start.26 = (bf16[256,1024]{1,0:T(8,128)(2,1)}, bf16[256,1024]{1,0:T(8,128)(2,1)S(1)}, u32[]{:S(2)}, u32[]{:S(2)}) collective-permute-start(bf16[256,1024]{1,0:T(8,128)(2,1)} %collective-permute-done.25.refs_8_), channel_id=1, source_target_pairs={{0,2},{2,0},{4,6},{6,4},{8,10},{10,8},{12,14},{14,12},{1,3},{3,1},... | collective-permute-start | bytes 1572872 | tf_op jit(solution)/shard_map/ppermute | solution.py:215
  189.9 14.6 %collective-permute-start.24 = (bf16[256,1024]{1,0:T(8,128)(2,1)}, bf16[256,1024]{1,0:T(8,128)(2,1)S(1)}, u32[]{:S(2)}, u32[]{:S(2)}) collective-permute-start(bf16[256,1024]{1,0:T(8,128)(2,1)} %collective-permute-done.23.refs_6_), channel_id=1, source_target_pairs={{0,2},{2,0},{4,6},{6,4},{8,10},{10,8},{12,14},{14,12},{1,3},{3,1},... | collective-permute-start | bytes 1572872 | tf_op jit(solution)/shard_map/ppermute | solution.py:215
  258.1 23.0 %all-to-all-start.3 = ((bf16[16,2,1,16,1024]{4,3,1,2,0:T(8,128)(2,1)}), bf16[16,2,1,16,1024]{4,3,1,2,0:T(8,128)(2,1)}, u32[]{:S(2)}, u32[]{:S(2)}) async-start(bf16[16,2,1,16,1024]{4,3,1,2,0:T(8,128)(2,1)} %bitcast.143), calls=%async_computation.3 | async-start | bytes 2097152 | tf_op jit(solution)/shard_map/all_to_all | solution.py:815
  281.1 167.1 %all-to-all-start.1 = ((bf16[32,16,1024]{2,1,0:T(8,128)(2,1)}), bf16[32,16,1024]{2,1,0:T(8,128)(2,1)}, u32[]{:S(2)}, u32[]{:S(2)}) async-start(bf16[32,16,1024]{2,1,0:T(8,128)(2,1)} %bitcast.147), calls=%async_computation.1 | async-start | bytes 2097152 | tf_op jit(solution)/shard_map/all_to_all | solution.py:793
  448.2 91.6 %all-to-all-start.4 = ((bf16[2,256,1024]{2,0,1:T(2,128)(2,1)}), bf16[2,256,1024]{2,0,1:T(2,128)(2,1)}, u32[]{:S(2)}, u32[]{:S(2)}) async-start(bf16[2,256,1024]{2,0,1:T(2,128)(2,1)} %copy.47), calls=%async_computation.4 | async-start | bytes 2097152 | tf_op jit(solution)/shard_map/all_to_all | solution.py:832
  (59 other events, 855.3 us)

commit v4 on v3

--- a/solution.py
+++ b/solution.py
@@ -72,6 +72,60 @@
     if isinstance(pair, int):
         return pl.ds(part * MODEL + pair * PAIR, PAIR)
     return pl.ds(pl.multiple_of(part * MODEL + pair * PAIR, PAIR), PAIR)
+
+
+def start_swap(to_all, src_ref, dst_ref, sems, local_sem):
+    me, size = lax.axis_index("tm"), sems.shape[0]
+    whole, part = (dst_ref, src_ref) if to_all else (src_ref, dst_ref)
+    frames, cut = part.shape[0], whole.shape[1]
+
+    def some_frames(ref, device):
+        return ref.at[pl.ds(pl.multiple_of(device * frames, frames), frames)]
+
+    def some_places(ref, device):
+        return ref.at[:, pl.ds(pl.multiple_of(device * cut, cut), cut), :]
+
+    def ends(device):
+        if to_all:
+            return some_places(src_ref, device), some_frames(dst_ref, me)
+        return some_frames(src_ref, device), some_places(dst_ref, me)
+
+    barrier = pltpu.get_barrier_semaphore()
+    for flip in range(1, size):
+        pl.semaphore_signal(
+            barrier, inc=1, device_id={"tm": me ^ flip}, device_id_type=pl.DeviceIdType.MESH
+        )
+    pl.semaphore_wait(barrier, size - 1)
+    copies = []
+    for flip in range(1, size):
+        src, dst = ends(me ^ flip)
+        copies.append(
+            pltpu.make_async_remote_copy(
+                src_ref=src,
+                dst_ref=dst,
+                send_sem=sems.at[flip, 0],
+                recv_sem=sems.at[flip, 1],
+                device_id={"tm": me ^ flip},
+                device_id_type=pl.DeviceIdType.MESH,
+            )
+        )
+    src, dst = ends(me)
+    copies.append(pltpu.make_async_copy(src, dst, local_sem))
+    for copy in copies:
+        copy.start()
+    return copies
+
+
+def swap_plain(to_all, block):
+    split, concat = (1, 0) if to_all else (0, 1)
+    return lax.all_to_all(block, "tm", split, concat, tiled=True)
+
+
+def swapped_shape(to_all, block, size):
+    first, second, width = block.shape
+    if to_all:
+        return (first * size, second // size, width)
+    return (first // size, second * size, width)
 
 
 def attn_fwd_kernel(tiles, masked, packed_ref, *refs):
@@ -111,48 +165,61 @@
     lax.fori_loop(0, PAIRS, one_pair, 0, unroll=2)
 
 
-def attn_bwd_pair(base, tiles, pair, packed_ref, probs_ref, grad_ref, out_ref, accs=None):
-    for t in reversed(range(tiles)):
-        mine = pl.ds(base + t * TILE, TILE)
-        seen = pl.ds(base, (t + 1) * TILE)
-        query = packed_ref[mine, pair_cols(pair, 0)] * jnp.asarray(SCALE, BF)
-        key = packed_ref[seen, pair_cols(pair, 1)]
-        value = packed_ref[seen, pair_cols(pair, 2)]
-        grad = grad_ref[mine, pair_cols(pair, 0)]
-        dqs, dks, dvs = [], [], []
-        for half in range(2):
+def attn_bwd_tile(
+    t, tiles, pair, packed_ref, probs_ref, grad_ref, out_ref, accs=None, base=0, probs_pair=None
+):
+    mine = pl.ds(base + t * TILE, TILE)
+    seen = pl.ds(base, (t + 1) * TILE)
+    query = packed_ref[mine, pair_cols(pair, 0)] * jnp.asarray(SCALE, BF)
+    key = packed_ref[seen, pair_cols(pair, 1)]
+    value = packed_ref[seen, pair_cols(pair, 2)]
+    grad = grad_ref[mine, pair_cols(pair, 0)]
+    dqs, dks, dvs = [], [], []
+    for half in range(2):
+        if probs_pair is None:
             probs_low = probs_ref[2 * pair + half, mine, pl.ds(0, (t + 1) * TILE)]
-            probs = probs_low.astype(F32)
-            dprobs = dot_nt(of_head(half, grad), value)
-            delta = jnp.sum(dprobs * probs, axis=1, keepdims=True)
-            dscores = (probs * (dprobs - delta)).astype(BF)
-            dqs.append(dot_nn(dscores, key))
-            dks.append(dot_tn(dscores, query))
-            dvs.append(dot_tn(probs_low, grad))
-        out_ref[mine, pair_cols(pair, 0)] = (join_heads(*dqs) * SCALE).astype(BF)
-        dkey, dvalue = join_heads(*dks), join_heads(*dvs)
-        if tiles == 1:
-            out_ref[seen, pair_cols(pair, 1)] = dkey.astype(BF)
-            out_ref[seen, pair_cols(pair, 2)] = dvalue.astype(BF)
-        elif t == tiles - 1:
-            accs[0][...] = dkey
-            accs[1][...] = dvalue
         else:
-            accs[0][pl.ds(0, (t + 1) * TILE), :] += dkey
-            accs[1][pl.ds(0, (t + 1) * TILE), :] += dvalue
-    if tiles > 1:
+            probs_low = probs_pair[half]
+        probs = probs_low.astype(F32)
+        dprobs = dot_nt(of_head(half, grad), value)
+        delta = jnp.sum(dprobs * probs, axis=1, keepdims=True)
+        dscores = (probs * (dprobs - delta)).astype(BF)
+        dqs.append(dot_nn(dscores, key))
+        dks.append(dot_tn(dscores, query))
+        dvs.append(dot_tn(probs_low, grad))
+    out_ref[mine, pair_cols(pair, 0)] = (join_heads(*dqs) * SCALE).astype(BF)
+    dkey, dvalue = join_heads(*dks), join_heads(*dvs)
+    if tiles == 1:
+        out_ref[seen, pair_cols(pair, 1)] = dkey.astype(BF)
+        out_ref[seen, pair_cols(pair, 2)] = dvalue.astype(BF)
+        return
+    if t == tiles - 1:
+        accs[0][...] = dkey
+        accs[1][...] = dvalue
+    else:
+        accs[0][pl.ds(0, (t + 1) * TILE), :] += dkey
+        accs[1][pl.ds(0, (t + 1) * TILE), :] += dvalue
+    if t == 0:
         out_ref[:, pair_cols(pair, 1)] = accs[0][...].astype(BF)
         out_ref[:, pair_cols(pair, 2)] = accs[1][...].astype(BF)
 
 
-def attn_bwd_kernel(tiles, packed_ref, probs_ref, grad_ref, out_ref, key_acc, value_acc):
+def attn_bwd_kernel(tiles, swapped, packed_ref, probs_ref, grad_ref, *refs):
+    copies = []
+    if swapped:
+        src_ref, out_ref, dst_ref, *accs, sems, local_sem = refs
+        copies = start_swap(False, src_ref, dst_ref, sems, local_sem)
+    else:
+        out_ref, *accs = refs
+
     def one_pair(pair, carry):
-        attn_bwd_pair(
-            0, tiles, pair, packed_ref, probs_ref, grad_ref, out_ref, (key_acc, value_acc)
-        )
+        for t in reversed(range(tiles)):
+            attn_bwd_tile(t, tiles, pair, packed_ref, probs_ref, grad_ref, out_ref, accs)
         return carry
 
     lax.fori_loop(0, PAIRS, one_pair, 0, unroll=2)
+    for copy in copies:
+        copy.wait()
 
 
 def blocks(rows, span):
@@ -163,6 +230,20 @@
         "col": pl.BlockSpec((span, 1), lambda t: (t, 0)),
         "row": pl.BlockSpec((1, span), lambda t: (0, t)),
     }
+
+
+def swap_parts(swap, to_all):
+    if swap is None:
+        return [], [], [], {}
+    size = lax.axis_size("tm")
+    dma = pltpu.SemaphoreType.DMA
+    shape = swapped_shape(to_all, swap, size)
+    return (
+        [swap],
+        [jax.ShapeDtypeStruct(shape, swap.dtype)],
+        [dma((size, 2)), dma(())],
+        {"collective_id": 4 + to_all, "has_side_effects": True},
+    )
 
 
 def attention(packed, span, groups=None):
@@ -182,7 +263,7 @@
         ],
         compiler_params=pltpu.CompilerParams(vmem_limit_bytes=48 * 2**20),
         cost_estimate=pl.CostEstimate(
-            flops=8 * HEADS * rows * span * HEAD_DIM,
+            flops=80 * HEADS * rows * span * HEAD_DIM,
             bytes_accessed=rows * (8 * MODEL + 2 * HEADS * span),
             transcendentals=HEADS * rows * span,
         ),
@@ -190,24 +271,177 @@
     )(packed, *extra)
 
 
-def attention_back(packed, probs, grad, span):
+def attention_back(packed, probs, grad, span, swap=None):
     rows = packed.shape[0]
     at = blocks(rows, span)
-    return pl.pallas_call(
-        lambda *refs: attn_bwd_kernel(span // TILE, *refs),
+    apart = swap if swap is not None and lax.axis_size("tm") != 8 else None
+    more, outs, scratch, parameters = swap_parts(None if apart is not None else swap, False)
+    anywhere = pl.BlockSpec(memory_space=pl.ANY)
+    result = pl.pallas_call(
+        lambda *refs: attn_bwd_kernel(span // TILE, bool(more), *refs),
         grid=(rows // span,),
-        in_specs=[at["packed"], at["probs"], at["mixed"]],
-        out_specs=at["packed"],
-        out_shape=jax.ShapeDtypeStruct((rows, 3 * MODEL), BF),
-        scratch_shapes=[pltpu.VMEM((span, PAIR), F32), pltpu.VMEM((span, PAIR), F32)],
-        compiler_params=pltpu.CompilerParams(vmem_limit_bytes=48 * 2**20),
+        in_specs=[at["packed"], at["probs"], at["mixed"]] + [anywhere] * len(more),
+        out_specs=[at["packed"]] + [anywhere] * len(outs),
+        out_shape=[jax.ShapeDtypeStruct((rows, 3 * MODEL), BF)] + outs,
+        scratch_shapes=[pltpu.VMEM((span, PAIR), F32), pltpu.VMEM((span, PAIR), F32)] + scratch,
+        compiler_params=pltpu.CompilerParams(vmem_limit_bytes=48 * 2**20, **parameters),
         cost_estimate=pl.CostEstimate(
-            flops=16 * HEADS * rows * span * HEAD_DIM,
+            flops=90 * HEADS * rows * span * HEAD_DIM,
             bytes_accessed=rows * (14 * MODEL + 2 * HEADS * span),
             transcendentals=0,
         ),
         name="attention_backward",
-    )(packed, probs, grad)
+    )(packed, probs, grad, *more)
+    if apart is not None:
+        return [*result, swap_plain(False, apart)]
+    return result if swap is not None else result[0]
+
+
+def back_norm_rows(grad, weight_ref, values, carried, gain):
+    back = dot_nt(grad, weight_ref[...])
+    centred = values - jnp.mean(values, axis=1, keepdims=True)
+    spread = jnp.mean(centred * centred, axis=1, keepdims=True)
+    scale = lax.rsqrt(spread + EPSILON)
+    unit = centred * scale
+    along = back * gain
+    level = jnp.mean(along, axis=1, keepdims=True)
+    slope = jnp.mean(along * unit, axis=1, keepdims=True)
+    result = carried + scale * (along - level - unit * slope)
+    sums = (jnp.sum(back * unit, axis=0, keepdims=True), jnp.sum(back, axis=0, keepdims=True))
+    return result, sums
+
+
+def back_norm_kernel(grad_ref, weight_ref, value_ref, carried_ref, gain_ref, out_ref, sum_ref):
+    result, sums = back_norm_rows(
+        grad_ref[...],
+        weight_ref,
+        value_ref[...].astype(F32),
+        carried_ref[...].astype(F32),
+        gain_ref[...],
+    )
+    out_ref[...] = result.astype(BF)
+
+    @pl.when(pl.program_id(0) == 0)
+    def _():
+        sum_ref[...] = jnp.zeros_like(sum_ref)
+
+    for i in range(2):
+        sum_ref[i : i + 1, :] += sums[i]
+
+
+def back_norm(grad, weight, values, carried, gain):
+    rows, width = values.shape
+    tile = min(rows, TILE)
+
+    def by_rows(columns):
+        return pl.BlockSpec((tile, columns), lambda i: (i, 0))
+
+    def whole(*shape):
+        return pl.BlockSpec(shape, lambda i: (0, 0))
+
+    return pl.pallas_call(
+        back_norm_kernel,
+        grid=(rows // tile,),
+        in_specs=[
+            by_rows(grad.shape[1]),
+            whole(*weight.shape),
+            by_rows(width),
+            by_rows(width),
+            whole(1, width),
+        ],
+        out_specs=[by_rows(width), whole(2, width)],
+        out_shape=[
+            jax.ShapeDtypeStruct((rows, width), BF),
+            jax.ShapeDtypeStruct((2, width), F32),
+        ],
+        compiler_params=pltpu.CompilerParams(vmem_limit_bytes=40 * 2**20),
+        cost_estimate=pl.CostEstimate(
+            flops=2 * rows * width * grad.shape[1],
+            bytes_accessed=2 * grad.shape[1] * (rows + width),
+            transcendentals=0,
+        ),
+        name="back_norm",
+    )(grad, weight, values, carried, gain[None])
+
+
+def act_kernel(normed_ref, weight_ref, bias_ref, act_ref, turned_ref, slope_ref):
+    hidden = dot_nn(normed_ref[...], weight_ref[...]) + bias_ref[...]
+    root, cubic = math.sqrt(2.0 / math.pi), 0.044715
+    square = hidden * hidden
+    tanh = jnp.tanh(root * hidden * (1.0 + cubic * square))
+    half = 0.5 + 0.5 * tanh
+    act = (hidden * half).astype(BF)
+    act_ref[...] = act
+    turned_ref[...] = act.T
+    slope_ref[...] = (
+        half + (0.5 * root) * hidden * (1.0 - tanh * tanh) * (1.0 + 3.0 * cubic * square)
+    ).astype(BF)
+
+
+def activate(normed, weight, bias):
+    rows, units = normed.shape[0], weight.shape[1]
+    tile = 512
+    return pl.pallas_call(
+        act_kernel,
+        grid=(units // tile,),
+        in_specs=[
+            pl.BlockSpec(normed.shape, lambda j: (0, 0)),
+            pl.BlockSpec((weight.shape[0], tile), lambda j: (0, j)),
+            pl.BlockSpec((1, tile), lambda j: (0, j)),
+        ],
+        out_specs=[
+            pl.BlockSpec((rows, tile), lambda j: (0, j)),
+            pl.BlockSpec((tile, rows), lambda j: (j, 0)),
+            pl.BlockSpec((rows, tile), lambda j: (0, j)),
+        ],
+        out_shape=[
+            pltpu.HBM((rows, units), BF),
+            pltpu.HBM((units, rows), BF),
+            pltpu.HBM((rows, units), BF),
+        ],
+        compiler_params=pltpu.CompilerParams(vmem_limit_bytes=24 * 2**20),
+        cost_estimate=pl.CostEstimate(
+            flops=2 * rows * units * weight.shape[0],
+            bytes_accessed=2 * units * (3 * rows + weight.shape[0]),
+            transcendentals=rows * units,
+        ),
+        name="activate",
+    )(normed, weight, bias[None])
+
+
+def back_act_kernel(grad_ref, weight_ref, slope_ref, out_ref, sum_ref):
+    back = (dot_nt(grad_ref[...], weight_ref[...]) * slope_ref[...].astype(F32)).astype(BF)
+    out_ref[...] = back
+    sum_ref[...] = jnp.sum(back.astype(F32), axis=0, keepdims=True)
+
+
+def back_act(grad, weight, slope):
+    rows, units = slope.shape
+    tile = 512
+    return pl.pallas_call(
+        back_act_kernel,
+        grid=(units // tile,),
+        in_specs=[
+            pl.BlockSpec(grad.shape, lambda j: (0, 0)),
+            pl.BlockSpec((tile, grad.shape[1]), lambda j: (j, 0)),
+            pl.BlockSpec((rows, tile), lambda j: (0, j)),
+        ],
+        out_specs=[
+            pl.BlockSpec((rows, tile), lambda j: (0, j)),
+            pl.BlockSpec((1, tile), lambda j: (0, j)),
+        ],
+        out_shape=[
+            jax.ShapeDtypeStruct((rows, units), BF),
+            jax.ShapeDtypeStruct((1, units), F32),
+        ],
+        compiler_params=pltpu.CompilerParams(vmem_limit_bytes=24 * 2**20),
+        cost_estimate=pl.CostEstimate(
+            flops=2 * rows * units * grad.shape[1],
+            bytes_accessed=2 * units * (2 * rows + grad.shape[1]),
+            transcendentals=0,
+        ),
+        name="back_act",
+    )(grad, weight, slope)
 
 
 def hop(block, axis, flip):
@@ -277,7 +511,7 @@
     return pl.pallas_call(
         lambda *refs: lay_kernel(rows, places, splits, *refs),
         in_specs=[pl.BlockSpec(memory_space=pl.ANY)] * len(parts),
-        out_specs=[pl.BlockSpec(memory_space=pl.ANY)] * len(splits),
+        out_specs=[pl.BlockSpec(memory_space=pltpu.HBM)] * len(splits),
         out_shape=[jax.ShapeDtypeStruct((8 * rows, n), block.dtype) for n in splits],
         scratch_shapes=[pltpu.VMEM(part.shape, part.dtype) for part in parts]
         + [
@@ -403,10 +637,9 @@
     first, second, smalls, whole_frames = pl.pallas_call(
         first_kernel,
         in_specs=[pl.BlockSpec(memory_space=pltpu.VMEM)] * 4,
-        out_specs=[pl.BlockSpec(memory_space=pl.ANY)] * 4,
+        out_specs=[pl.BlockSpec(memory_space=pltpu.HBM)] * 4,
         out_shape=[
-            jax.ShapeDtypeStruct((8 * weight.shape[0], weight.shape[1]), weight.dtype)
-            for weight in weights
+            pltpu.HBM((8 * weight.shape[0], weight.shape[1]), weight.dtype) for weight in weights
         ]
         + [
             jax.ShapeDtypeStruct((8,) + small.shape, small.dtype),
@@ -431,13 +664,33 @@
 
 UNIT = 128
 WIDE = 256
+ORDERS = ((3, 7, 1, 5), (5, 7, 1, 3), (2, 6, 0, 4), (4, 6, 0, 2))
+
+
+OPERANDS = (
+    "act_turned",
+    "out_low",
+    "normed_three",
+    "grad_pre",
+    "packed",
+    "grad_mixed",
+    "normed_two",
+    "grad_packed_two",
+    "time_mixed",
+    "time_branch",
+    "weight",
+    "inputs",
+    "branch",
+    "space_mixed",
+    "normed_one",
+    "small",
+)
 SLOTS = 6
 FINALS = 10
 DELAYS = (0, 1, 3, 5, 7, 9, 11, 13)
-ORDERS = ((3, 7, 1, 5), (5, 7, 1, 3), (2, 6, 0, 4), (4, 6, 0, 2))
-
-
-def reduce_kernel(chunks, places, with_small, units, *refs):
+
+
+def last_kernel(chunks, places, *refs):
     refs = list(refs)
 
     def take(count):
@@ -445,18 +698,36 @@
         del refs[:count]
         return taken
 
-    lefts, rights = take(chunks), take(chunks)
-    small_ref = take(1)[0] if with_small else None
-    packed_ref, probs_ref, grad_ref = take(3) if units else (None,) * 3
-    out_refs = take(chunks)
-    small_out = take(1)[0] if with_small else None
-    packed_out = take(1)[0] if units else None
+    count = len(OPERANDS)
+    far_off = dict(zip(OPERANDS, take(count)))
+    probs_ref, embedded_ref, gain_ref, one_hot_ref = take(4)
+    out_refs, small_out, frames_out = take(len(chunks)), take(1)[0], take(1)[0]
+    near = dict(zip(OPERANDS, take(count)))
+    (grad_packed, turned, lines, kept, probs_near) = take(5)
     (far, own, from_core, from_chip, from_owner, share, from_space, from_row, final) = take(9)
     (core_sem, chip_sem, owner_sem, space_sem, row_sem, back_sem, last_sem) = take(7)
-    turned = take(len(refs))
+    load_sem, probs_sem, frame_sem = take(3)
     me, side, level = lax.axis_index("tm"), lax.axis_index("space"), lax.axis_index("row")
     total = len(places)
     r = UNIT
+    frames = grad_packed.shape[0] // TILE
+    units = frames * PAIRS
+
+    loads = {
+        name: pltpu.make_async_copy(far_off[name], near[name], load_sem.at[i])
+        for i, name in enumerate(OPERANDS)
+    }
+    for name in OPERANDS:
+        loads[name].start()
+    waited = set()
+
+    def here(name):
+        if name == "grad_packed_one":
+            return grad_packed
+        if name not in waited:
+            waited.add(name)
+            loads[name].wait()
+        return near[name]
 
     def tm_at(flip):
         return {"tm": me ^ flip}
@@ -480,29 +751,25 @@
 
     cores, chips, owners, spaces, rows, backs, lasts = ({} for _ in range(7))
 
-    def buffer_of(which):
-        wide = lefts[which].shape[1] > 8 * UNIT
-        return turned[1] if wide else turned[0]
-
     def part(t, h, order):
         which, row, column, half = places[t]
-        if which == chunks:
-            return jnp.concatenate([small_ref[me ^ flip] for flip in order], axis=0)
-        rows_each = lefts[which].shape[1] // 8
+        if which == len(chunks):
+            return jnp.concatenate([lines[me ^ flip] for flip in order], axis=0)
+        left, right = chunks[which]
+        source = here(left) if left == "act_turned" else turned
+        rows_each = source.shape[0] // 8
         picked = [
-            buffer_of(which)[pl.ds(pl.multiple_of((me ^ flip) * rows_each + row, r), r), :]
-            for flip in order
+            source[pl.ds(pl.multiple_of((me ^ flip) * rows_each + row, r), r), :] for flip in order
         ]
         return dot_nn(
-            jnp.concatenate(picked, axis=0), rights[which][:, pl.ds(column + h * half, WIDE)]
-        )
-
-    mine = {}
+            jnp.concatenate(picked, axis=0), here(right)[:, pl.ds(column + h * half, WIDE)]
+        )
 
     def stage_core(t):
         which, slot = places[t][0], t % SLOTS
-        if which < chunks and (t == 0 or places[t - 1][0] != which):
-            buffer_of(which)[...] = lefts[which][...].T
+        if which < len(chunks) and (t == 0 or places[t - 1][0] != which):
+            if chunks[which][0] != "act_turned":
+                turned[...] = here(chunks[which][0])[...].T
         for h in range(2):
             if t >= SLOTS:
                 cores[t - SLOTS, h].wait_send()
@@ -569,10 +836,10 @@
     def stage_back(t):
         slot = t % SLOTS
         rows[t].wait_recv()
-        here = pl.ds(pl.multiple_of(level * (r // 2), r // 2), r // 2)
+        mine = pl.ds(pl.multiple_of(level * (r // 2), r // 2), r // 2)
         last = t % FINALS
-        final[last, side, here] = add_low(share[slot, side, here], from_row[slot])
-        place = final.at[last, side, here]
+        final[last, side, mine] = add_low(share[slot, side, mine], from_row[slot])
+        place = final.at[last, side, mine]
         backs[t] = start(place, place, back_sem.at[last], {"row": 1 - level})
 
     def stage_last(t):
@@ -585,15 +852,79 @@
         slot = t % FINALS
         lasts[t].wait_recv()
         out, row, column, half = places[t]
-        if out == chunks:
+        if out == len(chunks):
             small_out[...] = final[slot, 0].astype(F32)
         else:
             for h in range(2):
-                out_refs[out][pl.ds(row, r), pl.ds(column + h * half, WIDE)] = final[
-                    slot, h
-                ].astype(F32)
+                out_refs[out][pl.ds(row, r), pl.ds(column + h * half, WIDE)] = final[slot, h]
         backs[t].wait_send()
         lasts[t].wait_send()
+
+    def probs_copy(unit):
+        frame, pair = divmod(unit, PAIRS)
+        return pltpu.make_async_copy(
+            probs_ref.at[pl.ds(2 * pair, 2), pl.ds(frame * TILE, TILE), :],
+            probs_near.at[unit % 2],
+            probs_sem.at[unit % 2],
+        )
+
+    def attend(unit):
+        frame, pair = divmod(unit, PAIRS)
+        if unit + 1 < units:
+            probs_copy(unit + 1).start()
+        probs_copy(unit).wait()
+        attn_bwd_tile(
+            0,
+            1,
+            pair,
+            here("packed"),
+            None,
+            here("grad_mixed"),
+            grad_packed,
+            base=frame * TILE,
+            probs_pair=[probs_near[unit % 2, half] for half in range(2)],
+        )
+
+    def back_frame(frame):
+        some = pl.ds(frame * TILE, TILE)
+        values = here("inputs")[some, :].astype(F32) + embedded_ref[pl.ds(frame, 1), :]
+        result, sums = back_norm_rows(
+            grad_packed[some, :],
+            here("weight"),
+            values,
+            here("branch")[some, :].astype(F32),
+            gain_ref[...],
+        )
+        kept[frame] = result.astype(BF)
+        column = jnp.sum(result, axis=0, keepdims=True)
+        table = one_hot_ref[pl.ds(frame * ACTIONS, ACTIONS), :] * column
+        width = MODEL // 8
+        if frame == 0:
+            lines[...] = here("small")[...]
+        for k in range(8):
+            at = slice(k * width, (k + 1) * width)
+            lines[k, 0:ACTIONS, 0:width] += table[:, at]
+            lines[k, ACTIONS : ACTIONS + 1, 0:width] += sums[0][:, at]
+            lines[k, ACTIONS + 3 : ACTIONS + 4, 0:width] += sums[1][:, at]
+
+    exchanged = []
+
+    def exchange():
+        half_grid = kept.shape[1] // 2
+        own_frames = pl.ds(pl.multiple_of(side * frames, frames), frames)
+
+        def columns(which):
+            return pl.ds(pl.multiple_of(which * half_grid, half_grid), half_grid)
+
+        exchanged.append(
+            start(
+                kept.at[:, columns(1 - side), :],
+                frames_out.at[own_frames],
+                frame_sem,
+                {"space": 1 - side},
+            )
+        )
+        frames_out[own_frames] = kept[:, columns(side), :]
 
     stages = (
         stage_core,
@@ -605,13 +936,17 @@
         stage_last,
         stage_out,
     )
+    probs_copy(0).start()
     for step in range(total + DELAYS[-1]):
         for delay, stage in zip(DELAYS, stages):
             if 0 <= step - delay < total:
                 stage(step - delay)
         if 0 < step <= units:
-            frame, pair = divmod(step - 1, PAIRS)
-            attn_bwd_pair(frame * TILE, 1, pair, packed_ref, probs_ref, grad_ref, packed_out)
+            attend(step - 1)
+        elif 0 <= step - 1 - units < frames:
+            back_frame(step - 1 - units)
+        elif step == 1 + units + frames:
+            exchange()
     for t in range(max(0, total - SLOTS), total):
         for h in range(2):
             cores[t, h].wait_send()
@@ -619,50 +954,53 @@
             owners[t, h].wait_send()
         spaces[t].wait_send()
         rows[t].wait_send()
-
-
-def reduce_products(pairs, number, small=None, attend=None):
-    if lax.axis_size("tm") != 8:
-        result = []
-        for left, right in pairs:
-            whole = weight_grad(left, right).astype(BF)
-            block = lax.psum_scatter(whole, "tm", scatter_dimension=0, tiled=True)
-            result.append(lax.psum(block, ("row", "space")).astype(F32))
-        if small is not None:
-            block = lax.psum_scatter(small, "tm", scatter_dimension=0, tiled=True)[0]
-            result.append(lax.psum(block, ("row", "space")))
-        if attend is not None:
-            result.append(attention_back(*attend, TILE))
-        return result
+    exchanged[0].wait()
+
+
+CHUNKS = (
+    ("act_turned", "out_low"),
+    ("normed_three", "grad_pre"),
+    ("normed_two", "grad_packed_two"),
+    ("time_mixed", "time_branch"),
+    ("space_mixed", "branch"),
+    ("normed_one", "grad_packed_one"),
+)
+
+
+def last_stage(given, probs, embedded, gain, one_hot):
     places, shapes = [], []
-    for which, (left, right) in enumerate(pairs):
-        half = right.shape[1] // 2
-        shapes.append((left.shape[1] // 8, right.shape[1]))
-        for sub in range(left.shape[1] // (8 * UNIT)):
-            for j in range(half // WIDE):
-                places.append((which, sub * UNIT, j * WIDE, half))
-    operands = [left for left, _ in pairs] + [right for _, right in pairs]
-    outs = [jax.ShapeDtypeStruct(shape, F32) for shape in shapes]
-    if small is not None:
-        places.append((len(pairs), 0, 0, 0))
-        padding = ((0, 0), (0, UNIT - small.shape[1]), (0, WIDE - small.shape[2]))
-        operands.append(jnp.pad(small, padding))
-        outs.append(jax.ShapeDtypeStruct((UNIT, WIDE), F32))
-    units = 0
-    if attend is not None:
-        units = attend[0].shape[0] // TILE * PAIRS
-        operands += list(attend)
-        outs.append(jax.ShapeDtypeStruct(attend[0].shape, BF))
-    widths = sorted({left.shape[1] for left, _ in pairs})
-    tokens = pairs[0][0].shape[0]
+    for which, (left, right) in enumerate(CHUNKS):
+        width = given[left].shape[0 if left == "act_turned" else 1]
+        columns = 3 * MODEL if right == "grad_packed_one" else given[right].shape[1]
+        shapes.append((width // 8, columns))
+        for sub in range(width // (8 * UNIT)):
+            for j in range(columns // 2 // WIDE):
+                places.append((which, sub * UNIT, j * WIDE, columns // 2))
+    places.append((len(CHUNKS), 0, 0, 0))
+    small = given["small"]
+    padding = ((0, 0), (0, UNIT - small.shape[1]), (0, WIDE - small.shape[2]))
+    given = dict(given, small=jnp.pad(small, padding))
+    tokens = given["packed"].shape[0]
+    frames = tokens // TILE
     vmem = pltpu.VMEM
     dma = pltpu.SemaphoreType.DMA
+    in_vmem, anywhere = pl.BlockSpec(memory_space=pltpu.VMEM), pl.BlockSpec(memory_space=pl.ANY)
     result = pl.pallas_call(
-        lambda *refs: reduce_kernel(len(pairs), places, small is not None, units, *refs),
-        in_specs=[pl.BlockSpec(memory_space=pltpu.VMEM)] * len(operands),
-        out_specs=[pl.BlockSpec(memory_space=pltpu.VMEM)] * len(outs),
-        out_shape=outs,
-        scratch_shapes=[
+        lambda *refs: last_kernel(CHUNKS, places, *refs),
+        in_specs=[anywhere] * (len(OPERANDS) + 1) + [in_vmem] * 3,
+        out_specs=[in_vmem] * (len(shapes) + 2),
+        out_shape=[jax.ShapeDtypeStruct(shape, BF) for shape in shapes]
+        + [
+            jax.ShapeDtypeStruct((UNIT, WIDE), F32),
+            jax.ShapeDtypeStruct((2 * frames, TILE // 2, MODEL), BF),
+        ],
+        scratch_shapes=[vmem(given[name].shape, given[name].dtype) for name in OPERANDS]
+        + [
+            vmem((tokens, 3 * MODEL), BF),
+            vmem((MODEL, tokens), BF),
+            vmem((8, UNIT, WIDE), F32),
+            vmem((frames, TILE, MODEL), BF),
+            vmem((2, 2, TILE, TILE), BF),
             vmem((SLOTS, 2, 4 * UNIT, WIDE), BF),
             vmem((SLOTS, 2, 4 * UNIT, WIDE), BF),
             vmem((SLOTS, 2, 4 * UNIT, WIDE), BF),
@@ -679,20 +1017,48 @@
             dma((SLOTS, 2)),
             dma((FINALS, 2)),
             dma((FINALS, 2)),
-        ]
-        + [vmem((width, tokens), BF) for width in widths],
+            dma((len(OPERANDS),)),
+            dma((2,)),
+            dma((2,)),
+        ],
         compiler_params=pltpu.CompilerParams(
-            vmem_limit_bytes=58 * 2**20, collective_id=number, has_side_effects=True
+            vmem_limit_bytes=60 * 2**20, collective_id=1, has_side_effects=True
         ),
         cost_estimate=pl.CostEstimate(
             flops=1024, bytes_accessed=len(places) * 8 * UNIT * WIDE, transcendentals=0
         ),
-        name="reduce_products",
-    )(*operands)
-    if small is not None:
-        result = list(result)
-        result[len(pairs)] = result[len(pairs)][: small.shape[1], : small.shape[2]]
-    return result
+        name="last_stage",
+    )(*[given[name] for name in OPERANDS], probs, embedded, gain[None], one_hot)
+    grads = [grad.astype(F32) for grad in result[: len(shapes)]]
+    return grads, result[-2][: small.shape[1], : small.shape[2]], result[-1]
+
+
+def last_stage_plain(given, probs, embedded, gain, one_hot):
+    tokens = given["packed"].shape[0]
+    frames = tokens // TILE
+    grad_packed = attention_back(given["packed"], probs, given["grad_mixed"], TILE)
+    values = given["inputs"].astype(F32) + jnp.repeat(embedded, TILE, axis=0)
+    result, sums = back_norm(grad_packed, given["weight"], values, given["branch"], gain)
+    given = dict(given, grad_packed_one=grad_packed, act_turned=given["act_turned"].T)
+    grads = []
+    for left, right in CHUNKS:
+        whole = weight_grad(given[left], given[right]).astype(BF)
+        block = lax.psum_scatter(whole, "tm", scatter_dimension=0, tiled=True)
+        grads.append(lax.psum(block, ("row", "space")).astype(F32))
+    by_frame = jnp.sum(result.reshape(frames, TILE, MODEL).astype(F32), axis=1)
+    table = jnp.dot(
+        one_hot.reshape(frames, ACTIONS).T, by_frame, precision=lax.Precision.HIGHEST
+    )
+    none = jnp.zeros((2, MODEL), F32)
+    rows = jnp.concatenate((table, sums[:1], none, sums[1:], none))
+    size = lax.axis_size("tm")
+    more = rows.reshape(-1, size, MODEL // size).transpose(1, 0, 2)
+    small = given["small"].at[:, : more.shape[1]].add(more)
+    block = lax.psum_scatter(small, "tm", scatter_dimension=0, tiled=True)[0]
+    exchanged = lax.all_to_all(
+        result.reshape(frames, TILE, MODEL), "space", 1, 0, tiled=True
+    )
+    return grads, lax.psum(block, ("row", "space")), exchanged
 
 
 def body(
@@ -743,69 +1109,78 @@
     one_hot = (actions[:, None] == jnp.arange(ACTIONS)[None, :]).astype(BF)
     embedded = forward_dot(one_hot, table_full)
 
-    blocks_in = [jnp.concatenate((time_qkv, time_out), axis=1), ffn_in, ffn_out]
-    came, passed = [], []
-    for i, block in enumerate(blocks_in):
-        if tm == 8:
-            earlier = (passed[0] if i == 1 else came[1]) if i else (space_out_w,)
-            blocks_in[i] = after(block, *earlier)
-        came.append(first_hops(blocks_in[i]))
-        passed.append(second_hops(came[i]))
-    split = ((3 * MODEL, MODEL), (ffn_in.shape[1],), (MODEL,))
-    gathered = [gather_rows(*all_of) for all_of in zip(blocks_in, came, passed, split)]
-    time_in_w, time_out_w = gathered[0]
-    (ffn_in_w,), (ffn_out_w,) = gathered[1:]
-    if passed[1] is not None:
-        out_grad = after(out_grad, *passed[1])
+    time_block = jnp.concatenate((time_qkv, time_out), axis=1)
+    if tm == 8:
+        time_block = after(time_block, space_out_w)
+    time_came = first_hops(time_block)
 
     hidden_zero = (inputs.astype(F32) + embedded[:, None, :]).reshape(rows_dev, MODEL)
     normed_one = layer_norm(hidden_zero, gains[0], shifts[0]).astype(BF)
     packed_one = forward_dot(normed_one, space_in_w).astype(BF)
     space_mixed, space_probs = attention(packed_one, grid_all)
+    if tm == 8:
+        space_mixed, *time_came = lax.optimization_barrier((space_mixed, *time_came))
+    time_passed = second_hops(time_came)
+    time_in_w, time_out_w = gather_rows(time_block, time_came, time_passed, (3 * MODEL, MODEL))
+    in_block = after(ffn_in, *time_passed) if tm == 8 else ffn_in
+    in_came = first_hops(in_block)
     hidden_one_own = (hidden_zero + forward_dot(space_mixed, space_out_w)).astype(BF)
 
     sent = hidden_one_own.reshape(own_frames, halves * tm, cut, MODEL)
     blocks_t = lax.all_to_all(sent, ("space", "tm"), 1, 0)
-    hidden_one = lax.optimization_barrier(
+    hidden_one_low = lax.optimization_barrier(
         blocks_t.reshape(halves, tm, own_frames, cut, MODEL)
         .transpose(1, 0, 2, 3, 4)
         .reshape(rows_dev, MODEL)
-    ).astype(F32)
-    grad_out_low = lax.all_to_all(out_grad[0], "tm", 1, 0, tiled=True).reshape(rows_dev, MODEL)
-    grad_out = grad_out_low.astype(F32)
+    )
+    hidden_one = hidden_one_low.astype(F32)
     groups = (
         frame_segment[0].astype(jnp.int32)[:, None] * cut + jnp.arange(cut, dtype=jnp.int32)
     ).reshape(rows_dev)
 
     normed_two = layer_norm(hidden_one, gains[1], shifts[1]).astype(BF)
     packed_two = forward_dot(normed_two, time_in_w).astype(BF)
-    if came[1] is not None:
-        packed_two = after(packed_two, *came[1])
+    if tm == 8:
+        packed_two, out_grad, *in_came = lax.optimization_barrier(
+            (packed_two, out_grad, *in_came)
+        )
+    in_passed = second_hops(in_came)
+    grad_out_low = swap_plain(True, out_grad[0])
     time_mixed, time_probs = attention(packed_two, rows_dev, groups)
+    out_block = ffn_out
+    if tm == 8:
+        time_mixed, grad_out_low, out_block, *in_passed = lax.optimization_barrier(
+            (time_mixed, grad_out_low, ffn_out, *in_passed)
+        )
+    grad_out_low = grad_out_low.reshape(rows_dev, MODEL)
+    grad_out = grad_out_low.astype(F32)
+    out_came = first_hops(out_block)
+    (ffn_in_w,) = gather_rows(in_block, in_came, in_passed, (ffn_in.shape[1],))
     hidden_two = hidden_one + forward_dot(time_mixed, time_out_w)
     normed_three = layer_norm(hidden_two, gains[2], shifts[2]).astype(BF)
-    pre_act = forward_dot(normed_three, ffn_in_w) + bias_in
-    activated, gelu_pull = jax.vjp(jax.nn.gelu, pre_act)
-    act_low, slope = lax.optimization_barrier(
-        (activated.astype(BF), gelu_pull(jnp.ones_like(pre_act))[0].astype(BF))
-    )
+    act_low, act_turned, slope = activate(normed_three, ffn_in_w, bias_in)
+    if tm == 8:
+        slope, *out_came = lax.optimization_barrier((slope, *out_came))
+    (ffn_out_w,) = gather_rows(out_block, out_came, second_hops(out_came), (MODEL,))
+    bias_out_grad = jnp.sum(grad_out, axis=0)
+    grad_pre_low, bias_in_grad = back_act(grad_out_low, ffn_out_w, slope)
+    bias_in_grad = bias_in_grad[0]
+    time_branch, sums_three = back_norm(
+        grad_pre_low, ffn_in_w, hidden_two, grad_out_low, gains[2]
+    )
+    time_grad_mixed = back_dot(time_branch, time_out_w).astype(BF)
     block_out = (hidden_two + forward_dot(act_low, ffn_out_w) + bias_out).astype(BF)
-    block_output = lax.all_to_all(
-        block_out.reshape(all_frames, cut, MODEL), "tm", 0, 1, tiled=True
-    )[None]
-
-    bias_out_grad = jnp.sum(grad_out, axis=0)
-    grad_pre_low = (back_dot(grad_out_low, ffn_out_w) * slope.astype(F32)).astype(BF)
-    bias_in_grad = jnp.sum(grad_pre_low.astype(F32), axis=0)
-    norm_pull = jax.vjp(layer_norm, hidden_two, gains[2], shifts[2])[1]
-    grad_hidden, gain_three, shift_three = norm_pull(back_dot(grad_pre_low, ffn_in_w))
-    grad_two = grad_out + grad_hidden
-    time_branch = grad_two.astype(BF)
-    time_grad_mixed = back_dot(time_branch, time_out_w).astype(BF)
-    grad_packed_two = attention_back(packed_two, time_probs, time_grad_mixed, rows_dev)
-    norm_pull = jax.vjp(layer_norm, hidden_one, gains[1], shifts[1])[1]
-    grad_hidden, gain_two, shift_two = norm_pull(back_dot(grad_packed_two, time_in_w))
-    grad_one_low = (grad_two + grad_hidden).astype(BF)
+    grad_packed_two, block_output = attention_back(
+        packed_two,
+        time_probs,
+        time_grad_mixed,
+        rows_dev,
+        swap=block_out.reshape(all_frames, cut, MODEL),
+    )
+    block_output = block_output[None]
+    grad_one_low, sums_two = back_norm(
+        grad_packed_two, time_in_w, hidden_one_low, time_branch, gains[1]
+    )
 
     sent = (
         grad_one_low.reshape(tm, halves, own_frames, cut, MODEL)
@@ -814,31 +1189,15 @@
     )
     space_branch = lax.all_to_all(sent, ("space", "tm"), 0, 1).reshape(rows_dev, MODEL)
     space_grad_mixed = back_dot(space_branch, space_out_w).astype(BF)
-    ffn_out_grad, ffn_in_grad, time_qkv_grad, time_out_grad, grad_packed_one = reduce_products(
-        (
-            (act_low, grad_out_low),
-            (normed_three, grad_pre_low),
-            (normed_two, grad_packed_two),
-            (time_mixed, time_branch),
-        ),
-        1,
-        attend=(packed_one, space_probs, space_grad_mixed),
-    )
-    norm_pull = jax.vjp(layer_norm, hidden_zero, gains[0], shifts[0])[1]
-    grad_hidden, gain_one, shift_one = norm_pull(back_dot(grad_packed_one, space_in_w))
-    grad_zero = space_branch.astype(F32) + grad_hidden
-    frame_grad = jnp.sum(grad_zero.reshape(own_frames, grid_all, MODEL), axis=1)
-    action_grad = jnp.dot(one_hot.astype(F32).T, frame_grad, precision=lax.Precision.HIGHEST)
-    input_grad = lax.all_to_all(
-        grad_zero.astype(BF).reshape(own_frames, grid_all, MODEL), "space", 1, 0, tiled=True
-    ).astype(F32)[None]
-
+    none = jnp.zeros((1, MODEL), F32)
     by_row = jnp.concatenate(
-        (
-            action_grad,
-            jnp.stack((gain_one, gain_two, gain_three, shift_one, shift_two, shift_three)),
-            bias_out_grad[None],
-        )
+        [jnp.zeros((ACTIONS, MODEL), F32)]
+        + [
+            row
+            for i in range(2)
+            for row in (none, sums_two[i : i + 1], sums_three[i : i + 1])
+        ]
+        + [bias_out_grad[None]]
     )
     shares = jnp.concatenate(
         (
@@ -847,9 +1206,30 @@
         ),
         axis=1,
     )
-    space_out_grad, space_qkv_grad, small_grads = reduce_products(
-        ((space_mixed, space_branch), (normed_one, grad_packed_one)), 2, small=shares
-    )
+    given = {
+        "act_turned": act_turned,
+        "out_low": grad_out_low,
+        "normed_three": normed_three,
+        "grad_pre": grad_pre_low,
+        "packed": packed_one,
+        "grad_mixed": space_grad_mixed,
+        "normed_two": normed_two,
+        "grad_packed_two": grad_packed_two,
+        "time_mixed": time_mixed,
+        "time_branch": time_branch,
+        "weight": space_in_w,
+        "inputs": inputs.reshape(rows_dev, MODEL),
+        "branch": space_branch,
+        "space_mixed": space_mixed,
+        "normed_one": normed_one,
+        "small": shares,
+    }
+    finish = last_stage if tm == 8 else last_stage_plain
+    grads, small_grads, frames_grad = finish(
+        given, space_probs, embedded, gains[0], one_hot.astype(F32).reshape(-1, 1)
+    )
+    ffn_out_grad, ffn_in_grad, time_qkv_grad, time_out_grad, space_out_grad, space_qkv_grad = grads
+    input_grad = frames_grad.astype(F32)[None]
     return (
         block_output,
         input_grad,

time: 558 us -> 517 us (0.927)
  matrix products: 66.2 us -> 21.4 us
  waiting for transfers between devices: 60.4 us -> 71.5 us
  starting transfers between devices: 40.9 us -> 30.3 us
  local copies, waits for them, and re-layouts: 47 us -> 39.1 us
  Pallas kernels: 321 us -> 328 us
    dot_general x6 -> x2, matrix products: 33.8 us -> 4.53 us  [back_dot(): lax.dot_general(grad_rows, weight, (((1,), (1,)), ((), ())), preferred_el...]
    dot_general x7 -> x6, matrix products: 32.1 us -> 16.9 us  [forward_dot(): return jnp.dot(values, weight, preferred_element_type=F32)]
    all_to_all x3 -> x1, starting transfers between devices: 13.9 us -> 4.72 us  [swap_plain(): return lax.all_to_all(block, 'tm', split, concat, tiled=True)]
    all_to_all x1, waiting for transfers between devices: 6.08 us -> 13.9 us  [body(): lax.all_to_all(sent, ('space', 'tm'), 0, 1).reshape(rows_dev, MODEL)]
    pallas_call x3 -> x6, Pallas kernels: 244 us -> 251 us  [the longest x1 193 us: last_stage(): pl.pallas_call(lambda *refs: last_kernel(CHUNKS, places, *refs), in_specs...]
    unnamed x126 -> x89, local copies, waits for them, and re-layouts: 19.9 us -> 16.6 us
  transfers between devices with their start and end apart: 32 -> 30, of which waited for: 8 -> 18; matrix products, arithmetic and copies ran while one was open for 13% -> 5% of each run, Pallas kernels for 47% -> 9%
where the time goes in v4:
time: 517 us; the launch traced here: 508 us
  Pallas kernels  328 us (63%)
  waiting for transfers between devices  71.5 us (14%)
  local copies, waits for them, and re-layouts  39.1 us (8%)
  starting transfers between devices  30.3 us (6%)
  matrix products  21.4 us (4%)
  other arithmetic  16 us (3%)
    pallas_call x1, Pallas kernels, last_stage(): pl.pallas_call(lambda *refs: last_kernel(CHUNKS, places, *refs), in_specs...  193 us
    ppermute x27, waiting for transfers between devices, hop(): return lax.ppermute(block, axis, [(i, i ^ flip) for i in range(size)])  57.6 us
    pallas_call x1, Pallas kernels, first_gather(): pl.pallas_call(first_kernel, in_specs=[pl.BlockSpec(memory_space=pltpu.VM...  42.1 us
    pallas_call x2, Pallas kernels, attention(): pl.pallas_call(lambda *refs: attn_fwd_kernel(span // TILE, masked, *refs)...  26.3 us
    pallas_call x1, Pallas kernels, attention_back(): pl.pallas_call(lambda *refs: attn_bwd_kernel(span // TILE, bool(more), *r...  22.5 us
    dot_general x6, matrix products, forward_dot(): return jnp.dot(values, weight, preferred_element_type=F32)  16.9 us
    ppermute x27, starting transfers between devices, hop(): return lax.ppermute(block, axis, [(i, i ^ flip) for i in range(size)])  16.7 us
    unnamed x89, local copies, waits for them, and re-layouts  16.6 us
  transfers between devices with their start and end apart: 30, of which 18 were waited for; matrix products, arithmetic and copies ran while one was open for 5% of the time, Pallas kernels for 9%

profile of v4, /device:TPU:0, one launch (start us, length us, event | category | flops | bytes accessed | tf_op | source)
XLA Modules:
  0.0 508.0 jit_solution(7971389558163653724)
XLA Ops:
  0.7 2.3 concatenate.23
  4.5 42.1 %first_gather.1 = (bf16[1024,3072]{1,0:T(8,128)(2,1)}, bf16[1024,1024]{1,0:T(8,128)(2,1)}, bf16[8,32,128]{2,1,0:T(8,128)(2,1)S(1)}, bf16[2,256,1024]{2,1,0:T(8,128)(2,1)S(1)}) custom-call(bf16[128,3072]{1,0:T(8,128)(2,1)S(1)} %copy-done.15, bf16[128,1024]{1,0:T(8,128)(2,1)S(1)} %copy-done.16, bf16[32,128]{1,0:T(8,128)(2,1)S(1)} %pad.8.refs_2_, ...), custom_call_target="tpu_custom_call" | custom-call | bytes 16777216 | tf_op jit(solution)/shard_map/first_gather/pallas_call | solution.py:637
  52.5 3.6 convolution_convert_fusion.1.refs_0_.refs_4_
  56.2 10.4 %attention_forward.2 = (bf16[512,1024]{1,0:T(8,128)(2,1)S(1)}, bf16[16,512,256]{2,1,0:T(8,128)(2,1)}) custom-call(bf16[512,3072]{1,0:T(8,128)(2,1)S(1)} %convolution_convert_fusion.1.refs_0_.refs_4_), custom_call_target="tpu_custom_call" | custom-call | flops 10737418240 | bytes 8388608 | tf_op jit(solution)/shard_map/attention_forward/pallas_call | solution.py:255
  66.6 5.8 %collective-permute-done.refs_2_ = bf16[128,4096]{1,0:T(8,128)(2,1)} collective-permute-done((bf16[128,4096]{1,0:T(8,128)(2,1)S(1)}, bf16[128,4096]{1,0:T(8,128)(2,1)}, u32[]{:S(2)}, u32[]{:S(2)}) %collective-permute-start) | collective-permute-done | bytes 1048608 | tf_op jit(solution)/shard_map/ppermute | solution.py:449
  75.7 4.5 all-to-all-start
  86.2 19.5 %collective-permute-done.5.refs_6_ = bf16[64,4096]{1,0:T(8,128)(2,1)} collective-permute-done((bf16[64,4096]{1,0:T(8,128)(2,1)S(1)}, bf16[64,4096]{1,0:T(8,128)(2,1)}, u32[]{:S(2)}, u32[]{:S(2)}) %collective-permute-start.5) | collective-permute-done | bytes 524320 | tf_op jit(solution)/shard_map/ppermute | solution.py:449
  109.3 3.0 lay_rows.3
  112.3 2.7 copy-done.17
  119.4 5.0 convolution_convert_fusion.refs_0_
  124.4 9.0 %collective-permute-done.9.refs_2_ = bf16[128,4096]{1,0:T(8,128)(2,1)} collective-permute-done((bf16[128,4096]{1,0:T(8,128)(2,1)}, bf16[128,4096]{1,0:T(8,128)(2,1)}, u32[]{:S(2)}, u32[]{:S(2)}) %collective-permute-start.9) | collective-permute-done | bytes 1048608 | tf_op jit(solution)/shard_map/ppermute | solution.py:449
  139.5 4.7 all-to-all-start.1
  144.2 2.0 collective-permute-start.11
  149.6 16.0 %attention_forward.3 = (bf16[512,1024]{1,0:T(8,128)(2,1)S(1)}, bf16[16,512,512]{2,1,0:T(8,128)(2,1)}) custom-call(bf16[512,3072]{1,0:T(8,128)(2,1)S(1)} %copy-done.24, s32[512,1]{1,0:T(8,128)S(1)} %add.145.refs_1_, s32[1,512]{1,0:T(1,128)S(1)} %add.136.refs_2_), custom_call_target="tpu_custom_call" | custom-call | flops 21474836480 | bytes 12582912 | tf_op jit(solution)/shard_map/attention_forward/pallas_call | solution.py:255
  167.6 2.3 collective-permute-done.11.refs_6_
  176.6 3.3 lay_rows.4.weight_ref
  180.0 12.9 %activate.1 = (bf16[512,4096]{1,0:T(8,128)(2,1)}, bf16[4096,512]{1,0:T(8,128)(2,1)}, bf16[512,4096]{1,0:T(8,128)(2,1)}) custom-call(bf16[512,1024]{1,0:T(8,128)(2,1)S(1)} %add_convert_fusion.1.normed_ref.refs_2_, bf16[1024,4096]{1,0:T(8,128)(2,1)S(1)} %lay_rows.4.weight_ref, f32[1,4096]{1,0:T(1,128)S(1)} %bitcast.119), custom_call_target="tpu_custom_call" | custom-call | flops 4294967296 | bytes 20971520 | tf_op jit(solution)/shard_map/activate/pallas_call | solution.py:384
  192.9 2.1 collective-permute-done.19.refs_2_
  198.8 10.4 %collective-permute-done.23.refs_6_ = bf16[256,1024]{1,0:T(8,128)(2,1)S(1)} collective-permute-done((bf16[256,1024]{1,0:T(8,128)(2,1)S(1)}, bf16[256,1024]{1,0:T(8,128)(2,1)S(1)}, u32[]{:S(2)}, u32[]{:S(2)}) %collective-permute-start.23) | collective-permute-done | bytes 524320 | tf_op jit(solution)/shard_map/ppermute | solution.py:449
  211.9 2.0 lay_rows.5.weight_ref
  213.9 7.0 %back_act.1 = (bf16[512,4096]{1,0:T(8,128)(2,1)S(1)}, f32[1,4096]{1,0:T(1,128)S(1)}) custom-call(bf16[512,1024]{1,0:T(8,128)(2,1)S(1)} %bitcast.111, bf16[4096,1024]{1,0:T(8,128)(2,1)S(1)} %lay_rows.5.weight_ref, bf16[512,4096]{1,0:T(8,128)(2,1)S(1)} %copy-done.22), custom_call_target="tpu_custom_call" | custom-call | flops 4294967296 | bytes 16777216 | tf_op jit(solution)/shard_map/back_act/pallas_call | solution.py:421
  220.9 10.8 %back_norm.2 = (bf16[512,1024]{1,0:T(8,128)(2,1)S(1)}, f32[2,1024]{1,0:T(2,128)S(1)}) custom-call(bf16[512,4096]{1,0:T(8,128)(2,1)S(1)} %get-tuple-element.86.grad_ref.refs_3_, bf16[1024,4096]{1,0:T(8,128)(2,1)} %copy-done.4, f32[512,1024]{1,0:T(8,128)S(1)} %get-tuple-element.127.value_ref, bf16[512,1024]{1,0:T(8,128)(2,1)S(1)} %bitcast.112, ...), custom_call_target="tpu_custom_call" | custom-call | flops 4294967296 | bytes 12582912 | tf_op jit(solution)/shard_map/back_norm/pallas_call | solution.py:342
  231.8 2.3 convolution_convert_fusion.3.refs_2_
  234.7 5.5 %add_convert_fusion = bf16[512,1024]{1,0:T(8,128)(2,1)} fusion(f32[512,1024]{1,0:T(8,128)S(1)} %get-tuple-element.127.value_ref, bf16[512,4096]{1,0:T(8,128)(2,1)S(1)} %copy-done.40, bf16[4096,1024]{1,0:T(8,128)(2,1)S(1)} %lay_rows.5.weight_ref, f32[1024]{0:T(1024)S(1)} %bitcast.137), kind=kOutput, calls=%fused_computation.19 | convolution fusion | flops 4296540160 | bytes 15732736 | tf_op jit(solution)/shard_map/dot_general | solution.py:33
  242.7 22.5 %attention_backward.1 = (bf16[512,3072]{1,0:T(8,128)(2,1)}, bf16[4,128,1024]{2,1,0:T(8,128)(2,1)S(1)}) custom-call(bf16[512,3072]{1,0:T(8,128)(2,1)} %convolution_convert_fusion.refs_0_, bf16[16,512,512]{2,1,0:T(8,128)(2,1)} %get-tuple-element.71.refs_1_, bf16[512,1024]{1,0:T(8,128)(2,1)S(1)} %copy-done.23, bf16[32,16,1024]{2,1,0:T(8,128)(2,1)S(1)} %bitcast.122), custom_call_target="tpu_custom_call" | custom-call | flops 24159191040 | bytes 15728640 | tf_op jit(solution)/shard_map/attention_backward/pallas_call | solution.py:280
  265.2 2.2 copy-done.8
  267.4 4.8 back_norm.3
  273.3 4.4 all-to-all-start.2
  279.8 13.9 %all-to-all-done.2 = bf16[16,2,1,16,1024]{4,3,1,2,0:T(8,128)(2,1)S(1)} async-done(((bf16[16,2,1,16,1024]{4,3,1,2,0:T(8,128)(2,1)}), bf16[16,2,1,16,1024]{4,3,1,2,0:T(8,128)(2,1)S(1)}, u32[]{:S(2)}, u32[]{:S(2)}) %all-to-all-start.2) | async-done | bytes 1048608 | tf_op jit(solution)/shard_map/all_to_all | solution.py:1190
  295.7 2.3 convolution_convert_fusion.2.refs_5_
  297.9 193.2 %last_stage.1 = (bf16[512,1024]{1,0:T(8,128)(2,1)}, bf16[128,4096]{1,0:T(8,128)(2,1)}, bf16[128,3072]{1,0:T(8,128)(2,1)}, bf16[128,1024]{1,0:T(8,128)(2,1)}, bf1...) custom-call(bf16[4096,512]{1,0:T(8,128)(2,1)} %get-tuple-element.90.refs, ...), custom_call_target="tpu_custom_call" | custom-call | flops 1024 | bytes 8650752 | tf_op jit(solution)/shard_map/last_stage/pallas_call | solution.py:988
  496.3 2.8 bitcast_convert_fusion
  (197 shorter events, 71.2 us)
Async XLA Ops:
  0.6 48.1 %copy-start = (s32[1,4]{1,0:T(1,128)S(1)}, s32[1,4]{1,0:T(1,128)}, u32[]{:S(2)}) copy-start(s32[1,4]{1,0:T(1,128)} %param.29) | copy-start | bytes 52
  46.7 25.7 %collective-permute-start = (bf16[128,4096]{1,0:T(8,128)(2,1)S(1)}, bf16[128,4096]{1,0:T(8,128)(2,1)}, u32[]{:S(2)}, u32[]{:S(2)}) collective-permute-start(bf16[128,4096]{1,0:T(8,128)(2,1)S(1)} %pad_maximum_fusion.refs_0_), channel_id=1, source_target_pairs={{0,4},{2,6},{4,0},{6,2},{8,12},{10,14},{12,8},{14,10},{1,5},{3,7},... | collective-permute-start | bytes 3145736 | tf_op jit(solution)/shard_map/ppermute | solution.py:449
  48.0 25.3 %collective-permute-start.1 = (bf16[128,4096]{1,0:T(8,128)(2,1)S(1)}, bf16[128,4096]{1,0:T(8,128)(2,1)}, u32[]{:S(2)}, u32[]{:S(2)}) collective-permute-start(bf16[128,4096]{1,0:T(8,128)(2,1)S(1)} %pad_maximum_fusion.refs_0_), channel_id=1, source_target_pairs={{0,8},{2,10},{4,12},{6,14},{8,0},{10,2},{12,4},{14,6},{1,9},{3,11}... | collective-permute-start | bytes 3145736 | tf_op jit(solution)/shard_map/ppermute | solution.py:449
  75.7 40.6 %all-to-all-start = ((bf16[1,2,16,16,1024]{4,3,1,0,2:T(8,128)(2,1)}), bf16[1,2,16,16,1024]{4,3,1,0,2:T(8,128)(2,1)}, u32[]{:S(2)}, u32[]{:S(2)}) async-start(bf16[1,2,16,16,1024]{4,3,1,0,2:T(8,128)(2,1)} %copy.37), calls=%async_computation | async-start | bytes 2097152 | tf_op jit(solution)/shard_map/all_to_all | solution.py:1130
  81.2 24.5 %collective-permute-start.5 = (bf16[64,4096]{1,0:T(8,128)(2,1)S(1)}, bf16[64,4096]{1,0:T(8,128)(2,1)}, u32[]{:S(2)}, u32[]{:S(2)}) collective-permute-start(bf16[64,4096]{1,0:T(8,128)(2,1)S(1)} %slice.120), channel_id=1, source_target_pairs={{0,8},{2,10},{4,12},{6,14},{8,0},{10,2},{12,4},{14,6},{1,9},{3,11}... | collective-permute-start | bytes 1572872 | tf_op jit(solution)/shard_map/ppermute | solution.py:449
  84.1 22.9 %collective-permute-start.7 = (bf16[64,4096]{1,0:T(8,128)(2,1)S(1)}, bf16[64,4096]{1,0:T(8,128)(2,1)}, u32[]{:S(2)}, u32[]{:S(2)}) collective-permute-start(bf16[64,4096]{1,0:T(8,128)(2,1)S(1)} %slice.121), channel_id=1, source_target_pairs={{0,4},{2,6},{4,0},{6,2},{8,12},{10,14},{12,8},{14,10},{1,5},{3,7},... | collective-permute-start | bytes 1572872 | tf_op jit(solution)/shard_map/ppermute | solution.py:449
  85.7 21.7 %collective-permute-start.2 = (bf16[128,4096]{1,0:T(8,128)(2,1)S(1)}, bf16[128,4096]{1,0:T(8,128)(2,1)S(1)}, u32[]{:S(2)}, u32[]{:S(2)}) collective-permute-start(bf16[128,4096]{1,0:T(8,128)(2,1)S(1)} %pad_maximum_fusion.refs_0_), channel_id=1, source_target_pairs={{0,2},{2,0},{4,6},{6,4},{8,10},{10,8},{12,14},{14,12},{1,3},{3,1},... | collective-permute-start | bytes 3145736 | tf_op jit(solution)/shard_map/ppermute | solution.py:449
  85.7 22.4 %collective-permute-start.3 = (bf16[128,4096]{1,0:T(8,128)(2,1)}, bf16[128,4096]{1,0:T(8,128)(2,1)S(1)}, u32[]{:S(2)}, u32[]{:S(2)}) collective-permute-start(bf16[128,4096]{1,0:T(8,128)(2,1)} %collective-permute-done.refs_2_), channel_id=1, source_target_pairs={{0,2},{2,0},{4,6},{6,4},{8,10},{10,8},{12,14},{14,12},{1,3},{3,1},... | collective-permute-start | bytes 3145736 | tf_op jit(solution)/shard_map/ppermute | solution.py:449
  86.2 22.4 %collective-permute-start.4 = (bf16[128,4096]{1,0:T(8,128)(2,1)}, bf16[128,4096]{1,0:T(8,128)(2,1)}, u32[]{:S(2)}, u32[]{:S(2)}) collective-permute-start(bf16[128,4096]{1,0:T(8,128)(2,1)} %collective-permute-done.1.refs_4_), channel_id=1, source_target_pairs={{0,2},{2,0},{4,6},{6,4},{8,10},{10,8},{12,14},{14,12},{1,3},{3,1},... | collective-permute-start | bytes 3145736 | tf_op jit(solution)/shard_map/ppermute | solution.py:449
  105.7 2.9 collective-permute-start.6
  107.0 2.3 collective-permute-start.8
  107.4 26.0 %collective-permute-start.9 = (bf16[128,4096]{1,0:T(8,128)(2,1)}, bf16[128,4096]{1,0:T(8,128)(2,1)}, u32[]{:S(2)}, u32[]{:S(2)}) collective-permute-start(bf16[128,4096]{1,0:T(8,128)(2,1)} %refs_0_.2), channel_id=1, source_target_pairs={{0,4},{2,6},{4,0},{6,2},{8,12},{10,14},{12,8},{14,10},{1,5},{3,7},... | collective-permute-start | bytes 3145736 | tf_op jit(solution)/shard_map/ppermute | solution.py:449
  108.1 25.3 %collective-permute-start.10 = (bf16[128,4096]{1,0:T(8,128)(2,1)}, bf16[128,4096]{1,0:T(8,128)(2,1)}, u32[]{:S(2)}, u32[]{:S(2)}) collective-permute-start(bf16[128,4096]{1,0:T(8,128)(2,1)} %refs_0_.2), channel_id=1, source_target_pairs={{0,8},{2,10},{4,12},{6,14},{8,0},{10,2},{12,4},{14,6},{1,9},{3,11}... | collective-permute-start | bytes 3145736 | tf_op jit(solution)/shard_map/ppermute | solution.py:449
  108.6 65.1 %collective-permute-start.14 = (bf16[128,4096]{1,0:T(8,128)(2,1)}, bf16[128,4096]{1,0:T(8,128)(2,1)}, u32[]{:S(2)}, u32[]{:S(2)}) collective-permute-start(bf16[128,4096]{1,0:T(8,128)(2,1)} %refs_0_.2), channel_id=1, source_target_pairs={{0,2},{2,0},{4,6},{6,4},{8,10},{10,8},{12,14},{14,12},{1,3},{3,1},... | collective-permute-start | bytes 3145736 | tf_op jit(solution)/shard_map/ppermute | solution.py:449
  135.3 38.5 %collective-permute-start.15 = (bf16[128,4096]{1,0:T(8,128)(2,1)}, bf16[128,4096]{1,0:T(8,128)(2,1)}, u32[]{:S(2)}, u32[]{:S(2)}) collective-permute-start(bf16[128,4096]{1,0:T(8,128)(2,1)} %collective-permute-done.9.refs_2_), channel_id=1, source_target_pairs={{0,2},{2,0},{4,6},{6,4},{8,10},{10,8},{12,14},{14,12},{1,3},{3,1},... | collective-permute-start | bytes 3145736 | tf_op jit(solution)/shard_map/ppermute | solution.py:449
  137.2 37.6 %collective-permute-start.16 = (bf16[128,4096]{1,0:T(8,128)(2,1)}, bf16[128,4096]{1,0:T(8,128)(2,1)}, u32[]{:S(2)}, u32[]{:S(2)}) collective-permute-start(bf16[128,4096]{1,0:T(8,128)(2,1)} %collective-permute-done.10.refs_4_), channel_id=1, source_target_pairs={{0,2},{2,0},{4,6},{6,4},{8,10},{10,8},{12,14},{14,12},{1,3},{3,1},... | collective-permute-start | bytes 3145736 | tf_op jit(solution)/shard_map/ppermute | solution.py:449
  139.5 26.1 %all-to-all-start.1 = ((bf16[4,128,1024]{2,0,1:T(4,128)(2,1)}), bf16[4,128,1024]{2,0,1:T(4,128)(2,1)}, u32[]{:S(2)}, u32[]{:S(2)}) async-start(bf16[4,128,1024]{2,0,1:T(4,128)(2,1)} %bitcast.104), calls=%async_computation.1 | async-start | bytes 2097152 | tf_op jit(solution)/shard_map/all_to_all | solution.py:121
  144.2 25.7 %collective-permute-start.11 = (bf16[64,4096]{1,0:T(8,128)(2,1)}, bf16[64,4096]{1,0:T(8,128)(2,1)}, u32[]{:S(2)}, u32[]{:S(2)}) collective-permute-start(bf16[64,4096]{1,0:T(8,128)(2,1)} %slice.122), channel_id=1, source_target_pairs={{0,8},{2,10},{4,12},{6,14},{8,0},{10,2},{12,4},{14,6},{1,9},{3,11}... | collective-permute-start | bytes 1572872 | tf_op jit(solution)/shard_map/ppermute | solution.py:449
  146.2 23.7 %collective-permute-start.12 = (bf16[64,4096]{1,0:T(8,128)(2,1)}, bf16[64,4096]{1,0:T(8,128)(2,1)}, u32[]{:S(2)}, u32[]{:S(2)}) collective-permute-start(bf16[64,4096]{1,0:T(8,128)(2,1)} %slice.123), channel_id=1, source_target_pairs={{0,4},{2,6},{4,0},{6,2},{8,12},{10,14},{12,8},{14,10},{1,5},{3,7},... | collective-permute-start | bytes 1572872 | tf_op jit(solution)/shard_map/ppermute | solution.py:449
  167.6 110.9 %copy-start.3 = (bf16[8,4,16,1024]{3,2,1,0:T(8,128)(2,1)}, bf16[8,4,16,1024]{3,2,1,0:T(8,128)(2,1)S(1)}, u32[]{:S(2)}) copy-start(bf16[8,4,16,1024]{3,2,1,0:T(8,128)(2,1)S(1)} %copy.41) | copy-start | bytes 3145732
  170.0 25.0 %collective-permute-start.19 = (bf16[512,1024]{1,0:T(8,128)(2,1)}, bf16[512,1024]{1,0:T(8,128)(2,1)S(1)}, u32[]{:S(2)}, u32[]{:S(2)}) collective-permute-start(bf16[512,1024]{1,0:T(8,128)(2,1)} %refs_0_.3), channel_id=1, source_target_pairs={{0,4},{2,6},{4,0},{6,2},{8,12},{10,14},{12,8},{14,10},{1,5},{3,7},... | collective-permute-start | bytes 3145736 | tf_op jit(solution)/shard_map/ppermute | solution.py:449
  171.3 25.1 %collective-permute-start.20 = (bf16[512,1024]{1,0:T(8,128)(2,1)}, bf16[512,1024]{1,0:T(8,128)(2,1)S(1)}, u32[]{:S(2)}, u32[]{:S(2)}) collective-permute-start(bf16[512,1024]{1,0:T(8,128)(2,1)} %refs_0_.3), channel_id=1, source_target_pairs={{0,8},{2,10},{4,12},{6,14},{8,0},{10,2},{12,4},{14,6},{1,9},{3,11}... | collective-permute-start | bytes 3145736 | tf_op jit(solution)/shard_map/ppermute | solution.py:449
  173.7 2.2 collective-permute-start.17
  173.8 2.8 collective-permute-start.18
  174.7 35.0 %collective-permute-start.13 = (bf16[512,1024]{1,0:T(8,128)(2,1)}, bf16[512,1024]{1,0:T(8,128)(2,1)S(1)}, u32[]{:S(2)}, u32[]{:S(2)}) collective-permute-start(bf16[512,1024]{1,0:T(8,128)(2,1)} %refs_0_.3), channel_id=1, source_target_pairs={{0,2},{2,0},{4,6},{6,4},{8,10},{10,8},{12,14},{14,12},{1,3},{3,1},... | collective-permute-start | bytes 3145736 | tf_op jit(solution)/shard_map/ppermute | solution.py:449
  196.4 12.8 %collective-permute-start.23 = (bf16[256,1024]{1,0:T(8,128)(2,1)S(1)}, bf16[256,1024]{1,0:T(8,128)(2,1)S(1)}, u32[]{:S(2)}, u32[]{:S(2)}) collective-permute-start(bf16[256,1024]{1,0:T(8,128)(2,1)S(1)} %slice.127), channel_id=1, source_target_pairs={{0,8},{2,10},{4,12},{6,14},{8,0},{10,2},{12,4},{14,6},{1,9},{3,11}... | collective-permute-start | bytes 1572872 | tf_op jit(solution)/shard_map/ppermute | solution.py:449
  196.9 12.5 %collective-permute-start.25 = (bf16[256,1024]{1,0:T(8,128)(2,1)S(1)}, bf16[256,1024]{1,0:T(8,128)(2,1)S(1)}, u32[]{:S(2)}, u32[]{:S(2)}) collective-permute-start(bf16[256,1024]{1,0:T(8,128)(2,1)S(1)} %slice.128), channel_id=1, source_target_pairs={{0,4},{2,6},{4,0},{6,2},{8,12},{10,14},{12,8},{14,10},{1,5},{3,7},... | collective-permute-start | bytes 1572872 | tf_op jit(solution)/shard_map/ppermute | solution.py:449
  198.3 13.6 %collective-permute-start.21 = (bf16[512,1024]{1,0:T(8,128)(2,1)S(1)}, bf16[512,1024]{1,0:T(8,128)(2,1)S(1)}, u32[]{:S(2)}, u32[]{:S(2)}) collective-permute-start(bf16[512,1024]{1,0:T(8,128)(2,1)S(1)} %collective-permute-done.19.refs_2_), channel_id=1, source_target_pairs={{0,2},{2,0},{4,6},{6,4},{8,10},{10,8},{12,14},{14,12},{1,3},{3,1},... | collective-permute-start | bytes 3145736 | tf_op jit(solution)/shard_map/ppermute | solution.py:449
  198.3 13.6 %collective-permute-start.22 = (bf16[512,1024]{1,0:T(8,128)(2,1)S(1)}, bf16[512,1024]{1,0:T(8,128)(2,1)S(1)}, u32[]{:S(2)}, u32[]{:S(2)}) collective-permute-start(bf16[512,1024]{1,0:T(8,128)(2,1)S(1)} %collective-permute-done.20.refs_4_), channel_id=1, source_target_pairs={{0,2},{2,0},{4,6},{6,4},{8,10},{10,8},{12,14},{14,12},{1,3},{3,1},... | collective-permute-start | bytes 3145736 | tf_op jit(solution)/shard_map/ppermute | solution.py:449
  209.2 1.9 collective-permute-start.24
  209.4 2.5 collective-permute-start.26
  273.3 20.4 %all-to-all-start.2 = ((bf16[16,2,1,16,1024]{4,3,1,2,0:T(8,128)(2,1)}), bf16[16,2,1,16,1024]{4,3,1,2,0:T(8,128)(2,1)S(1)}, u32[]{:S(2)}, u32[]{:S(2)}) async-start(bf16[16,2,1,16,1024]{4,3,1,2,0:T(8,128)(2,1)} %bitcast.33), calls=%async_computation.2 | async-start | bytes 2097152 | tf_op jit(solution)/shard_map/all_to_all | solution.py:1190
  (41 other events, 292.3 us)

commit v5 on v4

--- a/solution.py
+++ b/solution.py
@@ -685,6 +685,7 @@
     "normed_one",
     "small",
 )
+SMALL_ROWS, SMALL_COLUMNS = 32, 128
 SLOTS = 6
 FINALS = 10
 DELAYS = (0, 1, 3, 5, 7, 9, 11, 13)
@@ -751,6 +752,13 @@
 
     cores, chips, owners, spaces, rows, backs, lasts = ({} for _ in range(7))
 
+    def size(t):
+        return (SMALL_ROWS, SMALL_COLUMNS) if places[t][0] == len(chunks) else (UNIT, WIDE)
+
+    def box(t, first, count=1):
+        each, wide = size(t)
+        return pl.ds(first * each, count * each), pl.ds(0, wide)
+
     def part(t, h, order):
         which, row, column, half = places[t]
         if which == len(chunks):
@@ -773,24 +781,30 @@
         for h in range(2):
             if t >= SLOTS:
                 cores[t - SLOTS, h].wait_send()
-            far[slot, h] = part(t, h, ORDERS[h]).astype(BF)
+            every = box(t, 0, 4)
+            far[(slot, h, *every)] = part(t, h, ORDERS[h]).astype(BF)
             cores[t, h] = start(
-                far.at[slot, h], from_core.at[slot, h], core_sem.at[slot, h], tm_at(1)
+                far.at[(slot, h, *every)],
+                from_core.at[(slot, h, *every)],
+                core_sem.at[slot, h],
+                tm_at(1),
             )
         for h in range(2):
             if t >= SLOTS:
                 chips[t - SLOTS, h].wait_send()
                 owners[t - SLOTS, h].wait_send()
-            own[slot, h] = part(t, h, ORDERS[2 + h]).astype(BF)
+            own[(slot, h, *box(t, 0, 4))] = part(t, h, ORDERS[2 + h]).astype(BF)
 
     def stage_chip(t):
         slot = t % SLOTS
         for h in range(2):
             cores[t, h].wait_recv()
-            own[slot, h] = add_low(own[slot, h], from_core[slot, h])
+            every = (slot, h, *box(t, 0, 4))
+            own[every] = add_low(own[every], from_core[every])
+            near_half = (slot, h, *box(t, 0, 2))
             chips[t, h] = start(
-                own.at[slot, h, pl.ds(0, 2 * r)],
-                from_chip.at[slot, h],
+                own.at[near_half],
+                from_chip.at[near_half],
                 chip_sem.at[slot, h],
                 tm_at(4 if h else 2),
             )
@@ -799,12 +813,11 @@
         slot = t % SLOTS
         for h in range(2):
             chips[t, h].wait_recv()
-            own[slot, h, pl.ds(2 * r, 2 * r)] = add_low(
-                own[slot, h, pl.ds(2 * r, 2 * r)], from_chip[slot, h]
-            )
+            upper = (slot, h, *box(t, 2, 2))
+            own[upper] = add_low(own[upper], from_chip[(slot, h, *box(t, 0, 2))])
             owners[t, h] = start(
-                own.at[slot, h, pl.ds(3 * r, r)],
-                from_owner.at[slot, h],
+                own.at[(slot, h, *box(t, 3))],
+                from_owner.at[(slot, h, *box(t, 0))],
                 owner_sem.at[slot, h],
                 tm_at(2 if h else 4),
             )
@@ -816,19 +829,25 @@
             rows[t - SLOTS].wait_send()
         for h in range(2):
             owners[t, h].wait_recv()
-            share[slot, h] = add_low(own[slot, h, pl.ds(2 * r, r)], from_owner[slot, h])
+            first = (slot, h, *box(t, 0))
+            share[first] = add_low(own[(slot, h, *box(t, 2))], from_owner[first])
         spaces[t] = start(
-            share.at[slot, 1 - side], from_space.at[slot], space_sem.at[slot], {"space": 1 - side}
+            share.at[(slot, 1 - side, *box(t, 0))],
+            from_space.at[(slot, *box(t, 0))],
+            space_sem.at[slot],
+            {"space": 1 - side},
         )
 
     def stage_row(t):
         slot = t % SLOTS
         spaces[t].wait_recv()
-        share[slot, side] = add_low(share[slot, side], from_space[slot])
-        other = pl.multiple_of((1 - level) * (r // 2), r // 2)
+        first = (slot, side, *box(t, 0))
+        share[first] = add_low(share[first], from_space[(slot, *box(t, 0))])
+        half, wide = size(t)[0] // 2, pl.ds(0, size(t)[1])
+        other = pl.ds(pl.multiple_of((1 - level) * half, half), half)
         rows[t] = start(
-            share.at[slot, side, pl.ds(other, r // 2)],
-            from_row.at[slot],
+            share.at[slot, side, other, wide],
+            from_row.at[slot, pl.ds(0, half), wide],
             row_sem.at[slot],
             {"row": 1 - level},
         )
@@ -836,16 +855,19 @@
     def stage_back(t):
         slot = t % SLOTS
         rows[t].wait_recv()
-        mine = pl.ds(pl.multiple_of(level * (r // 2), r // 2), r // 2)
+        half, wide = size(t)[0] // 2, pl.ds(0, size(t)[1])
+        mine = pl.ds(pl.multiple_of(level * half, half), half)
         last = t % FINALS
-        final[last, side, mine] = add_low(share[slot, side, mine], from_row[slot])
-        place = final.at[last, side, mine]
+        final[last, side, mine, wide] = add_low(
+            share[slot, side, mine, wide], from_row[slot, pl.ds(0, half), wide]
+        )
+        place = final.at[last, side, mine, wide]
         backs[t] = start(place, place, back_sem.at[last], {"row": 1 - level})
 
     def stage_last(t):
         slot = t % FINALS
         backs[t].wait_recv()
-        place = final.at[slot, side]
+        place = final.at[(slot, side, *box(t, 0))]
         lasts[t] = start(place, place, last_sem.at[slot], {"space": 1 - side})
 
     def stage_out(t):
@@ -853,7 +875,7 @@
         lasts[t].wait_recv()
         out, row, column, half = places[t]
         if out == len(chunks):
-            small_out[...] = final[slot, 0].astype(F32)
+            small_out[...] = final[(slot, 0, *box(t, 0))].astype(F32)
         else:
             for h in range(2):
                 out_refs[out][pl.ds(row, r), pl.ds(column + h * half, WIDE)] = final[slot, h]
@@ -978,7 +1000,7 @@
                 places.append((which, sub * UNIT, j * WIDE, columns // 2))
     places.append((len(CHUNKS), 0, 0, 0))
     small = given["small"]
-    padding = ((0, 0), (0, UNIT - small.shape[1]), (0, WIDE - small.shape[2]))
+    padding = ((0, 0), (0, SMALL_ROWS - small.shape[1]), (0, SMALL_COLUMNS - small.shape[2]))
     given = dict(given, small=jnp.pad(small, padding))
     tokens = given["packed"].shape[0]
     frames = tokens // TILE
@@ -991,14 +1013,14 @@
         out_specs=[in_vmem] * (len(shapes) + 2),
         out_shape=[jax.ShapeDtypeStruct(shape, BF) for shape in shapes]
         + [
-            jax.ShapeDtypeStruct((UNIT, WIDE), F32),
+            jax.ShapeDtypeStruct((SMALL_ROWS, SMALL_COLUMNS), F32),
             jax.ShapeDtypeStruct((2 * frames, TILE // 2, MODEL), BF),
         ],
         scratch_shapes=[vmem(given[name].shape, given[name].dtype) for name in OPERANDS]
         + [
             vmem((tokens, 3 * MODEL), BF),
             vmem((MODEL, tokens), BF),
-            vmem((8, UNIT, WIDE), F32),
+            vmem((8, SMALL_ROWS, SMALL_COLUMNS), F32),
             vmem((frames, TILE, MODEL), BF),
             vmem((2, 2, TILE, TILE), BF),
             vmem((SLOTS, 2, 4 * UNIT, WIDE), BF),

time: 517 us -> 513 us (level)
  no operation moved by 1% of the time
where the time goes in v5:
time: 513 us; the launch traced here: 505 us
  Pallas kernels  324 us (63%)
  waiting for transfers between devices  71.9 us (14%)
  local copies, waits for them, and re-layouts  39.1 us (8%)
  starting transfers between devices  30.3 us (6%)
  matrix products  21.4 us (4%)
  other arithmetic  15.6 us (3%)
    pallas_call x1, Pallas kernels, last_stage(): pl.pallas_call(lambda *refs: last_kernel(CHUNKS, places, *refs), in_specs...  190 us
    ppermute x27, waiting for transfers between devices, hop(): return lax.ppermute(block, axis, [(i, i ^ flip) for i in range(size)])  57.6 us
    pallas_call x1, Pallas kernels, first_gather(): pl.pallas_call(first_kernel, in_specs=[pl.BlockSpec(memory_space=pltpu.VM...  42.1 us
    pallas_call x2, Pallas kernels, attention(): pl.pallas_call(lambda *refs: attn_fwd_kernel(span // TILE, masked, *refs)...  26.3 us
    pallas_call x1, Pallas kernels, attention_back(): pl.pallas_call(lambda *refs: attn_bwd_kernel(span // TILE, bool(more), *r...  22.5 us
    dot_general x6, matrix products, forward_dot(): return jnp.dot(values, weight, preferred_element_type=F32)  16.9 us
    ppermute x27, starting transfers between devices, hop(): return lax.ppermute(block, axis, [(i, i ^ flip) for i in range(size)])  16.7 us
    unnamed x89, local copies, waits for them, and re-layouts  16.6 us
  transfers between devices with their start and end apart: 30, of which 18 were waited for; matrix products, arithmetic and copies ran while one was open for 5% of the time, Pallas kernels for 9%

profile of v5, /device:TPU:0, one launch (start us, length us, event | category | flops | bytes accessed | tf_op | source)
XLA Modules:
  0.0 504.5 jit_solution(10024270160385554606)
XLA Ops:
  0.7 2.3 concatenate.23
  4.5 42.1 %first_gather.1 = (bf16[1024,3072]{1,0:T(8,128)(2,1)}, bf16[1024,1024]{1,0:T(8,128)(2,1)}, bf16[8,32,128]{2,1,0:T(8,128)(2,1)S(1)}, bf16[2,256,1024]{2,1,0:T(8,128)(2,1)S(1)}) custom-call(bf16[128,3072]{1,0:T(8,128)(2,1)S(1)} %copy-done.15, bf16[128,1024]{1,0:T(8,128)(2,1)S(1)} %copy-done.16, bf16[32,128]{1,0:T(8,128)(2,1)S(1)} %pad.8.refs_2_, ...), custom_call_target="tpu_custom_call" | custom-call | bytes 16777216 | tf_op jit(solution)/shard_map/first_gather/pallas_call | solution.py:637
  52.5 3.6 convolution_convert_fusion.1.refs_0_.refs_4_
  56.2 10.4 %attention_forward.2 = (bf16[512,1024]{1,0:T(8,128)(2,1)S(1)}, bf16[16,512,256]{2,1,0:T(8,128)(2,1)}) custom-call(bf16[512,3072]{1,0:T(8,128)(2,1)S(1)} %convolution_convert_fusion.1.refs_0_.refs_4_), custom_call_target="tpu_custom_call" | custom-call | flops 10737418240 | bytes 8388608 | tf_op jit(solution)/shard_map/attention_forward/pallas_call | solution.py:255
  66.6 5.8 %collective-permute-done.refs_2_ = bf16[128,4096]{1,0:T(8,128)(2,1)} collective-permute-done((bf16[128,4096]{1,0:T(8,128)(2,1)S(1)}, bf16[128,4096]{1,0:T(8,128)(2,1)}, u32[]{:S(2)}, u32[]{:S(2)}) %collective-permute-start) | collective-permute-done | bytes 1048608 | tf_op jit(solution)/shard_map/ppermute | solution.py:449
  75.7 4.5 all-to-all-start
  86.2 19.5 %collective-permute-done.5.refs_6_ = bf16[64,4096]{1,0:T(8,128)(2,1)} collective-permute-done((bf16[64,4096]{1,0:T(8,128)(2,1)S(1)}, bf16[64,4096]{1,0:T(8,128)(2,1)}, u32[]{:S(2)}, u32[]{:S(2)}) %collective-permute-start.5) | collective-permute-done | bytes 524320 | tf_op jit(solution)/shard_map/ppermute | solution.py:449
  109.3 3.0 lay_rows.3
  112.3 2.7 copy-done.17
  119.4 5.0 convolution_convert_fusion.refs_0_
  124.4 9.0 %collective-permute-done.9.refs_2_ = bf16[128,4096]{1,0:T(8,128)(2,1)} collective-permute-done((bf16[128,4096]{1,0:T(8,128)(2,1)}, bf16[128,4096]{1,0:T(8,128)(2,1)}, u32[]{:S(2)}, u32[]{:S(2)}) %collective-permute-start.9) | collective-permute-done | bytes 1048608 | tf_op jit(solution)/shard_map/ppermute | solution.py:449
  139.5 4.7 all-to-all-start.1
  144.2 2.0 collective-permute-start.11
  149.6 16.0 %attention_forward.3 = (bf16[512,1024]{1,0:T(8,128)(2,1)S(1)}, bf16[16,512,512]{2,1,0:T(8,128)(2,1)}) custom-call(bf16[512,3072]{1,0:T(8,128)(2,1)S(1)} %copy-done.24, s32[512,1]{1,0:T(8,128)S(1)} %add.145.refs_1_, s32[1,512]{1,0:T(1,128)S(1)} %add.136.refs_2_), custom_call_target="tpu_custom_call" | custom-call | flops 21474836480 | bytes 12582912 | tf_op jit(solution)/shard_map/attention_forward/pallas_call | solution.py:255
  167.6 2.3 collective-permute-done.11.refs_6_
  176.6 3.3 lay_rows.4.weight_ref
  180.0 12.9 %activate.1 = (bf16[512,4096]{1,0:T(8,128)(2,1)}, bf16[4096,512]{1,0:T(8,128)(2,1)}, bf16[512,4096]{1,0:T(8,128)(2,1)}) custom-call(bf16[512,1024]{1,0:T(8,128)(2,1)S(1)} %add_convert_fusion.1.normed_ref.refs_2_, bf16[1024,4096]{1,0:T(8,128)(2,1)S(1)} %lay_rows.4.weight_ref, f32[1,4096]{1,0:T(1,128)S(1)} %bitcast.118), custom_call_target="tpu_custom_call" | custom-call | flops 4294967296 | bytes 20971520 | tf_op jit(solution)/shard_map/activate/pallas_call | solution.py:384
  192.9 2.1 collective-permute-done.19.refs_2_
  198.8 10.4 %collective-permute-done.23.refs_6_ = bf16[256,1024]{1,0:T(8,128)(2,1)S(1)} collective-permute-done((bf16[256,1024]{1,0:T(8,128)(2,1)S(1)}, bf16[256,1024]{1,0:T(8,128)(2,1)S(1)}, u32[]{:S(2)}, u32[]{:S(2)}) %collective-permute-start.23) | collective-permute-done | bytes 524320 | tf_op jit(solution)/shard_map/ppermute | solution.py:449
  211.9 2.0 lay_rows.5.weight_ref
  213.9 7.0 %back_act.1 = (bf16[512,4096]{1,0:T(8,128)(2,1)S(1)}, f32[1,4096]{1,0:T(1,128)S(1)}) custom-call(bf16[512,1024]{1,0:T(8,128)(2,1)S(1)} %bitcast.111, bf16[4096,1024]{1,0:T(8,128)(2,1)S(1)} %lay_rows.5.weight_ref, bf16[512,4096]{1,0:T(8,128)(2,1)S(1)} %copy-done.22), custom_call_target="tpu_custom_call" | custom-call | flops 4294967296 | bytes 16777216 | tf_op jit(solution)/shard_map/back_act/pallas_call | solution.py:421
  220.9 10.8 %back_norm.2 = (bf16[512,1024]{1,0:T(8,128)(2,1)S(1)}, f32[2,1024]{1,0:T(2,128)S(1)}) custom-call(bf16[512,4096]{1,0:T(8,128)(2,1)S(1)} %get-tuple-element.86.grad_ref.refs_3_, bf16[1024,4096]{1,0:T(8,128)(2,1)} %copy-done.4, f32[512,1024]{1,0:T(8,128)S(1)} %get-tuple-element.127.value_ref, bf16[512,1024]{1,0:T(8,128)(2,1)S(1)} %bitcast.112, ...), custom_call_target="tpu_custom_call" | custom-call | flops 4294967296 | bytes 12582912 | tf_op jit(solution)/shard_map/back_norm/pallas_call | solution.py:342
  231.8 2.3 convolution_convert_fusion.3.refs_2_
  234.7 5.5 %add_convert_fusion = bf16[512,1024]{1,0:T(8,128)(2,1)} fusion(f32[512,1024]{1,0:T(8,128)S(1)} %get-tuple-element.127.value_ref, bf16[512,4096]{1,0:T(8,128)(2,1)S(1)} %copy-done.40, bf16[4096,1024]{1,0:T(8,128)(2,1)S(1)} %lay_rows.5.weight_ref, f32[1024]{0:T(1024)S(1)} %bitcast.137), kind=kOutput, calls=%fused_computation.19 | convolution fusion | flops 4296540160 | bytes 15732736 | tf_op jit(solution)/shard_map/dot_general | solution.py:33
  242.7 22.5 %attention_backward.1 = (bf16[512,3072]{1,0:T(8,128)(2,1)}, bf16[4,128,1024]{2,1,0:T(8,128)(2,1)S(1)}) custom-call(bf16[512,3072]{1,0:T(8,128)(2,1)} %convolution_convert_fusion.refs_0_, bf16[16,512,512]{2,1,0:T(8,128)(2,1)} %get-tuple-element.71.refs_1_, bf16[512,1024]{1,0:T(8,128)(2,1)S(1)} %copy-done.23, bf16[32,16,1024]{2,1,0:T(8,128)(2,1)S(1)} %bitcast.122), custom_call_target="tpu_custom_call" | custom-call | flops 24159191040 | bytes 15728640 | tf_op jit(solution)/shard_map/attention_backward/pallas_call | solution.py:280
  265.2 2.2 copy-done.8
  267.4 4.8 back_norm.3
  273.3 4.4 all-to-all-start.2
  279.4 14.3 %all-to-all-done.2 = bf16[16,2,1,16,1024]{4,3,1,2,0:T(8,128)(2,1)S(1)} async-done(((bf16[16,2,1,16,1024]{4,3,1,2,0:T(8,128)(2,1)}), bf16[16,2,1,16,1024]{4,3,1,2,0:T(8,128)(2,1)S(1)}, u32[]{:S(2)}, u32[]{:S(2)}) %all-to-all-start.2) | async-done | bytes 1048608 | tf_op jit(solution)/shard_map/all_to_all | solution.py:1212
  295.7 2.3 convolution_convert_fusion.2.refs_5_
  297.9 189.8 %last_stage.1 = (bf16[512,1024]{1,0:T(8,128)(2,1)}, bf16[128,4096]{1,0:T(8,128)(2,1)}, bf16[128,3072]{1,0:T(8,128)(2,1)}, bf16[128,1024]{1,0:T(8,128)(2,1)}, bf1...) custom-call(bf16[4096,512]{1,0:T(8,128)(2,1)} %get-tuple-element.90.refs_, ...), custom_call_target="tpu_custom_call" | custom-call | flops 1024 | bytes 8650752 | tf_op jit(solution)/shard_map/last_stage/pallas_call | solution.py:1010
  492.9 2.8 bitcast_convert_fusion
  (197 shorter events, 70.8 us)
Async XLA Ops:
  0.6 48.1 %copy-start = (s32[1,4]{1,0:T(1,128)S(1)}, s32[1,4]{1,0:T(1,128)}, u32[]{:S(2)}) copy-start(s32[1,4]{1,0:T(1,128)} %param.29) | copy-start | bytes 52
  46.7 25.7 %collective-permute-start = (bf16[128,4096]{1,0:T(8,128)(2,1)S(1)}, bf16[128,4096]{1,0:T(8,128)(2,1)}, u32[]{:S(2)}, u32[]{:S(2)}) collective-permute-start(bf16[128,4096]{1,0:T(8,128)(2,1)S(1)} %pad_maximum_fusion.refs_0_), channel_id=1, source_target_pairs={{0,4},{2,6},{4,0},{6,2},{8,12},{10,14},{12,8},{14,10},{1,5},{3,7},... | collective-permute-start | bytes 3145736 | tf_op jit(solution)/shard_map/ppermute | solution.py:449
  48.0 25.3 %collective-permute-start.1 = (bf16[128,4096]{1,0:T(8,128)(2,1)S(1)}, bf16[128,4096]{1,0:T(8,128)(2,1)}, u32[]{:S(2)}, u32[]{:S(2)}) collective-permute-start(bf16[128,4096]{1,0:T(8,128)(2,1)S(1)} %pad_maximum_fusion.refs_0_), channel_id=1, source_target_pairs={{0,8},{2,10},{4,12},{6,14},{8,0},{10,2},{12,4},{14,6},{1,9},{3,11}... | collective-permute-start | bytes 3145736 | tf_op jit(solution)/shard_map/ppermute | solution.py:449
  75.7 40.6 %all-to-all-start = ((bf16[1,2,16,16,1024]{4,3,1,0,2:T(8,128)(2,1)}), bf16[1,2,16,16,1024]{4,3,1,0,2:T(8,128)(2,1)}, u32[]{:S(2)}, u32[]{:S(2)}) async-start(bf16[1,2,16,16,1024]{4,3,1,0,2:T(8,128)(2,1)} %copy.37), calls=%async_computation | async-start | bytes 2097152 | tf_op jit(solution)/shard_map/all_to_all | solution.py:1152
  81.2 24.5 %collective-permute-start.5 = (bf16[64,4096]{1,0:T(8,128)(2,1)S(1)}, bf16[64,4096]{1,0:T(8,128)(2,1)}, u32[]{:S(2)}, u32[]{:S(2)}) collective-permute-start(bf16[64,4096]{1,0:T(8,128)(2,1)S(1)} %slice.120), channel_id=1, source_target_pairs={{0,8},{2,10},{4,12},{6,14},{8,0},{10,2},{12,4},{14,6},{1,9},{3,11}... | collective-permute-start | bytes 1572872 | tf_op jit(solution)/shard_map/ppermute | solution.py:449
  84.1 22.9 %collective-permute-start.7 = (bf16[64,4096]{1,0:T(8,128)(2,1)S(1)}, bf16[64,4096]{1,0:T(8,128)(2,1)}, u32[]{:S(2)}, u32[]{:S(2)}) collective-permute-start(bf16[64,4096]{1,0:T(8,128)(2,1)S(1)} %slice.121), channel_id=1, source_target_pairs={{0,4},{2,6},{4,0},{6,2},{8,12},{10,14},{12,8},{14,10},{1,5},{3,7},... | collective-permute-start | bytes 1572872 | tf_op jit(solution)/shard_map/ppermute | solution.py:449
  85.7 21.7 %collective-permute-start.2 = (bf16[128,4096]{1,0:T(8,128)(2,1)S(1)}, bf16[128,4096]{1,0:T(8,128)(2,1)S(1)}, u32[]{:S(2)}, u32[]{:S(2)}) collective-permute-start(bf16[128,4096]{1,0:T(8,128)(2,1)S(1)} %pad_maximum_fusion.refs_0_), channel_id=1, source_target_pairs={{0,2},{2,0},{4,6},{6,4},{8,10},{10,8},{12,14},{14,12},{1,3},{3,1},... | collective-permute-start | bytes 3145736 | tf_op jit(solution)/shard_map/ppermute | solution.py:449
  85.7 22.4 %collective-permute-start.3 = (bf16[128,4096]{1,0:T(8,128)(2,1)}, bf16[128,4096]{1,0:T(8,128)(2,1)S(1)}, u32[]{:S(2)}, u32[]{:S(2)}) collective-permute-start(bf16[128,4096]{1,0:T(8,128)(2,1)} %collective-permute-done.refs_2_), channel_id=1, source_target_pairs={{0,2},{2,0},{4,6},{6,4},{8,10},{10,8},{12,14},{14,12},{1,3},{3,1},... | collective-permute-start | bytes 3145736 | tf_op jit(solution)/shard_map/ppermute | solution.py:449
  86.2 22.4 %collective-permute-start.4 = (bf16[128,4096]{1,0:T(8,128)(2,1)}, bf16[128,4096]{1,0:T(8,128)(2,1)}, u32[]{:S(2)}, u32[]{:S(2)}) collective-permute-start(bf16[128,4096]{1,0:T(8,128)(2,1)} %collective-permute-done.1.refs_4_), channel_id=1, source_target_pairs={{0,2},{2,0},{4,6},{6,4},{8,10},{10,8},{12,14},{14,12},{1,3},{3,1},... | collective-permute-start | bytes 3145736 | tf_op jit(solution)/shard_map/ppermute | solution.py:449
  105.7 2.9 collective-permute-start.6
  107.0 2.3 collective-permute-start.8
  107.4 26.0 %collective-permute-start.9 = (bf16[128,4096]{1,0:T(8,128)(2,1)}, bf16[128,4096]{1,0:T(8,128)(2,1)}, u32[]{:S(2)}, u32[]{:S(2)}) collective-permute-start(bf16[128,4096]{1,0:T(8,128)(2,1)} %refs_0_.2), channel_id=1, source_target_pairs={{0,4},{2,6},{4,0},{6,2},{8,12},{10,14},{12,8},{14,10},{1,5},{3,7},... | collective-permute-start | bytes 3145736 | tf_op jit(solution)/shard_map/ppermute | solution.py:449
  108.1 25.3 %collective-permute-start.10 = (bf16[128,4096]{1,0:T(8,128)(2,1)}, bf16[128,4096]{1,0:T(8,128)(2,1)}, u32[]{:S(2)}, u32[]{:S(2)}) collective-permute-start(bf16[128,4096]{1,0:T(8,128)(2,1)} %refs_0_.2), channel_id=1, source_target_pairs={{0,8},{2,10},{4,12},{6,14},{8,0},{10,2},{12,4},{14,6},{1,9},{3,11}... | collective-permute-start | bytes 3145736 | tf_op jit(solution)/shard_map/ppermute | solution.py:449
  108.6 65.1 %collective-permute-start.14 = (bf16[128,4096]{1,0:T(8,128)(2,1)}, bf16[128,4096]{1,0:T(8,128)(2,1)}, u32[]{:S(2)}, u32[]{:S(2)}) collective-permute-start(bf16[128,4096]{1,0:T(8,128)(2,1)} %refs_0_.2), channel_id=1, source_target_pairs={{0,2},{2,0},{4,6},{6,4},{8,10},{10,8},{12,14},{14,12},{1,3},{3,1},... | collective-permute-start | bytes 3145736 | tf_op jit(solution)/shard_map/ppermute | solution.py:449
  135.3 38.5 %collective-permute-start.15 = (bf16[128,4096]{1,0:T(8,128)(2,1)}, bf16[128,4096]{1,0:T(8,128)(2,1)}, u32[]{:S(2)}, u32[]{:S(2)}) collective-permute-start(bf16[128,4096]{1,0:T(8,128)(2,1)} %collective-permute-done.9.refs_2_), channel_id=1, source_target_pairs={{0,2},{2,0},{4,6},{6,4},{8,10},{10,8},{12,14},{14,12},{1,3},{3,1},... | collective-permute-start | bytes 3145736 | tf_op jit(solution)/shard_map/ppermute | solution.py:449
  137.2 37.6 %collective-permute-start.16 = (bf16[128,4096]{1,0:T(8,128)(2,1)}, bf16[128,4096]{1,0:T(8,128)(2,1)}, u32[]{:S(2)}, u32[]{:S(2)}) collective-permute-start(bf16[128,4096]{1,0:T(8,128)(2,1)} %collective-permute-done.10.refs_4_), channel_id=1, source_target_pairs={{0,2},{2,0},{4,6},{6,4},{8,10},{10,8},{12,14},{14,12},{1,3},{3,1},... | collective-permute-start | bytes 3145736 | tf_op jit(solution)/shard_map/ppermute | solution.py:449
  139.5 26.1 %all-to-all-start.1 = ((bf16[4,128,1024]{2,0,1:T(4,128)(2,1)}), bf16[4,128,1024]{2,0,1:T(4,128)(2,1)}, u32[]{:S(2)}, u32[]{:S(2)}) async-start(bf16[4,128,1024]{2,0,1:T(4,128)(2,1)} %bitcast.104), calls=%async_computation.1 | async-start | bytes 2097152 | tf_op jit(solution)/shard_map/all_to_all | solution.py:121
  144.2 25.7 %collective-permute-start.11 = (bf16[64,4096]{1,0:T(8,128)(2,1)}, bf16[64,4096]{1,0:T(8,128)(2,1)}, u32[]{:S(2)}, u32[]{:S(2)}) collective-permute-start(bf16[64,4096]{1,0:T(8,128)(2,1)} %slice.122), channel_id=1, source_target_pairs={{0,8},{2,10},{4,12},{6,14},{8,0},{10,2},{12,4},{14,6},{1,9},{3,11}... | collective-permute-start | bytes 1572872 | tf_op jit(solution)/shard_map/ppermute | solution.py:449
  146.2 23.7 %collective-permute-start.12 = (bf16[64,4096]{1,0:T(8,128)(2,1)}, bf16[64,4096]{1,0:T(8,128)(2,1)}, u32[]{:S(2)}, u32[]{:S(2)}) collective-permute-start(bf16[64,4096]{1,0:T(8,128)(2,1)} %slice.123), channel_id=1, source_target_pairs={{0,4},{2,6},{4,0},{6,2},{8,12},{10,14},{12,8},{14,10},{1,5},{3,7},... | collective-permute-start | bytes 1572872 | tf_op jit(solution)/shard_map/ppermute | solution.py:449
  167.6 110.9 %copy-start.3 = (bf16[8,4,16,1024]{3,2,1,0:T(8,128)(2,1)}, bf16[8,4,16,1024]{3,2,1,0:T(8,128)(2,1)S(1)}, u32[]{:S(2)}) copy-start(bf16[8,4,16,1024]{3,2,1,0:T(8,128)(2,1)S(1)} %copy.41) | copy-start | bytes 3145732
  170.0 25.0 %collective-permute-start.19 = (bf16[512,1024]{1,0:T(8,128)(2,1)}, bf16[512,1024]{1,0:T(8,128)(2,1)S(1)}, u32[]{:S(2)}, u32[]{:S(2)}) collective-permute-start(bf16[512,1024]{1,0:T(8,128)(2,1)} %refs_0_.3), channel_id=1, source_target_pairs={{0,4},{2,6},{4,0},{6,2},{8,12},{10,14},{12,8},{14,10},{1,5},{3,7},... | collective-permute-start | bytes 3145736 | tf_op jit(solution)/shard_map/ppermute | solution.py:449
  171.3 25.1 %collective-permute-start.20 = (bf16[512,1024]{1,0:T(8,128)(2,1)}, bf16[512,1024]{1,0:T(8,128)(2,1)S(1)}, u32[]{:S(2)}, u32[]{:S(2)}) collective-permute-start(bf16[512,1024]{1,0:T(8,128)(2,1)} %refs_0_.3), channel_id=1, source_target_pairs={{0,8},{2,10},{4,12},{6,14},{8,0},{10,2},{12,4},{14,6},{1,9},{3,11}... | collective-permute-start | bytes 3145736 | tf_op jit(solution)/shard_map/ppermute | solution.py:449
  173.7 2.2 collective-permute-start.17
  173.8 2.8 collective-permute-start.18
  174.7 35.0 %collective-permute-start.13 = (bf16[512,1024]{1,0:T(8,128)(2,1)}, bf16[512,1024]{1,0:T(8,128)(2,1)S(1)}, u32[]{:S(2)}, u32[]{:S(2)}) collective-permute-start(bf16[512,1024]{1,0:T(8,128)(2,1)} %refs_0_.3), channel_id=1, source_target_pairs={{0,2},{2,0},{4,6},{6,4},{8,10},{10,8},{12,14},{14,12},{1,3},{3,1},... | collective-permute-start | bytes 3145736 | tf_op jit(solution)/shard_map/ppermute | solution.py:449
  196.4 12.8 %collective-permute-start.23 = (bf16[256,1024]{1,0:T(8,128)(2,1)S(1)}, bf16[256,1024]{1,0:T(8,128)(2,1)S(1)}, u32[]{:S(2)}, u32[]{:S(2)}) collective-permute-start(bf16[256,1024]{1,0:T(8,128)(2,1)S(1)} %slice.127), channel_id=1, source_target_pairs={{0,8},{2,10},{4,12},{6,14},{8,0},{10,2},{12,4},{14,6},{1,9},{3,11}... | collective-permute-start | bytes 1572872 | tf_op jit(solution)/shard_map/ppermute | solution.py:449
  196.9 12.5 %collective-permute-start.25 = (bf16[256,1024]{1,0:T(8,128)(2,1)S(1)}, bf16[256,1024]{1,0:T(8,128)(2,1)S(1)}, u32[]{:S(2)}, u32[]{:S(2)}) collective-permute-start(bf16[256,1024]{1,0:T(8,128)(2,1)S(1)} %slice.128), channel_id=1, source_target_pairs={{0,4},{2,6},{4,0},{6,2},{8,12},{10,14},{12,8},{14,10},{1,5},{3,7},... | collective-permute-start | bytes 1572872 | tf_op jit(solution)/shard_map/ppermute | solution.py:449
  198.3 13.6 %collective-permute-start.21 = (bf16[512,1024]{1,0:T(8,128)(2,1)S(1)}, bf16[512,1024]{1,0:T(8,128)(2,1)S(1)}, u32[]{:S(2)}, u32[]{:S(2)}) collective-permute-start(bf16[512,1024]{1,0:T(8,128)(2,1)S(1)} %collective-permute-done.19.refs_2_), channel_id=1, source_target_pairs={{0,2},{2,0},{4,6},{6,4},{8,10},{10,8},{12,14},{14,12},{1,3},{3,1},... | collective-permute-start | bytes 3145736 | tf_op jit(solution)/shard_map/ppermute | solution.py:449
  198.3 13.6 %collective-permute-start.22 = (bf16[512,1024]{1,0:T(8,128)(2,1)S(1)}, bf16[512,1024]{1,0:T(8,128)(2,1)S(1)}, u32[]{:S(2)}, u32[]{:S(2)}) collective-permute-start(bf16[512,1024]{1,0:T(8,128)(2,1)S(1)} %collective-permute-done.20.refs_4_), channel_id=1, source_target_pairs={{0,2},{2,0},{4,6},{6,4},{8,10},{10,8},{12,14},{14,12},{1,3},{3,1},... | collective-permute-start | bytes 3145736 | tf_op jit(solution)/shard_map/ppermute | solution.py:449
  209.2 1.9 collective-permute-start.24
  209.4 2.5 collective-permute-start.26
  273.3 20.4 %all-to-all-start.2 = ((bf16[16,2,1,16,1024]{4,3,1,2,0:T(8,128)(2,1)}), bf16[16,2,1,16,1024]{4,3,1,2,0:T(8,128)(2,1)S(1)}, u32[]{:S(2)}, u32[]{:S(2)}) async-start(bf16[16,2,1,16,1024]{4,3,1,2,0:T(8,128)(2,1)} %bitcast.33), calls=%async_computation.2 | async-start | bytes 2097152 | tf_op jit(solution)/shard_map/all_to_all | solution.py:1212
  (41 other events, 292.3 us)

commit v6 on v5

--- a/solution.py
+++ b/solution.py
@@ -162,7 +162,7 @@
             mixed_ref[mine, pair_cols(pair, 0)] = join_heads(*outs).astype(BF)
         return carry
 
-    lax.fori_loop(0, PAIRS, one_pair, 0, unroll=2)
+    lax.fori_loop(0, PAIRS, one_pair, 0, unroll=4)
 
 
 def attn_bwd_tile(
@@ -217,7 +217,7 @@
             attn_bwd_tile(t, tiles, pair, packed_ref, probs_ref, grad_ref, out_ref, accs)
         return carry
 
-    lax.fori_loop(0, PAIRS, one_pair, 0, unroll=2)
+    lax.fori_loop(0, PAIRS, one_pair, 0, unroll=4)
     for copy in copies:
         copy.wait()
 

time: 513 us -> 513 us (level)
  transfers between devices with their start and end apart: 30 -> 30, of which waited for: 18 -> 18; matrix products, arithmetic and copies ran while one was open for 5% -> 5% of each run, Pallas kernels for 9% -> 8%
where the time goes in v6:
time: 513 us; the launch traced here: 504 us
  Pallas kernels  321 us (63%)
  waiting for transfers between devices  75.4 us (15%)
  local copies, waits for them, and re-layouts  39.1 us (8%)
  starting transfers between devices  30.1 us (6%)
  matrix products  21.4 us (4%)
  other arithmetic  15.6 us (3%)
    pallas_call x1, Pallas kernels, last_stage(): pl.pallas_call(lambda *refs: last_kernel(CHUNKS, places, *refs), in_specs...  190 us
    ppermute x27, waiting for transfers between devices, hop(): return lax.ppermute(block, axis, [(i, i ^ flip) for i in range(size)])  61.1 us
    pallas_call x1, Pallas kernels, first_gather(): pl.pallas_call(first_kernel, in_specs=[pl.BlockSpec(memory_space=pltpu.VM...  42.1 us
    pallas_call x2, Pallas kernels, attention(): pl.pallas_call(lambda *refs: attn_fwd_kernel(span // TILE, masked, *refs)...  22.9 us
    pallas_call x1, Pallas kernels, attention_back(): pl.pallas_call(lambda *refs: attn_bwd_kernel(span // TILE, bool(more), *r...  22.3 us
    dot_general x6, matrix products, forward_dot(): return jnp.dot(values, weight, preferred_element_type=F32)  16.9 us
    ppermute x27, starting transfers between devices, hop(): return lax.ppermute(block, axis, [(i, i ^ flip) for i in range(size)])  16.7 us
    unnamed x89, local copies, waits for them, and re-layouts  16.6 us
  transfers between devices with their start and end apart: 30, of which 18 were waited for; matrix products, arithmetic and copies ran while one was open for 5% of the time, Pallas kernels for 8%

profile of v6, /device:TPU:0, one launch (start us, length us, event | category | flops | bytes accessed | tf_op | source)
XLA Modules:
  0.0 503.9 jit_solution(1113049547232805084)
XLA Ops:
  0.7 2.3 concatenate.23
  4.5 42.1 %first_gather.1 = (bf16[1024,3072]{1,0:T(8,128)(2,1)}, bf16[1024,1024]{1,0:T(8,128)(2,1)}, bf16[8,32,128]{2,1,0:T(8,128)(2,1)S(1)}, bf16[2,256,1024]{2,1,0:T(8,128)(2,1)S(1)}) custom-call(bf16[128,3072]{1,0:T(8,128)(2,1)S(1)} %copy-done.15, bf16[128,1024]{1,0:T(8,128)(2,1)S(1)} %copy-done.16, bf16[32,128]{1,0:T(8,128)(2,1)S(1)} %pad.8.refs_2_, ...), custom_call_target="tpu_custom_call" | custom-call | bytes 16777216 | tf_op jit(solution)/shard_map/first_gather/pallas_call | solution.py:637
  52.5 3.6 convolution_convert_fusion.1.refs_0_.refs_4_
  56.2 7.7 %attention_forward.2 = (bf16[512,1024]{1,0:T(8,128)(2,1)S(1)}, bf16[16,512,256]{2,1,0:T(8,128)(2,1)}) custom-call(bf16[512,3072]{1,0:T(8,128)(2,1)S(1)} %convolution_convert_fusion.1.refs_0_.refs_4_), custom_call_target="tpu_custom_call" | custom-call | flops 10737418240 | bytes 8388608 | tf_op jit(solution)/shard_map/attention_forward/pallas_call | solution.py:255
  63.9 8.4 %collective-permute-done.refs_2_ = bf16[128,4096]{1,0:T(8,128)(2,1)} collective-permute-done((bf16[128,4096]{1,0:T(8,128)(2,1)S(1)}, bf16[128,4096]{1,0:T(8,128)(2,1)}, u32[]{:S(2)}, u32[]{:S(2)}) %collective-permute-start) | collective-permute-done | bytes 1048608 | tf_op jit(solution)/shard_map/ppermute | solution.py:449
  75.7 4.5 all-to-all-start
  86.2 19.5 %collective-permute-done.5.refs_6_ = bf16[64,4096]{1,0:T(8,128)(2,1)} collective-permute-done((bf16[64,4096]{1,0:T(8,128)(2,1)S(1)}, bf16[64,4096]{1,0:T(8,128)(2,1)}, u32[]{:S(2)}, u32[]{:S(2)}) %collective-permute-start.5) | collective-permute-done | bytes 524320 | tf_op jit(solution)/shard_map/ppermute | solution.py:449
  109.3 3.0 lay_rows.3
  112.3 2.7 copy-done.17
  119.4 5.0 convolution_convert_fusion.refs_0_
  124.4 9.0 %collective-permute-done.9.refs_2_ = bf16[128,4096]{1,0:T(8,128)(2,1)} collective-permute-done((bf16[128,4096]{1,0:T(8,128)(2,1)}, bf16[128,4096]{1,0:T(8,128)(2,1)}, u32[]{:S(2)}, u32[]{:S(2)}) %collective-permute-start.9) | collective-permute-done | bytes 1048608 | tf_op jit(solution)/shard_map/ppermute | solution.py:449
  139.5 4.5 all-to-all-start.1
  143.9 2.0 collective-permute-start.11
  149.3 15.1 %attention_forward.3 = (bf16[512,1024]{1,0:T(8,128)(2,1)S(1)}, bf16[16,512,512]{2,1,0:T(8,128)(2,1)}) custom-call(bf16[512,3072]{1,0:T(8,128)(2,1)S(1)} %copy-done.24, s32[512,1]{1,0:T(8,128)S(1)} %add.145.refs_1_, s32[1,512]{1,0:T(1,128)S(1)} %add.136.refs_2_), custom_call_target="tpu_custom_call" | custom-call | flops 21474836480 | bytes 12582912 | tf_op jit(solution)/shard_map/attention_forward/pallas_call | solution.py:255
  166.5 3.1 collective-permute-done.11.refs_6_
  176.4 3.3 lay_rows.4.weight_ref
  179.7 12.9 %activate.1 = (bf16[512,4096]{1,0:T(8,128)(2,1)}, bf16[4096,512]{1,0:T(8,128)(2,1)}, bf16[512,4096]{1,0:T(8,128)(2,1)}) custom-call(bf16[512,1024]{1,0:T(8,128)(2,1)S(1)} %add_convert_fusion.1.normed_ref.refs_2_, bf16[1024,4096]{1,0:T(8,128)(2,1)S(1)} %lay_rows.4.weight_ref, f32[1,4096]{1,0:T(1,128)S(1)} %bitcast.118), custom_call_target="tpu_custom_call" | custom-call | flops 4294967296 | bytes 20971520 | tf_op jit(solution)/shard_map/activate/pallas_call | solution.py:384
  192.6 2.1 collective-permute-done.19.refs_2_
  198.6 10.4 %collective-permute-done.23.refs_6_ = bf16[256,1024]{1,0:T(8,128)(2,1)S(1)} collective-permute-done((bf16[256,1024]{1,0:T(8,128)(2,1)S(1)}, bf16[256,1024]{1,0:T(8,128)(2,1)S(1)}, u32[]{:S(2)}, u32[]{:S(2)}) %collective-permute-start.23) | collective-permute-done | bytes 524320 | tf_op jit(solution)/shard_map/ppermute | solution.py:449
  211.7 2.0 lay_rows.5.weight_ref
  213.7 7.0 %back_act.1 = (bf16[512,4096]{1,0:T(8,128)(2,1)S(1)}, f32[1,4096]{1,0:T(1,128)S(1)}) custom-call(bf16[512,1024]{1,0:T(8,128)(2,1)S(1)} %bitcast.111, bf16[4096,1024]{1,0:T(8,128)(2,1)S(1)} %lay_rows.5.weight_ref, bf16[512,4096]{1,0:T(8,128)(2,1)S(1)} %copy-done.22), custom_call_target="tpu_custom_call" | custom-call | flops 4294967296 | bytes 16777216 | tf_op jit(solution)/shard_map/back_act/pallas_call | solution.py:421
  220.7 10.6 %back_norm.2 = (bf16[512,1024]{1,0:T(8,128)(2,1)S(1)}, f32[2,1024]{1,0:T(2,128)S(1)}) custom-call(bf16[512,4096]{1,0:T(8,128)(2,1)S(1)} %get-tuple-element.86.grad_ref.refs_3_, bf16[1024,4096]{1,0:T(8,128)(2,1)} %copy-done.4, f32[512,1024]{1,0:T(8,128)S(1)} %get-tuple-element.127.value_ref, bf16[512,1024]{1,0:T(8,128)(2,1)S(1)} %bitcast.112, ...), custom_call_target="tpu_custom_call" | custom-call | flops 4294967296 | bytes 12582912 | tf_op jit(solution)/shard_map/back_norm/pallas_call | solution.py:342
  231.3 2.3 convolution_convert_fusion.3.refs_2_
  234.2 5.5 %add_convert_fusion = bf16[512,1024]{1,0:T(8,128)(2,1)} fusion(f32[512,1024]{1,0:T(8,128)S(1)} %get-tuple-element.127.value_ref, bf16[512,4096]{1,0:T(8,128)(2,1)S(1)} %copy-done.40, bf16[4096,1024]{1,0:T(8,128)(2,1)S(1)} %lay_rows.5.weight_ref, f32[1024]{0:T(1024)S(1)} %bitcast.137), kind=kOutput, calls=%fused_computation.19 | convolution fusion | flops 4296540160 | bytes 15732736 | tf_op jit(solution)/shard_map/dot_general | solution.py:33
  242.2 22.3 %attention_backward.1 = (bf16[512,3072]{1,0:T(8,128)(2,1)}, bf16[4,128,1024]{2,1,0:T(8,128)(2,1)S(1)}) custom-call(bf16[512,3072]{1,0:T(8,128)(2,1)} %convolution_convert_fusion.refs_0_, bf16[16,512,512]{2,1,0:T(8,128)(2,1)} %get-tuple-element.71.refs_1_, bf16[512,1024]{1,0:T(8,128)(2,1)S(1)} %copy-done.23, bf16[32,16,1024]{2,1,0:T(8,128)(2,1)S(1)} %bitcast.122), custom_call_target="tpu_custom_call" | custom-call | flops 24159191040 | bytes 15728640 | tf_op jit(solution)/shard_map/attention_backward/pallas_call | solution.py:280
  264.6 2.2 copy-done.8
  266.8 4.8 back_norm.3
  272.7 4.4 all-to-all-start.2
  278.8 14.3 %all-to-all-done.2 = bf16[16,2,1,16,1024]{4,3,1,2,0:T(8,128)(2,1)S(1)} async-done(((bf16[16,2,1,16,1024]{4,3,1,2,0:T(8,128)(2,1)}), bf16[16,2,1,16,1024]{4,3,1,2,0:T(8,128)(2,1)S(1)}, u32[]{:S(2)}, u32[]{:S(2)}) %all-to-all-start.2) | async-done | bytes 1048608 | tf_op jit(solution)/shard_map/all_to_all | solution.py:1212
  295.1 2.3 convolution_convert_fusion.2.refs_5_
  297.3 189.8 %last_stage.1 = (bf16[512,1024]{1,0:T(8,128)(2,1)}, bf16[128,4096]{1,0:T(8,128)(2,1)}, bf16[128,3072]{1,0:T(8,128)(2,1)}, bf16[128,1024]{1,0:T(8,128)(2,1)}, bf1...) custom-call(bf16[4096,512]{1,0:T(8,128)(2,1)} %get-tuple-element.90.refs_, ...), custom_call_target="tpu_custom_call" | custom-call | flops 1024 | bytes 8650752 | tf_op jit(solution)/shard_map/last_stage/pallas_call | solution.py:1010
  492.3 2.8 bitcast_convert_fusion
  (197 shorter events, 70.8 us)
Async XLA Ops:
  0.6 48.1 %copy-start = (s32[1,4]{1,0:T(1,128)S(1)}, s32[1,4]{1,0:T(1,128)}, u32[]{:S(2)}) copy-start(s32[1,4]{1,0:T(1,128)} %param.29) | copy-start | bytes 52
  46.7 25.7 %collective-permute-start = (bf16[128,4096]{1,0:T(8,128)(2,1)S(1)}, bf16[128,4096]{1,0:T(8,128)(2,1)}, u32[]{:S(2)}, u32[]{:S(2)}) collective-permute-start(bf16[128,4096]{1,0:T(8,128)(2,1)S(1)} %pad_maximum_fusion.refs_0_), channel_id=1, source_target_pairs={{0,4},{2,6},{4,0},{6,2},{8,12},{10,14},{12,8},{14,10},{1,5},{3,7},... | collective-permute-start | bytes 3145736 | tf_op jit(solution)/shard_map/ppermute | solution.py:449
  48.0 25.3 %collective-permute-start.1 = (bf16[128,4096]{1,0:T(8,128)(2,1)S(1)}, bf16[128,4096]{1,0:T(8,128)(2,1)}, u32[]{:S(2)}, u32[]{:S(2)}) collective-permute-start(bf16[128,4096]{1,0:T(8,128)(2,1)S(1)} %pad_maximum_fusion.refs_0_), channel_id=1, source_target_pairs={{0,8},{2,10},{4,12},{6,14},{8,0},{10,2},{12,4},{14,6},{1,9},{3,11}... | collective-permute-start | bytes 3145736 | tf_op jit(solution)/shard_map/ppermute | solution.py:449
  75.7 40.6 %all-to-all-start = ((bf16[1,2,16,16,1024]{4,3,1,0,2:T(8,128)(2,1)}), bf16[1,2,16,16,1024]{4,3,1,0,2:T(8,128)(2,1)}, u32[]{:S(2)}, u32[]{:S(2)}) async-start(bf16[1,2,16,16,1024]{4,3,1,0,2:T(8,128)(2,1)} %copy.37), calls=%async_computation | async-start | bytes 2097152 | tf_op jit(solution)/shard_map/all_to_all | solution.py:1152
  81.2 24.5 %collective-permute-start.5 = (bf16[64,4096]{1,0:T(8,128)(2,1)S(1)}, bf16[64,4096]{1,0:T(8,128)(2,1)}, u32[]{:S(2)}, u32[]{:S(2)}) collective-permute-start(bf16[64,4096]{1,0:T(8,128)(2,1)S(1)} %slice.120), channel_id=1, source_target_pairs={{0,8},{2,10},{4,12},{6,14},{8,0},{10,2},{12,4},{14,6},{1,9},{3,11}... | collective-permute-start | bytes 1572872 | tf_op jit(solution)/shard_map/ppermute | solution.py:449
  84.1 22.9 %collective-permute-start.7 = (bf16[64,4096]{1,0:T(8,128)(2,1)S(1)}, bf16[64,4096]{1,0:T(8,128)(2,1)}, u32[]{:S(2)}, u32[]{:S(2)}) collective-permute-start(bf16[64,4096]{1,0:T(8,128)(2,1)S(1)} %slice.121), channel_id=1, source_target_pairs={{0,4},{2,6},{4,0},{6,2},{8,12},{10,14},{12,8},{14,10},{1,5},{3,7},... | collective-permute-start | bytes 1572872 | tf_op jit(solution)/shard_map/ppermute | solution.py:449
  85.7 21.7 %collective-permute-start.2 = (bf16[128,4096]{1,0:T(8,128)(2,1)S(1)}, bf16[128,4096]{1,0:T(8,128)(2,1)S(1)}, u32[]{:S(2)}, u32[]{:S(2)}) collective-permute-start(bf16[128,4096]{1,0:T(8,128)(2,1)S(1)} %pad_maximum_fusion.refs_0_), channel_id=1, source_target_pairs={{0,2},{2,0},{4,6},{6,4},{8,10},{10,8},{12,14},{14,12},{1,3},{3,1},... | collective-permute-start | bytes 3145736 | tf_op jit(solution)/shard_map/ppermute | solution.py:449
  85.7 22.4 %collective-permute-start.3 = (bf16[128,4096]{1,0:T(8,128)(2,1)}, bf16[128,4096]{1,0:T(8,128)(2,1)S(1)}, u32[]{:S(2)}, u32[]{:S(2)}) collective-permute-start(bf16[128,4096]{1,0:T(8,128)(2,1)} %collective-permute-done.refs_2_), channel_id=1, source_target_pairs={{0,2},{2,0},{4,6},{6,4},{8,10},{10,8},{12,14},{14,12},{1,3},{3,1},... | collective-permute-start | bytes 3145736 | tf_op jit(solution)/shard_map/ppermute | solution.py:449
  86.2 22.4 %collective-permute-start.4 = (bf16[128,4096]{1,0:T(8,128)(2,1)}, bf16[128,4096]{1,0:T(8,128)(2,1)}, u32[]{:S(2)}, u32[]{:S(2)}) collective-permute-start(bf16[128,4096]{1,0:T(8,128)(2,1)} %collective-permute-done.1.refs_4_), channel_id=1, source_target_pairs={{0,2},{2,0},{4,6},{6,4},{8,10},{10,8},{12,14},{14,12},{1,3},{3,1},... | collective-permute-start | bytes 3145736 | tf_op jit(solution)/shard_map/ppermute | solution.py:449
  105.7 2.9 collective-permute-start.6
  107.0 2.3 collective-permute-start.8
  107.4 26.0 %collective-permute-start.9 = (bf16[128,4096]{1,0:T(8,128)(2,1)}, bf16[128,4096]{1,0:T(8,128)(2,1)}, u32[]{:S(2)}, u32[]{:S(2)}) collective-permute-start(bf16[128,4096]{1,0:T(8,128)(2,1)} %refs_0_.2), channel_id=1, source_target_pairs={{0,4},{2,6},{4,0},{6,2},{8,12},{10,14},{12,8},{14,10},{1,5},{3,7},... | collective-permute-start | bytes 3145736 | tf_op jit(solution)/shard_map/ppermute | solution.py:449
  108.1 25.3 %collective-permute-start.10 = (bf16[128,4096]{1,0:T(8,128)(2,1)}, bf16[128,4096]{1,0:T(8,128)(2,1)}, u32[]{:S(2)}, u32[]{:S(2)}) collective-permute-start(bf16[128,4096]{1,0:T(8,128)(2,1)} %refs_0_.2), channel_id=1, source_target_pairs={{0,8},{2,10},{4,12},{6,14},{8,0},{10,2},{12,4},{14,6},{1,9},{3,11}... | collective-permute-start | bytes 3145736 | tf_op jit(solution)/shard_map/ppermute | solution.py:449
  108.6 64.8 %collective-permute-start.14 = (bf16[128,4096]{1,0:T(8,128)(2,1)}, bf16[128,4096]{1,0:T(8,128)(2,1)}, u32[]{:S(2)}, u32[]{:S(2)}) collective-permute-start(bf16[128,4096]{1,0:T(8,128)(2,1)} %refs_0_.2), channel_id=1, source_target_pairs={{0,2},{2,0},{4,6},{6,4},{8,10},{10,8},{12,14},{14,12},{1,3},{3,1},... | collective-permute-start | bytes 3145736 | tf_op jit(solution)/shard_map/ppermute | solution.py:449
  135.3 38.2 %collective-permute-start.15 = (bf16[128,4096]{1,0:T(8,128)(2,1)}, bf16[128,4096]{1,0:T(8,128)(2,1)}, u32[]{:S(2)}, u32[]{:S(2)}) collective-permute-start(bf16[128,4096]{1,0:T(8,128)(2,1)} %collective-permute-done.9.refs_2_), channel_id=1, source_target_pairs={{0,2},{2,0},{4,6},{6,4},{8,10},{10,8},{12,14},{14,12},{1,3},{3,1},... | collective-permute-start | bytes 3145736 | tf_op jit(solution)/shard_map/ppermute | solution.py:449
  137.2 37.3 %collective-permute-start.16 = (bf16[128,4096]{1,0:T(8,128)(2,1)}, bf16[128,4096]{1,0:T(8,128)(2,1)}, u32[]{:S(2)}, u32[]{:S(2)}) collective-permute-start(bf16[128,4096]{1,0:T(8,128)(2,1)} %collective-permute-done.10.refs_4_), channel_id=1, source_target_pairs={{0,2},{2,0},{4,6},{6,4},{8,10},{10,8},{12,14},{14,12},{1,3},{3,1},... | collective-permute-start | bytes 3145736 | tf_op jit(solution)/shard_map/ppermute | solution.py:449
  139.5 25.0 %all-to-all-start.1 = ((bf16[4,128,1024]{2,0,1:T(4,128)(2,1)}), bf16[4,128,1024]{2,0,1:T(4,128)(2,1)}, u32[]{:S(2)}, u32[]{:S(2)}) async-start(bf16[4,128,1024]{2,0,1:T(4,128)(2,1)} %bitcast.104), calls=%async_computation.1 | async-start | bytes 2097152 | tf_op jit(solution)/shard_map/all_to_all | solution.py:121
  143.9 25.7 %collective-permute-start.11 = (bf16[64,4096]{1,0:T(8,128)(2,1)}, bf16[64,4096]{1,0:T(8,128)(2,1)}, u32[]{:S(2)}, u32[]{:S(2)}) collective-permute-start(bf16[64,4096]{1,0:T(8,128)(2,1)} %slice.122), channel_id=1, source_target_pairs={{0,8},{2,10},{4,12},{6,14},{8,0},{10,2},{12,4},{14,6},{1,9},{3,11}... | collective-permute-start | bytes 1572872 | tf_op jit(solution)/shard_map/ppermute | solution.py:449
  146.0 23.7 %collective-permute-start.12 = (bf16[64,4096]{1,0:T(8,128)(2,1)}, bf16[64,4096]{1,0:T(8,128)(2,1)}, u32[]{:S(2)}, u32[]{:S(2)}) collective-permute-start(bf16[64,4096]{1,0:T(8,128)(2,1)} %slice.123), channel_id=1, source_target_pairs={{0,4},{2,6},{4,0},{6,2},{8,12},{10,14},{12,8},{14,10},{1,5},{3,7},... | collective-permute-start | bytes 1572872 | tf_op jit(solution)/shard_map/ppermute | solution.py:449
  166.5 111.4 %copy-start.3 = (bf16[8,4,16,1024]{3,2,1,0:T(8,128)(2,1)}, bf16[8,4,16,1024]{3,2,1,0:T(8,128)(2,1)S(1)}, u32[]{:S(2)}) copy-start(bf16[8,4,16,1024]{3,2,1,0:T(8,128)(2,1)S(1)} %copy.41) | copy-start | bytes 3145732
  169.7 25.0 %collective-permute-start.19 = (bf16[512,1024]{1,0:T(8,128)(2,1)}, bf16[512,1024]{1,0:T(8,128)(2,1)S(1)}, u32[]{:S(2)}, u32[]{:S(2)}) collective-permute-start(bf16[512,1024]{1,0:T(8,128)(2,1)} %refs_0_.3), channel_id=1, source_target_pairs={{0,4},{2,6},{4,0},{6,2},{8,12},{10,14},{12,8},{14,10},{1,5},{3,7},... | collective-permute-start | bytes 3145736 | tf_op jit(solution)/shard_map/ppermute | solution.py:449
  171.1 25.1 %collective-permute-start.20 = (bf16[512,1024]{1,0:T(8,128)(2,1)}, bf16[512,1024]{1,0:T(8,128)(2,1)S(1)}, u32[]{:S(2)}, u32[]{:S(2)}) collective-permute-start(bf16[512,1024]{1,0:T(8,128)(2,1)} %refs_0_.3), channel_id=1, source_target_pairs={{0,8},{2,10},{4,12},{6,14},{8,0},{10,2},{12,4},{14,6},{1,9},{3,11}... | collective-permute-start | bytes 3145736 | tf_op jit(solution)/shard_map/ppermute | solution.py:449
  173.4 2.2 collective-permute-start.17
  173.5 2.8 collective-permute-start.18
  174.5 35.0 %collective-permute-start.13 = (bf16[512,1024]{1,0:T(8,128)(2,1)}, bf16[512,1024]{1,0:T(8,128)(2,1)S(1)}, u32[]{:S(2)}, u32[]{:S(2)}) collective-permute-start(bf16[512,1024]{1,0:T(8,128)(2,1)} %refs_0_.3), channel_id=1, source_target_pairs={{0,2},{2,0},{4,6},{6,4},{8,10},{10,8},{12,14},{14,12},{1,3},{3,1},... | collective-permute-start | bytes 3145736 | tf_op jit(solution)/shard_map/ppermute | solution.py:449
  196.2 12.8 %collective-permute-start.23 = (bf16[256,1024]{1,0:T(8,128)(2,1)S(1)}, bf16[256,1024]{1,0:T(8,128)(2,1)S(1)}, u32[]{:S(2)}, u32[]{:S(2)}) collective-permute-start(bf16[256,1024]{1,0:T(8,128)(2,1)S(1)} %slice.127), channel_id=1, source_target_pairs={{0,8},{2,10},{4,12},{6,14},{8,0},{10,2},{12,4},{14,6},{1,9},{3,11}... | collective-permute-start | bytes 1572872 | tf_op jit(solution)/shard_map/ppermute | solution.py:449
  196.6 12.5 %collective-permute-start.25 = (bf16[256,1024]{1,0:T(8,128)(2,1)S(1)}, bf16[256,1024]{1,0:T(8,128)(2,1)S(1)}, u32[]{:S(2)}, u32[]{:S(2)}) collective-permute-start(bf16[256,1024]{1,0:T(8,128)(2,1)S(1)} %slice.128), channel_id=1, source_target_pairs={{0,4},{2,6},{4,0},{6,2},{8,12},{10,14},{12,8},{14,10},{1,5},{3,7},... | collective-permute-start | bytes 1572872 | tf_op jit(solution)/shard_map/ppermute | solution.py:449
  198.1 13.6 %collective-permute-start.21 = (bf16[512,1024]{1,0:T(8,128)(2,1)S(1)}, bf16[512,1024]{1,0:T(8,128)(2,1)S(1)}, u32[]{:S(2)}, u32[]{:S(2)}) collective-permute-start(bf16[512,1024]{1,0:T(8,128)(2,1)S(1)} %collective-permute-done.19.refs_2_), channel_id=1, source_target_pairs={{0,2},{2,0},{4,6},{6,4},{8,10},{10,8},{12,14},{14,12},{1,3},{3,1},... | collective-permute-start | bytes 3145736 | tf_op jit(solution)/shard_map/ppermute | solution.py:449
  198.1 13.6 %collective-permute-start.22 = (bf16[512,1024]{1,0:T(8,128)(2,1)S(1)}, bf16[512,1024]{1,0:T(8,128)(2,1)S(1)}, u32[]{:S(2)}, u32[]{:S(2)}) collective-permute-start(bf16[512,1024]{1,0:T(8,128)(2,1)S(1)} %collective-permute-done.20.refs_4_), channel_id=1, source_target_pairs={{0,2},{2,0},{4,6},{6,4},{8,10},{10,8},{12,14},{14,12},{1,3},{3,1},... | collective-permute-start | bytes 3145736 | tf_op jit(solution)/shard_map/ppermute | solution.py:449
  209.0 1.9 collective-permute-start.24
  209.1 2.5 collective-permute-start.26
  272.7 20.4 %all-to-all-start.2 = ((bf16[16,2,1,16,1024]{4,3,1,2,0:T(8,128)(2,1)}), bf16[16,2,1,16,1024]{4,3,1,2,0:T(8,128)(2,1)S(1)}, u32[]{:S(2)}, u32[]{:S(2)}) async-start(bf16[16,2,1,16,1024]{4,3,1,2,0:T(8,128)(2,1)} %bitcast.33), calls=%async_computation.2 | async-start | bytes 2097152 | tf_op jit(solution)/shard_map/all_to_all | solution.py:1212
  (41 other events, 293.4 us)
